TPU v7x, 128 devices: a whole 4x4x4 slice. The times are simulated.
128 devices in a mesh: dp: 8 (over y, core), expert: 16 (over z, x).
Axes of the slice: x: 4, y: 4, z: 4, core: 2. Of those that a mesh axis runs over, the one named last changes fastest.
Arguments:
- tokens: bfloat16 [2, 16, 1024, 1024], P(None, 'expert', 'dp'), may hold values from -6 to 6
- cotangent: bfloat16 [2, 16, 1024, 1024], P(None, 'expert', 'dp'), may hold values from -6 to 6
- segments: int32 [2, 16, 1024], P(None, 'expert'), may hold values from 0 to 4, as said below
- routes: int32 [2, 16, 1024, 8], P(None, 'expert', 'dp'), may hold values from 0 to 31, all different within a row; in each aligned block of 128 rows (0 to 127, 128 to 255, ..., all dimensions but the last counted through in order) at most 48 rows name the same one
- w_qkv: bfloat16 [1024, 2048], P('dp'), may hold values from -0.1875 to 0.1875
- w_out: bfloat16 [1024, 1024], P('dp'), may hold values from -0.75 to 0.75
- attn_norm: bfloat16 [1024], P('dp'), may hold values from 0.099609375 to 1.8984375
- ffn_norm: bfloat16 [1024], P('dp'), may hold values from 0.099609375 to 1.8984375
- q_gain: bfloat16 [64], P('dp'), may hold values from 0.099609375 to 1.8984375
- k_gain: bfloat16 [64], P('dp'), may hold values from 0.099609375 to 1.8984375
- router: bfloat16 [1024, 32], P('dp'), may hold values from -0.09375 to 0.09375
- w_gate_up: bfloat16 [32, 1024, 1024], P('expert'), may hold values from -0.1875 to 0.1875
- w_down: bfloat16 [32, 512, 1024], P('expert'), may hold values from -1 to 1
Outputs:
- output: bfloat16 [2, 16, 1024, 1024], P(None, 'expert', 'dp')
- input_grad: bfloat16 [2, 16, 1024, 1024], P(None, 'expert', 'dp')
- grad_qkv: float32 [1024, 2048], P('dp')
- grad_out: float32 [1024, 1024], P('dp')
- grad_attn_norm: float32 [1024], P('dp')
- grad_ffn_norm: float32 [1024], P('dp')
- grad_q_gain: float32 [64], P('dp')
- grad_k_gain: float32 [64], P('dp')
- grad_router: float32 [1024, 32], P('dp')
- grad_gate_up: float32 [32, 1024, 1024], P('expert')
- grad_down: float32 [32, 512, 1024], P('expert')
Inputs may be any that keep to these rules, and one draw needn't show every extreme that they name: `segments`: segment numbers never fall along a sequence; equal numbers mark one document. `routes`: the 8 experts of a token differ. Within each aligned block of 128 positions of one sequence in one micro-batch no expert is named more than 48 times, a bound that some block reaches.
All inputs are finite; a program needn't handle non-finite values.
Results may differ from a plain program's by a relative error of at most 0.025.
Values may be sent and summed in bfloat16 or wider, within the bound.
A program may use at most 256 MiB of HBM per device.

v0:
```python
import jax
import jax.numpy as jnp
from jax import lax
from jax.sharding import PartitionSpec as P

HD = 64


EPSILON = 1e-06
THETA = 10000.0
MASKED = -1e30
HIGHEST = lax.Precision.HIGHEST


def in_one_piece(arrays, axis, dim, along):
    columns = [a.reshape(*a.shape[:along], -1) for a in arrays]
    both = jnp.concatenate(columns, axis=along)
    filled, at, done = (lax.all_gather(both, axis, axis=dim, tiled=True), 0, [])
    for a, column in zip(arrays, columns):
        section = filled[..., at : at + column.shape[along]]
        done.append(section.reshape(*section.shape[:along], *a.shape[along:]))
        at += column.shape[along]
    return tuple(done)


def sent_together(arrays, axis, dim, along):
    both = jnp.concatenate(arrays, axis=along)
    filled, at, done = (lax.all_gather(both, axis, axis=dim, tiled=True), 0, [])
    for a in arrays:
        done.append(lax.slice_in_dim(filled, at, at + a.shape[along], axis=along))
        at += a.shape[along]
    return tuple(done)


def in_one_piece_2(arrays, axis, dim, along):
    widths = [a.shape[along] for a in arrays]
    both = jnp.concatenate(arrays, axis=along)
    filled = lax.psum_scatter(both, axis, scatter_dimension=dim, tiled=True)
    return tuple(jnp.split(filled, [sum(widths[:k]) for k in range(1, len(widths))], axis=along))


def in_one_piece_3(arrays, axis, dim, along):
    columns = [a.reshape(*a.shape[:along], -1) for a in arrays]
    both = jnp.concatenate(columns, axis=along)
    filled, at, done = (lax.psum_scatter(both, axis, scatter_dimension=dim, tiled=True), 0, [])
    for a, column in zip(arrays, columns):
        section = filled[..., at : at + column.shape[along]]
        done.append(section.reshape(*section.shape[:along], *a.shape[along:]))
        at += column.shape[along]
    return tuple(done)


def together(arrays, axis):
    vector, at, done = (jnp.concatenate([a.reshape(-1) for a in arrays]), 0, [])
    subtotal = lax.psum(vector, axis)
    for a in arrays:
        done.append(subtotal[at : at + a.size].reshape(a.shape))
        at += a.size
    return tuple(done)


def norm_rows(values_in, gain_vec):
    inverse = lax.rsqrt(jnp.mean(values_in * values_in, axis=-1, keepdims=True) + EPSILON)
    return (values_in * inverse * gain_vec, inverse)


def norm_back(grad_in, values_in, inverse, gain_vec):
    scaled = grad_in * gain_vec
    moment = jnp.mean(scaled * values_in, axis=-1, keepdims=True)
    grad_values = inverse * (scaled - values_in * inverse * inverse * moment)
    grad_gain = grad_in * values_in * inverse
    return (grad_values, jnp.sum(grad_gain.reshape(-1, grad_gain.shape[-1]), axis=0))


def rotary(values_in, cosine, sine_vals):
    half_size = values_in.shape[-1] // 2
    front_half = values_in[..., :half_size]
    back_half = values_in[..., half_size:]
    return jnp.concatenate(
        [front_half * cosine - back_half * sine_vals, back_half * cosine + front_half * sine_vals],
        axis=-1,
    )


def angles(positions):
    frequency = jnp.power(THETA, -2.0 * jnp.arange(HD // 2, dtype=jnp.float32) / HD)
    turned = positions[:, None] * frequency[None, :]
    return (jnp.cos(turned)[:, None, :], jnp.sin(turned)[:, None, :])


def body(
    tokens,
    cotangent,
    segments,
    routes,
    w_qkv,
    w_out,
    attn_norm,
    ffn_norm,
    q_gain,
    k_gain,
    router,
    w_gate_up,
    w_down,
):
    micro_count, seq_count, query_rows, width = tokens.shape
    seq_length = segments.shape[2]
    experts_here = w_gate_up.shape[0]
    owners = lax.axis_size("expert")
    dp_size = lax.axis_size("dp")
    experts_all = experts_here * owners
    top_count = routes.shape[3]
    hidden_units = w_down.shape[1]
    q_width = w_out.shape[0] * dp_size
    kv_width = (w_qkv.shape[1] - q_width) // 2
    kv_heads = kv_width // HD
    head_group = q_width // HD // kv_heads
    scaling = HD ** (-0.5)
    tok_rows = seq_count * query_rows
    copy_rows = tok_rows * top_count
    capacity = seq_count * max(2, query_rows * top_count * 3 // (2 * experts_all))
    dp_index = lax.axis_index("dp")
    cosine, sine_vals = angles((dp_index * query_rows + jnp.arange(query_rows)).astype(jnp.float32))
    expert_ids = jnp.arange(experts_all, dtype=jnp.int32)
    zero_row = jnp.zeros((1, width), jnp.bfloat16)
    attn_totals = [
        jnp.zeros((piece.shape[0] * dp_size,) + piece.shape[1:], jnp.float32)
        for piece in (w_qkv, w_out, attn_norm, ffn_norm, q_gain, k_gain, router)
    ]
    gate_up_total = jnp.zeros(w_gate_up.shape, jnp.float32)
    down_total = jnp.zeros(w_down.shape, jnp.float32)
    outputs = []
    input_grads = []
    for micro_index in range(micro_count):
        gathered = (
            *in_one_piece((w_qkv, w_out, attn_norm, ffn_norm), "dp", 0, 1),
            lax.all_gather(q_gain, "dp", axis=0, tiled=True),
            lax.all_gather(k_gain, "dp", axis=0, tiled=True),
            lax.all_gather(router, "dp", axis=0, tiled=True),
        )
        full_qkv, full_out, full_attn_norm, full_ffn_norm, full_q_gain, full_k_gain, full_router = (
            gathered
        )
        attn_gain = full_attn_norm.astype(jnp.float32)
        ffn_gain = full_ffn_norm.astype(jnp.float32)
        query_gain = full_q_gain.astype(jnp.float32)
        key_gain = full_k_gain.astype(jnp.float32)
        states = tokens[micro_index].astype(jnp.float32).reshape(tok_rows, width)
        normed, inv_attn = norm_rows(states, attn_gain)
        normed_low = normed.astype(jnp.bfloat16)
        projected = jnp.dot(normed_low, full_qkv, preferred_element_type=jnp.float32)
        query_raw = projected[:, :q_width].reshape(seq_count, query_rows, q_width // HD, HD)
        key_raw = projected[:, q_width : q_width + kv_width].reshape(
            seq_count, query_rows, kv_heads, HD
        )
        value_low = (
            projected[:, q_width + kv_width :]
            .astype(jnp.bfloat16)
            .reshape(seq_count, query_rows, kv_width)
        )
        query_normed, inv_query = norm_rows(query_raw, query_gain)
        key_normed, inv_key = norm_rows(key_raw, key_gain)
        query_low = (
            rotary(query_normed, cosine, sine_vals)
            .astype(jnp.bfloat16)
            .reshape(seq_count, query_rows, kv_heads, head_group, HD)
        )
        key_low = (
            rotary(key_normed, cosine, sine_vals)
            .astype(jnp.bfloat16)
            .reshape(seq_count, query_rows, kv_width)
        )
        key_all, value_all = sent_together((key_low, value_low), "dp", 1, 0)
        key_all = key_all.reshape(seq_count, seq_length, kv_heads, HD)
        value_all = value_all.reshape(seq_count, seq_length, kv_heads, HD)
        segment_all = segments[micro_index]
        segment_own = lax.dynamic_slice_in_dim(segment_all, dp_index * query_rows, query_rows, 1)
        same_doc = (segment_own[:, :, None] == segment_all[:, None, :])[:, None, None]

        def attn_scores():
            raw_scores = (
                jnp.einsum(
                    "sqgrd,skgd->sgrqk", query_low, key_all, preferred_element_type=jnp.float32
                )
                * scaling
            )
            return jnp.where(same_doc, raw_scores, MASKED)

        scores = attn_scores()
        row_max = jnp.max(scores, axis=-1, keepdims=True)
        exp_scores = jnp.exp(scores - row_max)
        row_sum = jnp.sum(exp_scores, axis=-1, keepdims=True)
        log_norm = row_max + jnp.log(row_sum)
        probs_low = (exp_scores / row_sum).astype(jnp.bfloat16)
        mixed = jnp.einsum(
            "sgrqk,skgd->sqgrd", probs_low, value_all, preferred_element_type=jnp.float32
        )
        mixed_low = mixed.reshape(tok_rows, q_width).astype(jnp.bfloat16)
        residual = states + jnp.dot(mixed_low, full_out, preferred_element_type=jnp.float32)
        ffn_normed, inv_ffn = norm_rows(residual, ffn_gain)
        ffn_low = ffn_normed.astype(jnp.bfloat16)
        logits = jnp.dot(ffn_low, full_router, preferred_element_type=jnp.float32)
        route_ids = routes[micro_index].reshape(tok_rows, top_count)
        chosen = jnp.take_along_axis(logits, route_ids, axis=1)
        gate_vals = jax.nn.softmax(chosen, axis=-1)
        flat_ids = route_ids.reshape(copy_rows)
        one_hot = (flat_ids[:, None] == expert_ids[None, :]).astype(jnp.int32)
        earlier = jnp.cumsum(one_hot, axis=0) - one_hot
        slot_ids = jnp.sum(earlier * one_hot, axis=1)
        targets = flat_ids * capacity + slot_ids
        sources = (
            jnp.full((experts_all * capacity,), copy_rows, jnp.int32)
            .at[targets]
            .set(jnp.arange(copy_rows, dtype=jnp.int32))
        )
        token_of = jnp.where(sources < copy_rows, sources // top_count, tok_rows)
        padded = jnp.concatenate([ffn_low, zero_row], axis=0)
        outgoing = padded[token_of].reshape(owners, experts_here, capacity, width)
        expert_piece = lax.all_to_all(outgoing, "expert", split_axis=0, concat_axis=0, tiled=True)
        gate_up = jnp.einsum(
            "oecd,edf->oecf", expert_piece, w_gate_up, preferred_element_type=jnp.float32
        )
        active = (jax.nn.silu(gate_up[..., :hidden_units]) * gate_up[..., hidden_units:]).astype(
            jnp.bfloat16
        )
        result = jnp.einsum(
            "oecf,efd->oecd", active, w_down, preferred_element_type=jnp.float32
        ).astype(jnp.bfloat16)
        expert_out, arrived, gate_up = (result, expert_piece, gate_up)
        coming_back = lax.all_to_all(expert_out, "expert", split_axis=0, concat_axis=0, tiled=True)
        picked = (
            coming_back.reshape(experts_all * capacity, width)[targets]
            .astype(jnp.float32)
            .reshape(tok_rows, top_count, width)
        )
        final = residual + jnp.sum(gate_vals[:, :, None] * picked, axis=1)
        outputs.append(final.astype(jnp.bfloat16).reshape(seq_count, query_rows, width))
        grad_final = cotangent[micro_index].astype(jnp.float32).reshape(tok_rows, width)
        grad_gate = jnp.sum(picked * grad_final[:, None, :], axis=-1)
        grad_chosen = gate_vals * (
            grad_gate - jnp.sum(gate_vals * grad_gate, axis=-1, keepdims=True)
        )
        route_hot = (route_ids[:, :, None] == expert_ids[None, None, :]).astype(jnp.float32)
        grad_logits = jnp.sum(grad_chosen[:, :, None] * route_hot, axis=1)
        grad_router_now = jnp.einsum(
            "rd,re->de", ffn_low.astype(jnp.float32), grad_logits, precision=HIGHEST
        )
        grad_ffn_in = jnp.einsum(
            "re,de->rd", grad_logits, full_router.astype(jnp.float32), precision=HIGHEST
        )
        grad_copies = (
            (gate_vals[:, :, None] * grad_final[:, None, :])
            .astype(jnp.bfloat16)
            .reshape(copy_rows, width)
        )
        grad_padded = jnp.concatenate([grad_copies, zero_row], axis=0)
        grad_outgoing = grad_padded[jnp.minimum(sources, copy_rows)].reshape(
            owners, experts_here, capacity, width
        )
        grad_arrived = lax.all_to_all(
            grad_outgoing, "expert", split_axis=0, concat_axis=0, tiled=True
        )
        gate_part = gate_up[..., :hidden_units]
        up_part = gate_up[..., hidden_units:]
        sigmoid_gate = jax.nn.sigmoid(gate_part)
        silu_gate = gate_part * sigmoid_gate
        active = (silu_gate * up_part).astype(jnp.bfloat16)
        down_total = down_total + jnp.einsum(
            "oecf,oecd->efd", active, grad_arrived, preferred_element_type=jnp.float32
        )
        grad_active = jnp.einsum(
            "oecd,efd->oecf", grad_arrived, w_down, preferred_element_type=jnp.float32
        )
        grad_gate_part = (
            grad_active * up_part * sigmoid_gate * (1.0 + gate_part * (1.0 - sigmoid_gate))
        )
        grad_up_part = grad_active * silu_gate
        grad_both = jnp.concatenate([grad_gate_part, grad_up_part], axis=-1).astype(jnp.bfloat16)
        gate_up_total = gate_up_total + jnp.einsum(
            "oecd,oecf->edf", arrived, grad_both, preferred_element_type=jnp.float32
        )
        grad_rows = jnp.einsum(
            "oecf,edf->oecd", grad_both, w_gate_up, preferred_element_type=jnp.float32
        ).astype(jnp.bfloat16)
        grad_back = lax.all_to_all(grad_rows, "expert", split_axis=0, concat_axis=0, tiled=True)
        grad_picked = grad_back.reshape(experts_all * capacity, width)[targets].astype(jnp.float32)
        grad_ffn_in = grad_ffn_in + jnp.sum(grad_picked.reshape(tok_rows, top_count, width), axis=1)
        grad_residual_part, ffn_gain_grad = norm_back(grad_ffn_in, residual, inv_ffn, ffn_gain)
        grad_residual = grad_final + grad_residual_part
        grad_branch = grad_residual.astype(jnp.bfloat16)
        grad_out_now = jnp.einsum(
            "rq,rd->qd", mixed_low, grad_branch, preferred_element_type=jnp.float32
        )
        grad_mixed = jnp.einsum(
            "rd,qd->rq", grad_branch, full_out, preferred_element_type=jnp.float32
        )
        grad_mixed = grad_mixed.astype(jnp.bfloat16).reshape(
            seq_count, query_rows, kv_heads, head_group, HD
        )
        probs = jnp.exp(attn_scores() - log_norm)
        grad_probs = jnp.einsum(
            "sqgrd,skgd->sgrqk", grad_mixed, value_all, preferred_element_type=jnp.float32
        )
        inner = jnp.sum(probs * grad_probs, axis=-1, keepdims=True)
        grad_scores = (probs * (grad_probs - inner)).astype(jnp.bfloat16)
        grad_query = (
            jnp.einsum(
                "sgrqk,skgd->sqgrd", grad_scores, key_all, preferred_element_type=jnp.float32
            )
            * scaling
        )
        grad_key_part = (
            jnp.einsum(
                "sgrqk,sqgrd->skgd", grad_scores, query_low, preferred_element_type=jnp.float32
            )
            * scaling
        )
        grad_value_part = jnp.einsum(
            "sgrqk,sqgrd->skgd",
            probs.astype(jnp.bfloat16),
            grad_mixed,
            preferred_element_type=jnp.float32,
        )
        grad_key, grad_value = tuple(
            (
                part.astype(jnp.float32)
                for part in in_one_piece_2(
                    (
                        grad_key_part.reshape(seq_count, seq_length, kv_width).astype(jnp.bfloat16),
                        grad_value_part.reshape(seq_count, seq_length, kv_width).astype(
                            jnp.bfloat16
                        ),
                    ),
                    "dp",
                    1,
                    0,
                )
            )
        )
        grad_query = rotary(
            grad_query.reshape(seq_count, query_rows, q_width // HD, HD), cosine, -sine_vals
        )
        grad_query_raw, query_gain_grad = norm_back(grad_query, query_raw, inv_query, query_gain)
        grad_key = rotary(grad_key.reshape(seq_count, query_rows, kv_heads, HD), cosine, -sine_vals)
        grad_key_raw, key_gain_grad = norm_back(grad_key, key_raw, inv_key, key_gain)
        grad_projected = jnp.concatenate(
            [
                grad_query_raw.reshape(tok_rows, q_width),
                grad_key_raw.reshape(tok_rows, kv_width),
                grad_value.reshape(tok_rows, kv_width),
            ],
            axis=1,
        ).astype(jnp.bfloat16)
        grad_qkv_now = jnp.einsum(
            "rd,rf->df", normed_low, grad_projected, preferred_element_type=jnp.float32
        )
        grad_normed = jnp.einsum(
            "rf,df->rd", grad_projected, full_qkv, preferred_element_type=jnp.float32
        )
        grad_states_part, attn_gain_grad = norm_back(grad_normed, states, inv_attn, attn_gain)
        input_grads.append(
            (grad_residual + grad_states_part)
            .astype(jnp.bfloat16)
            .reshape(seq_count, query_rows, width)
        )
        fresh_terms = (
            grad_qkv_now,
            grad_out_now,
            attn_gain_grad,
            ffn_gain_grad,
            query_gain_grad,
            key_gain_grad,
            grad_router_now,
        )
        attn_totals = [running + fresh for running, fresh in zip(attn_totals, fresh_terms)]
    attn_full = (
        attn_totals[0],
        attn_totals[1],
        attn_totals[2],
        attn_totals[3],
        attn_totals[4],
        attn_totals[5],
        attn_totals[6],
    )
    shard_part = (
        *tuple(
            (
                part.astype(jnp.float32)
                for part in in_one_piece_3(
                    (
                        attn_full[0].astype(jnp.bfloat16),
                        attn_full[1].astype(jnp.bfloat16),
                        attn_full[2].astype(jnp.bfloat16),
                        attn_full[3].astype(jnp.bfloat16),
                    ),
                    "dp",
                    0,
                    1,
                )
            )
        ),
        lax.psum_scatter(
            attn_full[4].astype(jnp.bfloat16), "dp", scatter_dimension=0, tiled=True
        ).astype(jnp.float32),
        lax.psum_scatter(
            attn_full[5].astype(jnp.bfloat16), "dp", scatter_dimension=0, tiled=True
        ).astype(jnp.float32),
        lax.psum_scatter(
            attn_full[6].astype(jnp.bfloat16), "dp", scatter_dimension=0, tiled=True
        ).astype(jnp.float32),
    )
    shard_grads = (
        lax.psum(shard_part[0].astype(jnp.bfloat16), "expert").astype(jnp.float32),
        lax.psum(shard_part[1].astype(jnp.bfloat16), "expert").astype(jnp.float32),
        lax.psum(shard_part[2].astype(jnp.bfloat16), "expert").astype(jnp.float32),
        lax.psum(shard_part[3].astype(jnp.bfloat16), "expert").astype(jnp.float32),
        lax.psum(shard_part[4].astype(jnp.bfloat16), "expert").astype(jnp.float32),
        lax.psum(shard_part[5].astype(jnp.bfloat16), "expert").astype(jnp.float32),
        lax.psum(shard_part[6].astype(jnp.bfloat16), "expert").astype(jnp.float32),
    )
    grad_gate_up, grad_down = tuple(
        (
            part.astype(jnp.float32)
            for part in together(
                (gate_up_total.astype(jnp.bfloat16), down_total.astype(jnp.bfloat16)), "dp"
            )
        )
    )
    return (
        jnp.stack(outputs),
        jnp.stack(input_grads),
        shard_grads[0],
        shard_grads[1],
        shard_grads[2],
        shard_grads[3],
        shard_grads[4],
        shard_grads[5],
        shard_grads[6],
        grad_gate_up,
        grad_down,
    )


def solution(mesh):
    return jax.shard_map(
        body,
        mesh=mesh,
        in_specs=(
            P(None, "expert", "dp", None),
            P(None, "expert", "dp", None),
            P(None, "expert", None),
            P(None, "expert", "dp", None),
            P("dp", None),
            P("dp", None),
            P("dp"),
            P("dp"),
            P("dp"),
            P("dp"),
            P("dp", None),
            P("expert", None, None),
            P("expert", None, None),
        ),
        out_specs=(
            P(None, "expert", "dp", None),
            P(None, "expert", "dp", None),
            P("dp", None),
            P("dp", None),
            P("dp"),
            P("dp"),
            P("dp"),
            P("dp"),
            P("dp", None),
            P("expert", None, None),
            P("expert", None, None),
        ),
        check_vma=False,
    )
```

profile of v0, /device:TPU:0, one launch (start us, length us, event | category | flops | bytes accessed | tf_op | source)
XLA Modules:
  0.0 898.9 jit_solution(14967849241779224788)
XLA Ops:
  14.7 15.0 %all-reduce.11 = (bf16[64]{0:T(256)(128)(2,1)S(1)}, bf16[64]{0:T(256)(128)(2,1)S(1)}) all-reduce(bf16[64]{0:T(256)(128)(2,1)S(1)} %dynamic-update-slice, bf16[64]{0:T(256)(128)(2,1)S(1)} %dynamic-update-slice.1), channel_id=1, replica_groups=mesh['dp'=8,'expert'=16] {'dp'}, use_global_device_ids=true, to_apply=%add.4 | all-reduce | flops 128 | bytes 512
  32.4 23.3 %all-gather.4.cloned.1.call-done = bf16[1024,3074]{1,0:T(8,128)(2,1)} async-done(((bf16[128,3074]{1,0:T(8,128)(2,1)}), bf16[1024,3074]{1,0:T(8,128)(2,1)}) %all-gather.4.cloned.1.call-update) | async-done | bytes 6295568 | tf_op jit(solution)/shard_map/all_gather | solution.py:18
  66.7 9.0 %reduce-window.14 = s32[32,8,128]{2,1,0:T(8,128)S(1)} reduce-window(s32[32,8,128]{2,1,0:T(8,128)S(1)} %fusion.190, s32[]{:T(128)} %constant.100.clone.1), window={size=1x1x128 pad=0_0x0_0x127_0}, to_apply=%region_8.10 | reduce-window | flops 4161536 | bytes 262148 | tf_op jit(solution)/shard_map/reduce-window
  121.8 11.2 %all_gather.26 = bf16[1024,32]{0,1:T(8,128)(2,1)S(1)} all-gather(bf16[128,32]{0,1:T(8,128)(2,1)S(1)} %copy-done.114), channel_id=1, replica_groups=mesh['dp'=8,'expert'=16] {'dp'}, dimensions={0}, use_global_device_ids=true | all-gather | bytes 73728 | tf_op jit(solution)/shard_map/all_gather | solution.py:139
  144.6 9.7 %gather_fusion.4 = bf16[1536,1024]{1,0:T(8,128)(2,1)} fusion(bf16[1025,1024]{1,0:T(8,128)(2,1)} %concatenate.193, s32[2048]{0:T(1024)S(1)} %copy-done.99), kind=kCustom, calls=%fused_computation.6 | custom fusion | bytes 6297600 | tf_op jit(solution)/shard_map/gather | solution.py:257
  154.3 16.1 %all-to-all-done = bf16[16,2,48,1024]{3,2,1,0:T(8,128)(2,1)} async-done(((bf16[16,2,48,1024]{3,2,1,0:T(8,128)(2,1)}), bf16[16,2,48,1024]{3,2,1,0:T(8,128)(2,1)}, u32[]{:S(2)}, u32[]{:S(2)}) %all-to-all-start) | async-done | bytes 3145760 | tf_op jit(solution)/shard_map/all_to_all | solution.py:219
  177.2 9.3 %fusion.71 = f32[16,2,48,1024]{3,2,0,1:T(8,128)} fusion(bf16[2,1024,1024]{2,1,0:T(8,128)(2,1)} %param.26, bf16[16,2,48,1024]{3,2,1,0:T(8,128)(2,1)} %all-to-all-done), kind=kOutput, calls=%fused_computation.121 | convolution fusion | flops 3221225472 | bytes 13631488 | tf_op jit(solution)/shard_map/oecd,edf->oecf/dot_general | solution.py:220
  186.4 35.0 %all-to-all-done.4 = bf16[16,2,48,1024]{3,2,1,0:T(8,128)(2,1)} async-done(((bf16[16,2,48,1024]{3,2,1,0:T(8,128)(2,1)}), bf16[16,2,48,1024]{3,2,1,0:T(8,128)(2,1)}, u32[]{:S(2)}, u32[]{:S(2)}) %all-to-all-start.4) | async-done | bytes 3145760 | tf_op jit(solution)/shard_map/all_to_all | solution.py:260
  237.7 9.0 %reduce-window.16 = s32[32,8,128]{2,1,0:T(8,128)S(1)} reduce-window(s32[32,8,128]{2,1,0:T(8,128)S(1)} %fusion.191, s32[]{:T(128)} %constant.100.clone.1), window={size=1x1x128 pad=0_0x0_0x127_0}, to_apply=%region_21.23 | reduce-window | flops 4161536 | bytes 262148 | tf_op jit(solution)/shard_map/reduce-window.2
  266.7 14.2 %all-to-all-done.1 = bf16[16,2,48,1024]{3,2,1,0:T(8,128)(2,1)} async-done(((bf16[16,2,48,1024]{3,2,1,0:T(8,128)(2,1)}), bf16[16,2,48,1024]{3,2,1,0:T(8,128)(2,1)}, u32[]{:S(2)}, u32[]{:S(2)}) %all-to-all-start.1) | async-done | bytes 3145760 | tf_op jit(solution)/shard_map/all_to_all | solution.py:230
  303.7 8.4 gather_fusion.1
  316.4 12.0 %all-to-all-done.5 = bf16[16,2,48,1024]{3,2,1,0:T(8,128)(2,1)} async-done(((bf16[16,2,48,1024]{3,2,1,0:T(8,128)(2,1)}), bf16[16,2,48,1024]{3,2,1,0:T(8,128)(2,1)}, u32[]{:S(2)}, u32[]{:S(2)}) %all-to-all-start.5) | async-done | bytes 3145760 | tf_op jit(solution)/shard_map/all_to_all | solution.py:285
  386.0 9.6 %gather_fusion.6 = bf16[1536,1024]{1,0:T(8,128)(2,1)} fusion(bf16[1025,1024]{1,0:T(8,128)(2,1)} %concatenate.201, s32[2048]{0:T(1024)S(1)} %copy-done.98), kind=kCustom, calls=%fused_computation.8 | custom fusion | bytes 6297600 | tf_op jit(solution)/shard_map/gather | solution.py:257
  403.0 9.7 %fusion.49 = f32[2,1024,1024,1]{2,1,0,3:T(8,128)} fusion(bf16[16,2,48,1024]{3,2,1,0:T(8,128)(2,1)} %all-to-all-done, bf16[16,2,48,512]{3,2,0,1:T(8,128)(2,1)} %get-tuple-element.48, bf16[16,2,48,512]{3,2,0,1:T(8,128)(2,1)} %get-tuple-element.47), kind=kOutput, calls=%fused_computation.91 | convolution fusion | flops 3227516928 | bytes 14680064 | tf_op jit(solution)/shard_map/oecd,oecf->edf/dot_general | solution.py:279
  420.1 24.6 %all-to-all-done.6 = bf16[16,2,48,1024]{3,2,1,0:T(8,128)(2,1)} async-done(((bf16[16,2,48,1024]{3,2,1,0:T(8,128)(2,1)}), bf16[16,2,48,1024]{3,2,1,0:T(8,128)(2,1)}, u32[]{:S(2)}, u32[]{:S(2)}) %all-to-all-start.6) | async-done | bytes 3145760 | tf_op jit(solution)/shard_map/all_to_all | solution.py:260
  489.1 16.1 %all-to-all-done.3 = bf16[16,2,48,1024]{3,2,1,0:T(8,128)(2,1)} async-done(((bf16[16,2,48,1024]{3,2,1,0:T(8,128)(2,1)}), bf16[16,2,48,1024]{3,2,1,0:T(8,128)(2,1)}, u32[]{:S(2)}, u32[]{:S(2)}) %all-to-all-start.3) | async-done | bytes 3145760 | tf_op jit(solution)/shard_map/all_to_all | solution.py:230
  529.2 22.7 %all-to-all-done.7 = bf16[16,2,48,1024]{3,2,1,0:T(8,128)(2,1)} async-done(((bf16[16,2,48,1024]{3,2,1,0:T(8,128)(2,1)}), bf16[16,2,48,1024]{3,2,1,0:T(8,128)(2,1)}, u32[]{:S(2)}, u32[]{:S(2)}) %all-to-all-start.7) | async-done | bytes 3145760 | tf_op jit(solution)/shard_map/all_to_all | solution.py:285
  650.9 23.0 %reduce-scatter.7.cloned.1.call-done = bf16[2,128,512]{2,1,0:T(8,128)(2,1)} async-done(((bf16[2,1024,512]{2,1,0:T(8,128)(2,1)}), bf16[2,128,512]{2,1,0:T(8,128)(2,1)}) %reduce-scatter.7.cloned.1.call-update) | async-done | bytes 262160 | tf_op jit(solution)/shard_map/reduce_scatter | solution.py:38
  675.7 33.8 %reduce-scatter.9.cloned.1.call-done = bf16[2,128,512]{2,1,0:T(8,128)(2,1)} async-done(((bf16[2,1024,512]{2,1,0:T(8,128)(2,1)}), bf16[2,128,512]{2,1,0:T(8,128)(2,1)}) %reduce-scatter.9.cloned.1.call-update) | async-done | bytes 262160 | tf_op jit(solution)/shard_map/reduce_scatter | solution.py:38
  737.3 9.5 %concatenate.209 = bf16[1024,3074]{1,0:T(8,128)(2,1)} concatenate(bf16[1024,2048]{1,0:T(8,128)(2,1)} %add_convert_fusion, bf16[1024,1024]{1,0:T(8,128)(2,1)S(1)} %add_convert_fusion.1, bf16[1024,1]{1,0:T(8,128)(2,1)} %convert_element_type.594, bf16[1024,1]{1,0:T(8,128)(2,1)S(1)} %copy-done.74), dimensions={1} | concatenate | bytes 12591104 | tf_op jit(solution)/shard_map/concatenate | solution.py:44
  750.7 9.3 %reshape.1512 = f32[2,1024,1024]{2,1,0:T(8,128)} reshape(f32[2097152]{0:T(1024)} %slice_convert_fusion) | data formatting | bytes 16777216 | tf_op jit(solution)/shard_map/convert_element_type | solution.py:423
  768.9 20.7 %reduce-scatter.11.cloned.1.call-done = bf16[128,3074]{1,0:T(8,128)(2,1)} async-done(((bf16[1024,3074]{1,0:T(8,128)(2,1)}), bf16[128,3074]{1,0:T(8,128)(2,1)}) %reduce-scatter.11.cloned.1.call-update) | async-done | bytes 786960 | tf_op jit(solution)/shard_map/reduce_scatter | solution.py:45
  793.1 13.7 %all-reduce.10 = (bf16[64]{0:T(256)(128)(2,1)S(1)}, bf16[64]{0:T(256)(128)(2,1)S(1)}) all-reduce(bf16[64]{0:T(256)(128)(2,1)S(1)} %copy-done.134, bf16[64]{0:T(256)(128)(2,1)S(1)} %add_convert_fusion.10), channel_id=5, replica_groups=mesh['dp'=8,'expert'=16] {'dp'}, use_global_device_ids=true, to_apply=%region_57.59.clone | all-reduce | flops 128 | bytes 512
  810.8 74.9 %all-reduce.8 = (bf16[128]{0:T(256)(128)(2,1)S(1)}, bf16[128]{0:T(256)(128)(2,1)S(1)}, bf16[8]{0:T(256)(128)(2,1)S(1)}, bf16[8]{0:T(256)(128)(2,1)S(1)}, bf16[128,32]{0,1:T(8,128)(2,1)S(1)}) all-reduce(bf16[128]{0:T(256)(128)(2,1)S(1)} %get-tuple-element.27, ...), channel_id=1, replica_groups=mesh['dp'=8,'expert'=16] {'expert'}, use_global_device_ids=true, to_apply=%region_53.55 | all-reduce | flops 4368 | bytes 17472 | tf_op jit(solution)/shard_map/psum | solution.py:415
  (620 shorter events, 441.2 us)
Async XLA Ops:
  7.2 214.3 %copy-start = (bf16[2,512,1024]{2,1,0:T(8,128)(2,1)S(1)}, bf16[2,512,1024]{2,1,0:T(8,128)(2,1)}, u32[]{:S(2)}) copy-start(bf16[2,512,1024]{2,1,0:T(8,128)(2,1)} %param.27) | copy-start | bytes 6291460
  7.2 50.0 %copy-start.15 = (bf16[2,1,128,1024]{3,2,1,0:T(8,128)(2,1)S(1)}, bf16[2,1,128,1024]{3,2,1,0:T(8,128)(2,1)}, u32[]{:S(2)}) copy-start(bf16[2,1,128,1024]{3,2,1,0:T(8,128)(2,1)} %param.15) | copy-start | bytes 1572868
  7.2 48.5 %all-gather.4.cloned.1.call-start = ((), (), s32[]{:S(2)}) async-start(), calls=%async_computation.12 | async-start | bytes 7372800 | tf_op jit(solution)/shard_map/all_gather | solution.py:18
  11.0 80.1 %all-gather.6.cloned.1.call-start = ((), (), s32[]{:S(2)}) async-start(), calls=%async_computation.13 | async-start | bytes 2359296 | tf_op jit(solution)/shard_map/all_gather | solution.py:28
  32.4 56.6 %copy-start.80 = (f32[128,32]{0,1:T(8,128)}, f32[128,32]{0,1:T(8,128)S(1)}, u32[]{:S(2)}) copy-start(f32[128,32]{0,1:T(8,128)S(1)} %get-tuple-element.114) | copy-start | bytes 49156
  89.9 196.0 %copy-start.63 = (bf16[1,128,16,32]{1,3,2,0:T(8,128)(2,1)}, bf16[1,128,16,32]{1,3,2,0:T(8,128)(2,1)S(1)}, u32[]{:S(2)}) copy-start(bf16[1,128,16,32]{1,3,2,0:T(8,128)(2,1)S(1)} %get-tuple-element.93) | copy-start | bytes 393220
  114.6 55.8 %all-to-all-start = ((bf16[16,2,48,1024]{3,2,1,0:T(8,128)(2,1)}), bf16[16,2,48,1024]{3,2,1,0:T(8,128)(2,1)}, u32[]{:S(2)}, u32[]{:S(2)}) async-start(bf16[16,2,48,1024]{3,2,1,0:T(8,128)(2,1)} %bitcast.487), calls=%async_computation | async-start | bytes 6291456 | tf_op jit(solution)/shard_map/all_to_all | solution.py:219
  170.4 51.0 %all-to-all-start.4 = ((bf16[16,2,48,1024]{3,2,1,0:T(8,128)(2,1)}), bf16[16,2,48,1024]{3,2,1,0:T(8,128)(2,1)}, u32[]{:S(2)}, u32[]{:S(2)}) async-start(bf16[16,2,48,1024]{3,2,1,0:T(8,128)(2,1)} %bitcast.488), calls=%async_computation.4 | async-start | bytes 6291456 | tf_op jit(solution)/shard_map/all_to_all | solution.py:260
  175.1 78.1 %all-gather.8.cloned.1.call-start = ((), (), s32[]{:S(2)}) async-start(), calls=%async_computation.14 | async-start | bytes 2359296 | tf_op jit(solution)/shard_map/all_gather | solution.py:28
  232.7 48.2 %all-to-all-start.1 = ((bf16[16,2,48,1024]{3,2,1,0:T(8,128)(2,1)}), bf16[16,2,48,1024]{3,2,1,0:T(8,128)(2,1)}, u32[]{:S(2)}, u32[]{:S(2)}) async-start(bf16[16,2,48,1024]{3,2,1,0:T(8,128)(2,1)} %copy.324), calls=%async_computation.1 | async-start | bytes 6291456 | tf_op jit(solution)/shard_map/all_to_all | solution.py:230
  280.9 47.5 %all-to-all-start.5 = ((bf16[16,2,48,1024]{3,2,1,0:T(8,128)(2,1)}), bf16[16,2,48,1024]{3,2,1,0:T(8,128)(2,1)}, u32[]{:S(2)}, u32[]{:S(2)}) async-start(bf16[16,2,48,1024]{3,2,1,0:T(8,128)(2,1)} %copy.339), calls=%async_computation.5 | async-start | bytes 6291456 | tf_op jit(solution)/shard_map/all_to_all | solution.py:285
  348.4 48.3 %all-to-all-start.2 = ((bf16[16,2,48,1024]{3,2,1,0:T(8,128)(2,1)}), bf16[16,2,48,1024]{3,2,1,0:T(8,128)(2,1)}, u32[]{:S(2)}, u32[]{:S(2)}) async-start(bf16[16,2,48,1024]{3,2,1,0:T(8,128)(2,1)} %bitcast.486), calls=%async_computation.2 | async-start | bytes 6291456 | tf_op jit(solution)/shard_map/all_to_all | solution.py:219
  396.8 48.0 %all-to-all-start.6 = ((bf16[16,2,48,1024]{3,2,1,0:T(8,128)(2,1)}), bf16[16,2,48,1024]{3,2,1,0:T(8,128)(2,1)}, u32[]{:S(2)}, u32[]{:S(2)}) async-start(bf16[16,2,48,1024]{3,2,1,0:T(8,128)(2,1)} %bitcast.489), calls=%async_computation.7 | async-start | bytes 6291456 | tf_op jit(solution)/shard_map/all_to_all | solution.py:260
  456.2 49.0 %all-to-all-start.3 = ((bf16[16,2,48,1024]{3,2,1,0:T(8,128)(2,1)}), bf16[16,2,48,1024]{3,2,1,0:T(8,128)(2,1)}, u32[]{:S(2)}, u32[]{:S(2)}) async-start(bf16[16,2,48,1024]{3,2,1,0:T(8,128)(2,1)} %copy.335), calls=%async_computation.3 | async-start | bytes 6291456 | tf_op jit(solution)/shard_map/all_to_all | solution.py:230
  505.2 46.7 %all-to-all-start.7 = ((bf16[16,2,48,1024]{3,2,1,0:T(8,128)(2,1)}), bf16[16,2,48,1024]{3,2,1,0:T(8,128)(2,1)}, u32[]{:S(2)}, u32[]{:S(2)}) async-start(bf16[16,2,48,1024]{3,2,1,0:T(8,128)(2,1)} %copy.360), calls=%async_computation.8 | async-start | bytes 6291456 | tf_op jit(solution)/shard_map/all_to_all | solution.py:285
  509.7 134.5 %reduce-scatter.13.cloned.1.call-start = ((), (), s32[]{:S(2)}) async-start(), calls=%async_computation.19 | async-start | bytes 294912
  521.0 124.6 %all-reduce.15.cloned.1.call-start = ((), (), s32[]{:S(2)}) async-start(), calls=%async_computation.18 | async-start | bytes 12582912 | tf_op jit(solution)/shard_map/psum | solution.py:55
  529.1 144.8 %reduce-scatter.7.cloned.1.call-start = ((), (), s32[]{:S(2)}) async-start(), calls=%async_computation.15 | async-start | bytes 2359296 | tf_op jit(solution)/shard_map/reduce_scatter | solution.py:38
  592.8 116.7 %reduce-scatter.9.cloned.1.call-start = ((), (), s32[]{:S(2)}) async-start(), calls=%async_computation.16 | async-start | bytes 2359296 | tf_op jit(solution)/shard_map/reduce_scatter | solution.py:38
  635.8 153.7 %reduce-scatter.11.cloned.1.call-start = ((), (), s32[]{:S(2)}) async-start(), calls=%async_computation.17 | async-start | bytes 7372800 | tf_op jit(solution)/shard_map/reduce_scatter | solution.py:45
  650.9 62.2 %copy-start.44 = (f32[128,512]{0,1:T(8,128)S(1)}, f32[128,512]{0,1:T(8,128)}, u32[]{:S(2)}) copy-start(f32[128,512]{0,1:T(8,128)} %copy-done.43) | copy-start | bytes 786436
  746.8 141.5 %all-reduce.17.cloned.1.call-start = ((), (), s32[]{:S(2)}) async-start(), calls=%async_computation.20 | async-start | bytes 1572864 | tf_op jit(solution)/shard_map/psum | solution.py:413
  768.8 41.9 %copy-start.93 = (bf16[128,32]{0,1:T(8,128)(2,1)S(1)}, bf16[128,32]{0,1:T(8,128)(2,1)}, u32[]{:S(2)}) copy-start(bf16[128,32]{0,1:T(8,128)(2,1)} %copy.421) | copy-start | bytes 24580
  807.0 85.2 %copy-start.1 = (bf16[2,512,1024]{2,1,0:T(8,128)(2,1)S(1)}, bf16[2,512,1024]{2,1,0:T(8,128)(2,1)}, u32[]{:S(2)}) copy-start(bf16[2,512,1024]{2,1,0:T(8,128)(2,1)} %param.27) | copy-start | bytes 6291460
  (141 other events, 1123.1 us)
Sparse Core Ops, SparseCore 0:
  11.1 44.5 all-gather.3
  65.8 25.2 all-gather.5
  178.2 25.5 all-gather.7
  521.2 31.4 reduce-scatter.12
  554.9 83.1 all-reduce.14
  640.5 33.3 reduce-scatter.6
  677.0 32.4 reduce-scatter.8
  746.9 42.5 reduce-scatter.10
  793.8 85.9 all-reduce.16
where the time goes:
time: 907 us; the launch traced here: 899 us
  waiting for transfers between devices  244 us (27%)
  local copies, waits for them, and re-layouts  224 us (25%)
  matrix products  148 us (16%)
  blocking collectives  115 us (13%)
  other arithmetic  107 us (12%)
  starting transfers between devices  43.1 us (5%)
  between operations  17.9 us (2%)
    psum x1, blocking collectives, body(): lax.psum(shard_part[2].astype(jnp.bfloat16), 'expert').astype(jnp.float32)  74.9 us
    all_to_all x2, waiting for transfers between devices, body(): lax.all_to_all(grad_outgoing, 'expert', split_axis=0, concat_axis=0, tile...  59.6 us
    reduce_scatter x2, waiting for transfers between devices, in_one_piece_2(): filled = lax.psum_scatter(both, axis, scatter_dimension=dim, tiled=True)  56.9 us
    all_to_all x2, waiting for transfers between devices, body(): lax.all_to_all(grad_rows, 'expert', split_axis=0, concat_axis=0, tiled=True)  34.7 us
    all_to_all x2, waiting for transfers between devices, body(): lax.all_to_all(expert_out, 'expert', split_axis=0, concat_axis=0, tiled=T...  30.3 us
    unnamed x2, blocking collectives  28.7 us
    another operation x12, other arithmetic  27.3 us
    unnamed x309, local copies, waits for them, and re-layouts  25.4 us
  transfers between devices with their start and end apart: 17, of which 13 were waited for; matrix products, arithmetic and copies ran while one was open for 40% of the time, Pallas kernels for 0%

commit v1 on v0

--- a/solution.py
+++ b/solution.py
@@ -1,6 +1,8 @@
 import jax
 import jax.numpy as jnp
 from jax import lax
+from jax.experimental import pallas as pl
+from jax.experimental.pallas import tpu as pltpu
 from jax.sharding import PartitionSpec as P
 
 HD = 64
@@ -86,6 +88,487 @@
     frequency = jnp.power(THETA, -2.0 * jnp.arange(HD // 2, dtype=jnp.float32) / HD)
     turned = positions[:, None] * frequency[None, :]
     return (jnp.cos(turned)[:, None, :], jnp.sin(turned)[:, None, :])
+
+
+BF = jnp.bfloat16
+F32 = jnp.float32
+SLOTS = 48
+CHUNK = 256
+
+
+def nn(a, b):
+    return lax.dot_general(a, b, (((1,), (0,)), ((), ())), preferred_element_type=F32)
+
+
+def nt(a, b):
+    return lax.dot_general(a, b, (((1,), (1,)), ((), ())), preferred_element_type=F32)
+
+
+def tn(a, b):
+    return lax.dot_general(a, b, (((0,), (0,)), ((), ())), preferred_element_type=F32)
+
+
+class Plane:
+    def __init__(self):
+        self.me = lax.axis_index("expert")
+        self.z = self.me // 4
+        self.x = self.me % 4
+
+    def own(self, half):
+        return (self.x, self.z) if half == 0 else (self.z, self.x)
+
+    def device(self, half, p, q):
+        return {"expert": q * 4 + p if half == 0 else p * 4 + q}
+
+    def barrier(self):
+        sem = pltpu.get_barrier_semaphore()
+        for step in range(1, 16):
+            pl.semaphore_signal(sem, inc=1, device_id={"expert": (self.me + step) % 16})
+        pl.semaphore_wait(sem, 15)
+
+
+def at(ref, half, p, q, rows):
+    return ref.at[q, p, rows] if half == 0 else ref.at[p, q, rows]
+
+
+def line(ref, half, q, rows):
+    return ref.at[q, :, rows] if half == 0 else ref.at[:, q, rows]
+
+
+def next_to(p):
+    return (p + 1) % 4, (p + 3) % 4, (p + 2) % 4
+
+
+def full_rows(half):
+    return pl.ds(64 * half, 64)
+
+
+def part_rows(half, part):
+    return pl.ds(64 * half + 32 * part, 32)
+
+
+class Gather:
+    def __init__(self, plane, ref, send, recv):
+        self.plane, self.ref, self.send, self.recv = plane, ref, send, recv
+
+    def message(self, half, i):
+        p, q = self.plane.own(half)
+        pn, pp, _ = next_to(p)
+        qn, qp, _ = next_to(q)
+        ref, full = self.ref, full_rows(half)
+        first, second = part_rows(half, 0), part_rows(half, 1)
+        view, to = [
+            lambda: (at(ref, half, p, q, full), (pn, q)),
+            lambda: (at(ref, half, p, q, full), (pp, q)),
+            lambda: (at(ref, half, pp, q, first), (pn, q)),
+            lambda: (at(ref, half, pn, q, second), (pp, q)),
+            lambda: (line(ref, half, q, full), (p, qn)),
+            lambda: (line(ref, half, q, full), (p, qp)),
+            lambda: (line(ref, half, qp, first), (p, qn)),
+            lambda: (line(ref, half, qn, second), (p, qp)),
+        ][i]()
+        return pltpu.make_async_remote_copy(
+            src_ref=view,
+            dst_ref=view,
+            send_sem=self.send.at[half, i],
+            recv_sem=self.recv.at[half, i],
+            device_id=self.plane.device(half, *to),
+        )
+
+    def step(self, n):
+        waits, starts = [
+            ((), (0, 1)),
+            ((0, 1), (2, 3)),
+            ((2, 3), (4, 5)),
+            ((4, 5), (6, 7)),
+            ((6, 7), ()),
+        ][n]
+        for half in range(2):
+            for i in waits:
+                self.message(half, i).wait_recv()
+            for i in starts:
+                self.message(half, i).start()
+        if n == 4:
+            for half in range(2):
+                for i in range(8):
+                    self.message(half, i).wait_send()
+
+
+class Scatter:
+    def __init__(self, plane, ref, r1, r2, r3, r4, send, recv, free, out):
+        self.plane, self.ref, self.out = plane, ref, out
+        self.r1, self.r2, self.r3, self.r4 = r1, r2, r3, r4
+        self.send, self.recv, self.free = send, recv, free
+
+    def message(self, half, i):
+        p, q = self.plane.own(half)
+        pn, pp, po = next_to(p)
+        qn, qp, qo = next_to(q)
+        ref, full = self.ref, full_rows(half)
+        first, second = part_rows(half, 0), part_rows(half, 1)
+        view, slot, to = [
+            lambda: (line(ref, half, qo, first), self.r1.at[half, 0], (p, qn)),
+            lambda: (line(ref, half, qo, second), self.r1.at[half, 1], (p, qp)),
+            lambda: (line(ref, half, qn, full), self.r2.at[half, 0], (p, qn)),
+            lambda: (line(ref, half, qp, full), self.r2.at[half, 1], (p, qp)),
+            lambda: (at(ref, half, po, q, first), self.r3.at[half, 0], (pn, q)),
+            lambda: (at(ref, half, po, q, second), self.r3.at[half, 1], (pp, q)),
+            lambda: (at(ref, half, pn, q, full), self.r4.at[half, 0], (pn, q)),
+            lambda: (at(ref, half, pp, q, full), self.r4.at[half, 1], (pp, q)),
+        ][i]()
+        return pltpu.make_async_remote_copy(
+            src_ref=view,
+            dst_ref=slot,
+            send_sem=self.send.at[half, i],
+            recv_sem=self.recv.at[half, i],
+            device_id=self.plane.device(half, *to),
+        )
+
+    def add_line(self, half, q, offset, count, slots):
+        @pl.loop(0, 4)
+        def _(j):
+            @pl.loop(0, count // 16)
+            def _(k):
+                rows = pl.ds(pl.multiple_of(offset + k * 16, 16), 16)
+                place = (q, j, rows) if half == 0 else (j, q, rows)
+                total = self.ref[place].astype(F32)
+                for slot in slots:
+                    total += self.r_line(half, slot, j, k)
+                self.ref[place] = total.astype(BF)
+
+    def r_line(self, half, slot, j, k):
+        ref, side = slot
+        return ref[half, side, j, pl.ds(pl.multiple_of(k * 16, 16), 16)].astype(F32)
+
+    def add_at(self, half, p, q, part, slot):
+        @pl.loop(0, 2)
+        def _(k):
+            rows = pl.ds(pl.multiple_of(64 * half + 32 * part + k * 16, 16), 16)
+            place = (q, p, rows) if half == 0 else (p, q, rows)
+            ref, side = slot
+            got = ref[half, side, pl.ds(pl.multiple_of(k * 16, 16), 16)].astype(F32)
+            self.ref[place] = (self.ref[place].astype(F32) + got).astype(BF)
+
+    def step(self, n):
+        for half in range(2):
+            p, q = self.plane.own(half)
+            pn, pp, po = next_to(p)
+            qn, qp, qo = next_to(q)
+            if n == 0:
+                self.message(half, 0).start()
+                self.message(half, 1).start()
+            elif n == 1:
+                self.message(half, 0).wait_recv()
+                self.add_line(half, qn, 64 * half, 32, [(self.r1, 0)])
+                self.message(half, 2).start()
+                self.message(half, 1).wait_recv()
+                self.add_line(half, qp, 64 * half + 32, 32, [(self.r1, 1)])
+                self.message(half, 3).start()
+            elif n == 2:
+                self.message(half, 2).wait_recv()
+                self.message(half, 3).wait_recv()
+                self.add_line(half, q, 64 * half, 64, [(self.r2, 0), (self.r2, 1)])
+                self.message(half, 4).start()
+                self.message(half, 5).start()
+            elif n == 3:
+                self.message(half, 4).wait_recv()
+                self.add_at(half, pn, q, 0, (self.r3, 0))
+                self.message(half, 6).start()
+                self.message(half, 5).wait_recv()
+                self.add_at(half, pp, q, 1, (self.r3, 1))
+                self.message(half, 7).start()
+            elif n == 4:
+                self.message(half, 6).wait_recv()
+                self.message(half, 7).wait_recv()
+
+                @pl.loop(0, 4)
+                def _(k):
+                    rows = pl.ds(pl.multiple_of(64 * half + k * 16, 16), 16)
+                    place = (q, p, rows) if half == 0 else (p, q, rows)
+                    some = pl.ds(pl.multiple_of(k * 16, 16), 16)
+                    total = self.ref[place].astype(F32)
+                    total += self.r4[half, 0, some].astype(F32)
+                    total += self.r4[half, 1, some].astype(F32)
+                    self.out[rows] = total
+        if n == 4:
+            for half in range(2):
+                for i in range(8):
+                    self.message(half, i).wait_send()
+
+    def give_credit(self):
+        for half in range(2):
+            p, q = self.plane.own(half)
+            for to in (p + 1) % 4, (p + 3) % 4:
+                pl.semaphore_signal(self.free, inc=1, device_id=self.plane.device(half, to, q))
+
+    def take_credit(self):
+        pl.semaphore_wait(self.free, 4)
+
+
+def moe_kernel(
+    ffn_ref, cot_ref, gates_ref, wgu_hbm, wd_hbm,
+    out_ref, dx_ref, h_ref, dgu_ref, dd_ref,
+    x_all, dy_all, r1, r2, r3, r4, xs, ds, os, act, a1, a2, ggu, g_all, ranks, hcol, hs,
+    wgu, wd, send, recv, gsend, grecv, hsend, hrecv, free, local,
+):
+    plane = Plane()
+    me, z, x = plane.me, plane.z, plane.x
+    w1 = pltpu.make_async_copy(wgu_hbm, wgu, local.at[0])
+    w2 = pltpu.make_async_copy(wd_hbm, wd, local.at[1])
+    w1.start()
+    w2.start()
+    own = []
+    for mb in range(2):
+        own.append(pltpu.make_async_copy(cot_ref.at[mb], dy_all.at[mb, z, x], local.at[2 + mb]))
+        own.append(pltpu.make_async_copy(ffn_ref.at[mb], x_all.at[mb, z, x], local.at[4 + mb]))
+    for copy in own:
+        copy.start()
+    plane.barrier()
+    for copy in own:
+        copy.wait()
+
+    def gate_message(step):
+        to = (me + step) % 16
+        return pltpu.make_async_remote_copy(
+            src_ref=gates_ref.at[to], dst_ref=g_all.at[me],
+            send_sem=gsend.at[step], recv_sem=grecv.at[step], device_id={"expert": to},
+        )
+
+    def h_message(step):
+        to = (me + step) % 16
+        return pltpu.make_async_remote_copy(
+            src_ref=hs.at[to], dst_ref=h_ref.at[me],
+            send_sem=hsend.at[step], recv_sem=hrecv.at[step], device_id={"expert": to},
+        )
+
+    for step in range(1, 16):
+        gate_message(step).start()
+    g_all[me] = gates_ref[me]
+    gx = [Gather(plane, x_all.at[mb], send.at[mb], recv.at[mb]) for mb in range(2)]
+    gdy = [Gather(plane, dy_all.at[mb], send.at[2 + mb], recv.at[2 + mb]) for mb in range(2)]
+    sout = [
+        Scatter(plane, x_all.at[mb], r1.at[0], r2.at[0], r3.at[0], r4.at[0],
+                send.at[4 + mb], recv.at[4 + mb], free.at[0], out_ref.at[mb])
+        for mb in range(2)
+    ]
+    sdx = [
+        Scatter(plane, dy_all.at[mb], r1.at[1], r2.at[1], r3.at[1], r4.at[1],
+                send.at[6 + mb], recv.at[6 + mb], free.at[1], dx_ref.at[mb])
+        for mb in range(2)
+    ]
+    for n in range(5):
+        gx[0].step(n)
+        gdy[0].step(n)
+    gx[1].step(0)
+    gdy[1].step(0)
+    for step in range(1, 16):
+        gate_message(step).wait_recv()
+    for step in range(1, 16):
+        gate_message(step).wait_send()
+
+    earlier = (
+        lax.broadcasted_iota(jnp.int32, (128, 128), 0)
+        < lax.broadcasted_iota(jnp.int32, (128, 128), 1)
+    ).astype(F32).astype(BF)
+
+    @pl.loop(0, 16)
+    def _(s):
+        named = g_all[s] > 0.0
+        before = nn(named.astype(F32).astype(BF), earlier)
+        ranks[s] = jnp.where(named, before, -1.0)
+
+    slot_ids = lax.broadcasted_iota(jnp.int32, (SLOTS, 128), 0).astype(F32)
+
+    def places(s, mb):
+        r = ranks[s]
+        return [(slot_ids == r[2 * mb + e : 2 * mb + e + 1]).astype(F32) for e in range(2)]
+
+    def gated(s, mb, hot):
+        g = g_all[s]
+        return [hot[e] * g[2 * mb + e : 2 * mb + e + 1] for e in range(2)]
+
+    def span(s):
+        return pl.ds(pl.multiple_of(s * SLOTS, 16), SLOTS)
+
+    def select(mb):
+        @pl.loop(0, 16)
+        def _(s):
+            hot = places(s, mb)
+            pick = jnp.concatenate(hot, axis=0).astype(BF)
+            scaled = jnp.concatenate(gated(s, mb, hot), axis=0).astype(BF)
+            rows = nn(pick, x_all[mb, s // 4, s % 4]).astype(BF)
+            drows = nn(scaled, dy_all[mb, s // 4, s % 4]).astype(BF)
+            for e in range(2):
+                xs[e, span(s)] = rows[SLOTS * e : SLOTS * (e + 1)]
+                ds[e, span(s)] = drows[SLOTS * e : SLOTS * (e + 1)]
+
+    chunks = 16 * SLOTS // CHUNK
+
+    def forward(e):
+        @pl.loop(0, chunks)
+        def _(c):
+            r = pl.ds(pl.multiple_of(c * CHUNK, CHUNK), CHUNK)
+            gu = nn(xs[e, r], wgu[e])
+            g, u = gu[:, :512], gu[:, 512:]
+            sig = 1.0 / (1.0 + jnp.exp(-g))
+            silu = g * sig
+            active = (silu * u).astype(BF)
+            act[e, r] = active
+            a1[e, r] = (u * sig * (1.0 + g * (1.0 - sig))).astype(BF)
+            a2[e, r] = silu.astype(BF)
+            o = nn(active, wd[e]).astype(BF)
+            os[e, r] = o
+            hcol[e, r] = jnp.sum(o.astype(F32) * ds[e, r].astype(F32), axis=-1, keepdims=True)
+
+    def combine_out(mb):
+        @pl.loop(0, 16)
+        def _(s):
+            hot = places(s, mb)
+            scaled = jnp.concatenate(gated(s, mb, hot), axis=0).astype(BF)
+            both = jnp.concatenate([os[0, span(s)], os[1, span(s)]], axis=0)
+            x_all[mb, s // 4, s % 4] = tn(scaled, both).astype(BF)
+            for e in range(2):
+                row = 2 * mb + e
+                hs[s, row : row + 1] = jnp.sum(hot[e] * hcol[e, span(s)], axis=0, keepdims=True)
+
+    def backward(mb, e):
+        @pl.loop(0, chunks)
+        def _(c):
+            r = pl.ds(pl.multiple_of(c * CHUNK, CHUNK), CHUNK)
+            ga = nt(ds[e, r], wd[e])
+            grad = jnp.concatenate(
+                [ga * a1[e, r].astype(F32), ga * a2[e, r].astype(F32)], axis=1
+            ).astype(BF)
+            ggu[r] = grad
+            os[e, r] = nt(grad, wgu[e]).astype(BF)
+
+        @pl.loop(0, 4)
+        def _(m):
+            cols = pl.ds(pl.multiple_of(m * 256, 256), 256)
+            fresh = tn(xs[e, :, cols], ggu[...])
+            dgu_ref[e, cols] = fresh if mb == 0 else dgu_ref[e, cols] + fresh
+
+        @pl.loop(0, 2)
+        def _(m):
+            cols = pl.ds(pl.multiple_of(m * 256, 256), 256)
+            fresh = tn(act[e, :, cols], ds[e])
+            dd_ref[e, cols] = fresh if mb == 0 else dd_ref[e, cols] + fresh
+
+    def combine_dx(mb):
+        @pl.loop(0, 16)
+        def _(s):
+            pick = jnp.concatenate(places(s, mb), axis=0).astype(BF)
+            both = jnp.concatenate([os[0, span(s)], os[1, span(s)]], axis=0)
+            dy_all[mb, s // 4, s % 4] = tn(pick, both).astype(BF)
+
+    w1.wait()
+    w2.wait()
+    select(0)
+    gx[1].step(1)
+    gdy[1].step(1)
+    forward(0)
+    gx[1].step(2)
+    gdy[1].step(2)
+    forward(1)
+    combine_out(0)
+    gx[1].step(3)
+    gdy[1].step(3)
+    sout[0].step(0)
+    backward(0, 0)
+    gx[1].step(4)
+    gdy[1].step(4)
+    sout[0].step(1)
+    backward(0, 1)
+    combine_dx(0)
+    sout[0].step(2)
+    sdx[0].step(0)
+    select(1)
+    sout[0].step(3)
+    sdx[0].step(1)
+    forward(0)
+    sout[0].step(4)
+    sout[0].give_credit()
+    sdx[0].step(2)
+    forward(1)
+    sdx[0].step(3)
+    combine_out(1)
+    hs_own = hs[me]
+    h_ref[me] = hs_own
+    for step in range(1, 16):
+        h_message(step).start()
+    sout[1].take_credit()
+    sout[1].step(0)
+    sdx[0].step(4)
+    sdx[0].give_credit()
+    backward(1, 0)
+    sout[1].step(1)
+    backward(1, 1)
+    sout[1].step(2)
+    combine_dx(1)
+    sdx[1].take_credit()
+    sdx[1].step(0)
+    sout[1].step(3)
+    sdx[1].step(1)
+    sout[1].step(4)
+    for n in range(2, 5):
+        sdx[1].step(n)
+    for step in range(1, 16):
+        h_message(step).wait_recv()
+    for step in range(1, 16):
+        h_message(step).wait_send()
+
+
+def moe(ffn, cot, gates, w_gate_up, w_down):
+    vmem = pl.BlockSpec(memory_space=pltpu.VMEM)
+    anywhere = pl.BlockSpec(memory_space=pl.ANY)
+    rows = 16 * SLOTS
+    return pl.pallas_call(
+        moe_kernel,
+        out_shape=(
+            jax.ShapeDtypeStruct((2, 128, 1024), F32),
+            jax.ShapeDtypeStruct((2, 128, 1024), F32),
+            jax.ShapeDtypeStruct((16, 8, 128), F32),
+            jax.ShapeDtypeStruct((2, 1024, 1024), F32),
+            jax.ShapeDtypeStruct((2, 512, 1024), F32),
+        ),
+        in_specs=[anywhere, anywhere, vmem, anywhere, anywhere],
+        out_specs=(vmem,) * 5,
+        scratch_shapes=[
+            pltpu.VMEM((2, 4, 4, 128, 1024), BF),
+            pltpu.VMEM((2, 4, 4, 128, 1024), BF),
+            pltpu.VMEM((2, 2, 2, 4, 32, 1024), BF),
+            pltpu.VMEM((2, 2, 2, 4, 64, 1024), BF),
+            pltpu.VMEM((2, 2, 2, 32, 1024), BF),
+            pltpu.VMEM((2, 2, 2, 64, 1024), BF),
+            pltpu.VMEM((2, rows, 1024), BF),
+            pltpu.VMEM((2, rows, 1024), BF),
+            pltpu.VMEM((2, rows, 1024), BF),
+            pltpu.VMEM((2, rows, 512), BF),
+            pltpu.VMEM((2, rows, 512), BF),
+            pltpu.VMEM((2, rows, 512), BF),
+            pltpu.VMEM((rows, 1024), BF),
+            pltpu.VMEM((16, 8, 128), F32),
+            pltpu.VMEM((16, 8, 128), F32),
+            pltpu.VMEM((2, rows, 1), F32),
+            pltpu.VMEM((16, 8, 128), F32),
+            pltpu.VMEM((2, 1024, 1024), BF),
+            pltpu.VMEM((2, 512, 1024), BF),
+            pltpu.SemaphoreType.DMA((8, 2, 8)),
+            pltpu.SemaphoreType.DMA((8, 2, 8)),
+            pltpu.SemaphoreType.DMA((16,)),
+            pltpu.SemaphoreType.DMA((16,)),
+            pltpu.SemaphoreType.DMA((16,)),
+            pltpu.SemaphoreType.DMA((16,)),
+            pltpu.SemaphoreType.REGULAR((2,)),
+            pltpu.SemaphoreType.DMA((6,)),
+        ],
+        compiler_params=pltpu.CompilerParams(
+            collective_id=0, has_side_effects=True, vmem_limit_bytes=63 * 1024 * 1024
+        ),
+        cost_estimate=pl.CostEstimate(
+            flops=30_000_000_000, bytes_accessed=30_000_000, transcendentals=2_000_000
+        ),
+    )(ffn, cot, gates, w_gate_up, w_down)
 
 
 def body(
@@ -110,41 +593,36 @@
     dp_size = lax.axis_size("dp")
     experts_all = experts_here * owners
     top_count = routes.shape[3]
-    hidden_units = w_down.shape[1]
     q_width = w_out.shape[0] * dp_size
     kv_width = (w_qkv.shape[1] - q_width) // 2
     kv_heads = kv_width // HD
     head_group = q_width // HD // kv_heads
     scaling = HD ** (-0.5)
     tok_rows = seq_count * query_rows
-    copy_rows = tok_rows * top_count
-    capacity = seq_count * max(2, query_rows * top_count * 3 // (2 * experts_all))
     dp_index = lax.axis_index("dp")
     cosine, sine_vals = angles((dp_index * query_rows + jnp.arange(query_rows)).astype(jnp.float32))
     expert_ids = jnp.arange(experts_all, dtype=jnp.int32)
-    zero_row = jnp.zeros((1, width), jnp.bfloat16)
     attn_totals = [
         jnp.zeros((piece.shape[0] * dp_size,) + piece.shape[1:], jnp.float32)
         for piece in (w_qkv, w_out, attn_norm, ffn_norm, q_gain, k_gain, router)
     ]
-    gate_up_total = jnp.zeros(w_gate_up.shape, jnp.float32)
-    down_total = jnp.zeros(w_down.shape, jnp.float32)
     outputs = []
     input_grads = []
+    kept = []
+    gathered = (
+        *in_one_piece((w_qkv, w_out, attn_norm, ffn_norm), "dp", 0, 1),
+        lax.all_gather(q_gain, "dp", axis=0, tiled=True),
+        lax.all_gather(k_gain, "dp", axis=0, tiled=True),
+        lax.all_gather(router, "dp", axis=0, tiled=True),
+    )
+    full_qkv, full_out, full_attn_norm, full_ffn_norm, full_q_gain, full_k_gain, full_router = (
+        gathered
+    )
+    attn_gain = full_attn_norm.astype(jnp.float32)
+    ffn_gain = full_ffn_norm.astype(jnp.float32)
+    query_gain = full_q_gain.astype(jnp.float32)
+    key_gain = full_k_gain.astype(jnp.float32)
     for micro_index in range(micro_count):
-        gathered = (
-            *in_one_piece((w_qkv, w_out, attn_norm, ffn_norm), "dp", 0, 1),
-            lax.all_gather(q_gain, "dp", axis=0, tiled=True),
-            lax.all_gather(k_gain, "dp", axis=0, tiled=True),
-            lax.all_gather(router, "dp", axis=0, tiled=True),
-        )
-        full_qkv, full_out, full_attn_norm, full_ffn_norm, full_q_gain, full_k_gain, full_router = (
-            gathered
-        )
-        attn_gain = full_attn_norm.astype(jnp.float32)
-        ffn_gain = full_ffn_norm.astype(jnp.float32)
-        query_gain = full_q_gain.astype(jnp.float32)
-        key_gain = full_k_gain.astype(jnp.float32)
         states = tokens[micro_index].astype(jnp.float32).reshape(tok_rows, width)
         normed, inv_attn = norm_rows(states, attn_gain)
         normed_low = normed.astype(jnp.bfloat16)
@@ -201,90 +679,55 @@
         ffn_low = ffn_normed.astype(jnp.bfloat16)
         logits = jnp.dot(ffn_low, full_router, preferred_element_type=jnp.float32)
         route_ids = routes[micro_index].reshape(tok_rows, top_count)
-        chosen = jnp.take_along_axis(logits, route_ids, axis=1)
-        gate_vals = jax.nn.softmax(chosen, axis=-1)
-        flat_ids = route_ids.reshape(copy_rows)
-        one_hot = (flat_ids[:, None] == expert_ids[None, :]).astype(jnp.int32)
-        earlier = jnp.cumsum(one_hot, axis=0) - one_hot
-        slot_ids = jnp.sum(earlier * one_hot, axis=1)
-        targets = flat_ids * capacity + slot_ids
-        sources = (
-            jnp.full((experts_all * capacity,), copy_rows, jnp.int32)
-            .at[targets]
-            .set(jnp.arange(copy_rows, dtype=jnp.int32))
-        )
-        token_of = jnp.where(sources < copy_rows, sources // top_count, tok_rows)
-        padded = jnp.concatenate([ffn_low, zero_row], axis=0)
-        outgoing = padded[token_of].reshape(owners, experts_here, capacity, width)
-        expert_piece = lax.all_to_all(outgoing, "expert", split_axis=0, concat_axis=0, tiled=True)
-        gate_up = jnp.einsum(
-            "oecd,edf->oecf", expert_piece, w_gate_up, preferred_element_type=jnp.float32
-        )
-        active = (jax.nn.silu(gate_up[..., :hidden_units]) * gate_up[..., hidden_units:]).astype(
-            jnp.bfloat16
-        )
-        result = jnp.einsum(
-            "oecf,efd->oecd", active, w_down, preferred_element_type=jnp.float32
-        ).astype(jnp.bfloat16)
-        expert_out, arrived, gate_up = (result, expert_piece, gate_up)
-        coming_back = lax.all_to_all(expert_out, "expert", split_axis=0, concat_axis=0, tiled=True)
-        picked = (
-            coming_back.reshape(experts_all * capacity, width)[targets]
-            .astype(jnp.float32)
-            .reshape(tok_rows, top_count, width)
-        )
-        final = residual + jnp.sum(gate_vals[:, :, None] * picked, axis=1)
+        route_hot = (route_ids[:, :, None] == expert_ids[None, None, :])
+        routed = jnp.any(route_hot, axis=1)
+        top = jnp.max(jnp.where(routed, logits, MASKED), axis=1, keepdims=True)
+        weight = jnp.where(routed, jnp.exp(logits - top), 0.0)
+        gates = weight / jnp.sum(weight, axis=1, keepdims=True)
+        kept.append((
+            states, normed_low, inv_attn, query_raw, key_raw, inv_query, inv_key, query_low,
+            key_all, value_all, same_doc, log_norm, mixed_low, residual, inv_ffn, ffn_low, gates,
+        ))
+    gates_sent = jnp.stack([k[-1].T.reshape(owners, experts_here, tok_rows) for k in kept], axis=1)
+    gates_sent = gates_sent.reshape(owners, micro_count * experts_here, tok_rows)
+    gates_sent = jnp.pad(gates_sent, ((0, 0), (0, 8 - micro_count * experts_here), (0, 0)))
+    moved_out, moved_dx, weighed, gate_up_total, down_total = moe(
+        jnp.stack([k[-2] for k in kept]),
+        cotangent.reshape(micro_count, tok_rows, width),
+        gates_sent,
+        w_gate_up,
+        w_down,
+    )
+    weighed = weighed[:, : micro_count * experts_here].reshape(
+        owners, micro_count, experts_here, tok_rows
+    )
+    for micro_index in range(micro_count):
+        (
+            states, normed_low, inv_attn, query_raw, key_raw, inv_query, inv_key, query_low,
+            key_all, value_all, same_doc, log_norm, mixed_low, residual, inv_ffn, ffn_low, gates,
+        ) = kept[micro_index]
+
+        def attn_scores():
+            raw_scores = (
+                jnp.einsum(
+                    "sqgrd,skgd->sgrqk", query_low, key_all, preferred_element_type=jnp.float32
+                )
+                * scaling
+            )
+            return jnp.where(same_doc, raw_scores, MASKED)
+
+        final = residual + moved_out[micro_index]
         outputs.append(final.astype(jnp.bfloat16).reshape(seq_count, query_rows, width))
         grad_final = cotangent[micro_index].astype(jnp.float32).reshape(tok_rows, width)
-        grad_gate = jnp.sum(picked * grad_final[:, None, :], axis=-1)
-        grad_chosen = gate_vals * (
-            grad_gate - jnp.sum(gate_vals * grad_gate, axis=-1, keepdims=True)
-        )
-        route_hot = (route_ids[:, :, None] == expert_ids[None, None, :]).astype(jnp.float32)
-        grad_logits = jnp.sum(grad_chosen[:, :, None] * route_hot, axis=1)
+        share = weighed[:, micro_index].reshape(experts_all, tok_rows).T
+        grad_logits = share - gates * jnp.sum(share, axis=1, keepdims=True)
         grad_router_now = jnp.einsum(
             "rd,re->de", ffn_low.astype(jnp.float32), grad_logits, precision=HIGHEST
         )
         grad_ffn_in = jnp.einsum(
             "re,de->rd", grad_logits, full_router.astype(jnp.float32), precision=HIGHEST
         )
-        grad_copies = (
-            (gate_vals[:, :, None] * grad_final[:, None, :])
-            .astype(jnp.bfloat16)
-            .reshape(copy_rows, width)
-        )
-        grad_padded = jnp.concatenate([grad_copies, zero_row], axis=0)
-        grad_outgoing = grad_padded[jnp.minimum(sources, copy_rows)].reshape(
-            owners, experts_here, capacity, width
-        )
-        grad_arrived = lax.all_to_all(
-            grad_outgoing, "expert", split_axis=0, concat_axis=0, tiled=True
-        )
-        gate_part = gate_up[..., :hidden_units]
-        up_part = gate_up[..., hidden_units:]
-        sigmoid_gate = jax.nn.sigmoid(gate_part)
-        silu_gate = gate_part * sigmoid_gate
-        active = (silu_gate * up_part).astype(jnp.bfloat16)
-        down_total = down_total + jnp.einsum(
-            "oecf,oecd->efd", active, grad_arrived, preferred_element_type=jnp.float32
-        )
-        grad_active = jnp.einsum(
-            "oecd,efd->oecf", grad_arrived, w_down, preferred_element_type=jnp.float32
-        )
-        grad_gate_part = (
-            grad_active * up_part * sigmoid_gate * (1.0 + gate_part * (1.0 - sigmoid_gate))
-        )
-        grad_up_part = grad_active * silu_gate
-        grad_both = jnp.concatenate([grad_gate_part, grad_up_part], axis=-1).astype(jnp.bfloat16)
-        gate_up_total = gate_up_total + jnp.einsum(
-            "oecd,oecf->edf", arrived, grad_both, preferred_element_type=jnp.float32
-        )
-        grad_rows = jnp.einsum(
-            "oecf,edf->oecd", grad_both, w_gate_up, preferred_element_type=jnp.float32
-        ).astype(jnp.bfloat16)
-        grad_back = lax.all_to_all(grad_rows, "expert", split_axis=0, concat_axis=0, tiled=True)
-        grad_picked = grad_back.reshape(experts_all * capacity, width)[targets].astype(jnp.float32)
-        grad_ffn_in = grad_ffn_in + jnp.sum(grad_picked.reshape(tok_rows, top_count, width), axis=1)
+        grad_ffn_in = grad_ffn_in + moved_dx[micro_index]
         grad_residual_part, ffn_gain_grad = norm_back(grad_ffn_in, residual, inv_ffn, ffn_gain)
         grad_residual = grad_final + grad_residual_part
         grad_branch = grad_residual.astype(jnp.bfloat16)

time: 907 us -> 734 us (0.81)
  Pallas kernels: 0 us -> 209 us
  waiting for transfers between devices: 244 us -> 99.1 us
  local copies, waits for them, and re-layouts: 224 us -> 113 us
  matrix products: 148 us -> 71.7 us
  starting transfers between devices: 43.1 us -> 0.37 us
    pallas_call x0 -> x1, Pallas kernels: none -> 209 us  [moe(): pl.pallas_call(moe_kernel, out_shape=(jax.ShapeDtypeStruct((2, 128, 1024)...]
    all_to_all x8 -> x0, waiting for transfers between devices: 142 us -> none  [the longest x2 59.6 us: body(): lax.all_to_all(grad_outgoing, 'expert', split_axis=0, concat_axis=0, tile...]
    gather x14 -> x0, local copies, waits for them, and re-layouts: 77.5 us -> none  [the longest x2 19.3 us: body(): grad_padded[jnp.minimum(sources, copy_rows)]]
    dot_general x12 -> x0, matrix products: 71.1 us -> none  [the longest x2 18 us: body(): jnp.einsum('oecd,oecf->edf', arrived, grad_both, preferred_element_type=j...]
    all_to_all x8 -> x0, starting transfers between devices: 41.8 us -> none  [the longest x2 11.9 us: body(): lax.all_to_all(outgoing, 'expert', split_axis=0, concat_axis=0, tiled=True)]
    concatenate x1, other arithmetic: 8.02 us -> 23.2 us  [together(): vector, at, done = (jnp.concatenate([a.reshape(-1) for a in arrays]), 0, [])]
    another operation x12 -> x8, other arithmetic: 27.3 us -> 13.5 us
    reduce_sum x12 -> x3, other arithmetic: 11.6 us -> 0.09 us  [the longest x2 0.06 us: body(): gates = weight / jnp.sum(weight, axis=1, keepdims=True)]
  transfers between devices with their start and end apart: 17 -> 9, of which waited for: 13 -> 5; matrix products, arithmetic and copies ran while one was open for 40% -> 28% of each run, Pallas kernels for 0% -> 0%
where the time goes in v1:
time: 734 us; the launch traced here: 725 us
  Pallas kernels  209 us (28%)
  blocking collectives  115 us (16%)
  local copies, waits for them, and re-layouts  113 us (15%)
  other arithmetic  100 us (14%)
  waiting for transfers between devices  99.1 us (14%)
  matrix products  71.7 us (10%)
  between operations  17.1 us (2%)
    pallas_call x1, Pallas kernels, moe(): pl.pallas_call(moe_kernel, out_shape=(jax.ShapeDtypeStruct((2, 128, 1024)...  209 us
    psum x1, blocking collectives, body(): lax.psum(shard_part[2].astype(jnp.bfloat16), 'expert').astype(jnp.float32)  74.6 us
    reduce_scatter x2, waiting for transfers between devices, in_one_piece_2(): filled = lax.psum_scatter(both, axis, scatter_dimension=dim, tiled=True)  48.2 us
    unnamed x2, blocking collectives  28.8 us
    all_gather x1, waiting for transfers between devices, in_one_piece(): filled, at, done = (lax.all_gather(both, axis, axis=dim, tiled=True), 0, [])  23.9 us
    concatenate x1, other arithmetic, together(): vector, at, done = (jnp.concatenate([a.reshape(-1) for a in arrays]), 0, [])  23.2 us
    reduce_scatter x1, waiting for transfers between devices, in_one_piece_3(): lax.psum_scatter(both, axis, scatter_dimension=dim, tiled=True)  19.7 us
    unnamed x225, local copies, waits for them, and re-layouts  16.3 us
  transfers between devices with their start and end apart: 9, of which 5 were waited for; matrix products, arithmetic and copies ran while one was open for 28% of the time, Pallas kernels for 0%

profile of v1, /device:TPU:0, one launch (start us, length us, event | category | flops | bytes accessed | tf_op | source)
XLA Modules:
  0.0 725.5 jit_solution(13233286166195956910)
XLA Ops:
  14.6 15.0 %all-reduce.8 = (bf16[64]{0:T(256)(128)(2,1)S(1)}, bf16[64]{0:T(256)(128)(2,1)S(1)}) all-reduce(bf16[64]{0:T(256)(128)(2,1)S(1)} %dynamic-update-slice, bf16[64]{0:T(256)(128)(2,1)S(1)} %dynamic-update-slice.1), channel_id=1, replica_groups=mesh['dp'=8,'expert'=16] {'dp'}, use_global_device_ids=true, to_apply=%add.1 | all-reduce | flops 128 | bytes 512
  31.7 23.9 %all-gather.4.cloned.1.call-done = bf16[1024,3074]{1,0:T(8,128)(2,1)} async-done(((bf16[128,3074]{1,0:T(8,128)(2,1)}), bf16[1024,3074]{1,0:T(8,128)(2,1)}) %all-gather.4.cloned.1.call-update) | async-done | bytes 6295568 | tf_op jit(solution)/shard_map/all_gather | solution.py:20
  68.4 11.2 %all_gather.23 = bf16[1024,32]{0,1:T(8,128)(2,1)S(1)} all-gather(bf16[128,32]{0,1:T(8,128)(2,1)S(1)} %copy-done.91), channel_id=1, replica_groups=mesh['dp'=8,'expert'=16] {'dp'}, dimensions={0}, use_global_device_ids=true | all-gather | bytes 73728 | tf_op jit(solution)/shard_map/all_gather | solution.py:616
  112.4 7.1 all-gather.6.cloned.1.call-done
  136.9 209.2 %shard_map.212 = (f32[2,128,1024]{2,1,0:T(8,128)}, f32[2,128,1024]{2,1,0:T(8,128)}, f32[16,8,128]{2,1,0:T(8,128)}, f32[2,1024,1024]{2,1,0:T(8,128)}, f32[2,512,1024]{2,1,0:T(8,128)}) custom-call(bf16[2,128,1024]{2,1,0:T(8,128)(2,1)} %pad_maximum_fusion.3.ffn_ref, bf16[2,128,1024]{2,1,0:T(8,128)(2,1)} %bitcast.368, f32[16,8,128]{2,1,0:T(8,128)} %pad.4.gates_ref, ...), custom_call_target="tpu_custom_call" | custom-call | flops 30000001024 | bytes 30000000 | tf_op jit(solution)/shard_map/pallas_call | solution.py:525
  354.3 4.1 convert_element_type.448
  361.5 23.2 %pad_maximum_fusion = bf16[3145728]{0:T(1024)(128)(2,1)} fusion(bf16[1048576]{0:T(1024)(128)(2,1)S(1)} %bitcast.315, bf16[2097152]{0:T(1024)(128)(2,1)S(1)} %bitcast.304), kind=kLoop, calls=%fused_computation.23 | loop fusion | flops 12582912 | bytes 12582912 | tf_op jit(solution)/shard_map/concatenate | solution.py:56
  390.7 5.9 fusion.3
  396.7 4.9 fusion.16
  406.3 5.9 bitcast_convert_fusion.1
  420.5 5.5 fusion
  426.1 4.4 fusion.17
  435.2 6.0 bitcast_convert_fusion
  481.4 5.4 slice_convert_fusion
  486.8 16.2 %reduce-scatter.7.cloned.1.call-done = bf16[2,128,512]{2,1,0:T(8,128)(2,1)} async-done(((bf16[2,1024,512]{2,1,0:T(8,128)(2,1)}), bf16[2,128,512]{2,1,0:T(8,128)(2,1)}) %reduce-scatter.7.cloned.1.call-update) | async-done | bytes 262160 | tf_op jit(solution)/shard_map/reduce_scatter | solution.py:40
  506.5 32.0 %reduce-scatter.9.cloned.1.call-done = bf16[2,128,512]{2,1,0:T(8,128)(2,1)} async-done(((bf16[2,1024,512]{2,1,0:T(8,128)(2,1)}), bf16[2,128,512]{2,1,0:T(8,128)(2,1)}) %reduce-scatter.9.cloned.1.call-update) | async-done | bytes 262160 | tf_op jit(solution)/shard_map/reduce_scatter | solution.py:40
  559.7 3.4 add_convert_fusion
  563.1 9.5 %concatenate.182 = bf16[1024,3074]{1,0:T(8,128)(2,1)} concatenate(bf16[1024,2048]{1,0:T(8,128)(2,1)} %add_convert_fusion, bf16[1024,1024]{1,0:T(8,128)(2,1)S(1)} %add_convert_fusion.1, bf16[1024,1]{1,0:T(8,128)(2,1)} %convert_element_type.462, bf16[1024,1]{1,0:T(8,128)(2,1)S(1)} %copy-done.52), dimensions={1} | concatenate | bytes 12591104 | tf_op jit(solution)/shard_map/concatenate | solution.py:46
  572.7 3.8 slice_convert_fusion.1
  576.5 9.3 %reshape.1327 = f32[2,1024,1024]{2,1,0:T(8,128)} reshape(f32[2097152]{0:T(1024)} %slice_convert_fusion) | data formatting | bytes 16777216 | tf_op jit(solution)/shard_map/convert_element_type | solution.py:866
  585.8 5.0 reshape.1328
  595.6 19.7 %reduce-scatter.11.cloned.1.call-done = bf16[128,3074]{1,0:T(8,128)(2,1)} async-done(((bf16[1024,3074]{1,0:T(8,128)(2,1)}), bf16[128,3074]{1,0:T(8,128)(2,1)}) %reduce-scatter.11.cloned.1.call-update) | async-done | bytes 786960 | tf_op jit(solution)/shard_map/reduce_scatter | solution.py:47
  619.6 13.8 %all-reduce.7 = (bf16[64]{0:T(256)(128)(2,1)S(1)}, bf16[64]{0:T(256)(128)(2,1)S(1)}) all-reduce(bf16[64]{0:T(256)(128)(2,1)} %add_convert_fusion.9, bf16[64]{0:T(256)(128)(2,1)S(1)} %add_convert_fusion.8), channel_id=5, replica_groups=mesh['dp'=8,'expert'=16] {'dp'}, use_global_device_ids=true, to_apply=%region_43.44.clone | all-reduce | flops 128 | bytes 512
  637.6 74.6 %all-reduce.5 = (bf16[128]{0:T(256)(128)(2,1)S(1)}, bf16[128]{0:T(256)(128)(2,1)S(1)}, bf16[8]{0:T(256)(128)(2,1)S(1)}, bf16[8]{0:T(256)(128)(2,1)S(1)}, bf16[128,32]{0,1:T(8,128)(2,1)S(1)}) all-reduce(bf16[128]{0:T(256)(128)(2,1)S(1)} %get-tuple-element.32, ...), channel_id=1, replica_groups=mesh['dp'=8,'expert'=16] {'expert'}, use_global_device_ids=true, to_apply=%region_39.40 | all-reduce | flops 4368 | bytes 17472 | tf_op jit(solution)/shard_map/psum | solution.py:858
  (435 shorter events, 189.3 us)
Async XLA Ops:
  7.2 53.7 %copy-start.11 = (bf16[2,1,128,1024]{3,2,1,0:T(8,128)(2,1)S(1)}, bf16[2,1,128,1024]{3,2,1,0:T(8,128)(2,1)}, u32[]{:S(2)}) copy-start(bf16[2,1,128,1024]{3,2,1,0:T(8,128)(2,1)} %param.13) | copy-start | bytes 1572868
  7.2 48.4 %all-gather.4.cloned.1.call-start = ((), (), s32[]{:S(2)}) async-start(), calls=%async_computation.4 | async-start | bytes 7372800 | tf_op jit(solution)/shard_map/all_gather | solution.py:20
  10.8 86.7 %all-gather.8.cloned.1.call-start = ((), (), s32[]{:S(2)}) async-start(), calls=%async_computation.6 | async-start | bytes 2359296 | tf_op jit(solution)/shard_map/all_gather | solution.py:30
  29.6 35.6 %copy-start.102 = (f32[64]{0:T(128)}, f32[64]{0:T(128)S(1)}, u32[]{:S(2)}) copy-start(f32[64]{0:T(128)S(1)} %convert_element_type.378) | copy-start | bytes 772
  30.9 29.9 %copy-start.100 = (f32[128]{0:T(128)}, f32[128]{0:T(128)S(1)}, u32[]{:S(2)}) copy-start(f32[128]{0:T(128)S(1)} %get-tuple-element.139) | copy-start | bytes 1540
  30.9 33.1 %copy-start.94 = (f32[128]{0:T(128)}, f32[128]{0:T(128)S(1)}, u32[]{:S(2)}) copy-start(f32[128]{0:T(128)S(1)} %get-tuple-element.140) | copy-start | bytes 1540
  31.7 33.7 %copy-start.61 = (f32[128,32]{0,1:T(8,128)}, f32[128,32]{0,1:T(8,128)S(1)}, u32[]{:S(2)}) copy-start(f32[128,32]{0,1:T(8,128)S(1)} %get-tuple-element.114) | copy-start | bytes 49156
  31.7 33.7 %copy-start.72 = (f32[128,32]{0,1:T(8,128)}, f32[128,32]{0,1:T(8,128)S(1)}, u32[]{:S(2)}) copy-start(f32[128,32]{0,1:T(8,128)S(1)} %get-tuple-element.113) | copy-start | bytes 49156
  66.4 53.1 %all-gather.6.cloned.1.call-start = ((), (), s32[]{:S(2)}) async-start(), calls=%async_computation.5 | async-start | bytes 2359296 | tf_op jit(solution)/shard_map/all_gather | solution.py:30
  66.4 30.6 %copy-start.103 = (f32[64]{0:T(128)}, f32[64]{0:T(128)S(1)}, u32[]{:S(2)}) copy-start(f32[64]{0:T(128)S(1)} %convert_element_type.381) | copy-start | bytes 772
  92.3 387.7 %reduce-scatter.13.cloned.1.call-start = ((), (), s32[]{:S(2)}) async-start(), calls=%async_computation.11 | async-start | bytes 294912
  97.5 29.2 %copy-start.42 = (bf16[1,128,16,32]{1,3,2,0:T(8,128)(2,1)}, bf16[1,128,16,32]{1,3,2,0:T(8,128)(2,1)S(1)}, u32[]{:S(2)}) copy-start(bf16[1,128,16,32]{1,3,2,0:T(8,128)(2,1)S(1)} %get-tuple-element.64) | copy-start | bytes 393220
  97.5 29.2 %copy-start.44 = (bf16[1,128,16,32]{1,3,2,0:T(8,128)(2,1)}, bf16[1,128,16,32]{1,3,2,0:T(8,128)(2,1)S(1)}, u32[]{:S(2)}) copy-start(bf16[1,128,16,32]{1,3,2,0:T(8,128)(2,1)S(1)} %get-tuple-element.65) | copy-start | bytes 393220
  349.9 131.5 %all-reduce.12.cloned.1.call-start = ((), (), s32[]{:S(2)}) async-start(), calls=%async_computation.10 | async-start | bytes 12582912 | tf_op jit(solution)/shard_map/psum | solution.py:57
  361.5 23.3 %copy-start.19 = (f32[128,1024]{1,0:T(8,128)S(1)}, f32[128,1024]{1,0:T(8,128)}, u32[]{:S(2)}) copy-start(f32[128,1024]{1,0:T(8,128)} %copy-done.18) | copy-start | bytes 1572868
  384.8 118.2 %reduce-scatter.7.cloned.1.call-start = ((), (), s32[]{:S(2)}) async-start(), calls=%async_computation.7 | async-start | bytes 2359296 | tf_op jit(solution)/shard_map/reduce_scatter | solution.py:40
  387.7 27.0 %copy-start.16 = (f32[128,1024]{1,0:T(8,128)}, f32[128,1024]{1,0:T(8,128)S(1)}, u32[]{:S(2)}) copy-start(f32[128,1024]{1,0:T(8,128)S(1)} %get-tuple-element.71) | copy-start | bytes 1572868
  420.5 118.1 %reduce-scatter.9.cloned.1.call-start = ((), (), s32[]{:S(2)}) async-start(), calls=%async_computation.8 | async-start | bytes 2359296 | tf_op jit(solution)/shard_map/reduce_scatter | solution.py:40
  471.1 144.2 %reduce-scatter.11.cloned.1.call-start = ((), (), s32[]{:S(2)}) async-start(), calls=%async_computation.9 | async-start | bytes 7372800 | tf_op jit(solution)/shard_map/reduce_scatter | solution.py:47
  481.4 61.9 %copy-start.27 = (f32[128,512]{0,1:T(8,128)S(1)}, f32[128,512]{0,1:T(8,128)}, u32[]{:S(2)}) copy-start(f32[128,512]{0,1:T(8,128)} %copy-done.26) | copy-start | bytes 786436
  486.8 64.9 %copy-start.12 = (bf16[2,1,128,1024]{3,2,1,0:T(8,128)(2,1)S(1)}, bf16[2,1,128,1024]{3,2,1,0:T(8,128)(2,1)}, u32[]{:S(2)}) copy-start(bf16[2,1,128,1024]{3,2,1,0:T(8,128)(2,1)} %param.13) | copy-start | bytes 1572868
  572.6 142.2 %all-reduce.14.cloned.1.call-start = ((), (), s32[]{:S(2)}) async-start(), calls=%async_computation.12 | async-start | bytes 1572864 | tf_op jit(solution)/shard_map/psum | solution.py:856
  585.8 48.4 %copy-start.15 = (f32[128,1024]{1,0:T(8,128)S(1)}, f32[128,1024]{1,0:T(8,128)}, u32[]{:S(2)}) copy-start(f32[128,1024]{1,0:T(8,128)} %copy-done.13) | copy-start | bytes 1572868
  590.8 46.8 %copy-start.84 = (bf16[128,32]{0,1:T(8,128)(2,1)S(1)}, bf16[128,32]{0,1:T(8,128)(2,1)}, u32[]{:S(2)}) copy-start(bf16[128,32]{0,1:T(8,128)(2,1)} %copy.361) | copy-start | bytes 24580
  (92 other events, 681.0 us)
Sparse Core Ops, SparseCore 0:
  11.0 44.5 all-gather.3
  66.5 25.1 all-gather.7
  94.0 25.4 all-gather.5
  350.0 28.6 reduce-scatter.12
  384.9 82.3 all-reduce.11
  469.6 33.3 reduce-scatter.6
  506.1 32.3 reduce-scatter.8
  572.7 42.5 reduce-scatter.10
  619.0 85.9 all-reduce.13

commit v2 on v1

v2 whole, which is shorter than its diff:
```python
import jax
import jax.numpy as jnp
import numpy as np
from jax import lax
from jax.experimental import pallas as pl
from jax.experimental.pallas import tpu as pltpu
from jax.sharding import PartitionSpec as P

HD = 64
EPSILON = 1e-06
THETA = 10000.0
MASKED = -1e30

BF = jnp.bfloat16
F32 = jnp.float32
SLOTS = 48
CHUNK = 256
MIB = 1024 * 1024


def nn(a, b):
    return lax.dot_general(a, b, (((1,), (0,)), ((), ())), preferred_element_type=F32)


def nt(a, b):
    return lax.dot_general(a, b, (((1,), (1,)), ((), ())), preferred_element_type=F32)


def tn(a, b):
    return lax.dot_general(a, b, (((0,), (0,)), ((), ())), preferred_element_type=F32)


def send(src, dst, send_sem, recv_sem, device):
    return pltpu.make_async_remote_copy(
        src_ref=src, dst_ref=dst, send_sem=send_sem, recv_sem=recv_sem, device_id=device
    )


def next_to(p):
    return (p + 1) % 4, (p + 3) % 4, (p + 2) % 4


def greet(devices):
    sem = pltpu.get_barrier_semaphore()
    for device in devices:
        pl.semaphore_signal(sem, inc=1, device_id=device)
    pl.semaphore_wait(sem, len(devices))


class Plane:
    def __init__(self):
        self.me = lax.axis_index("expert")
        self.z = self.me // 4
        self.x = self.me % 4

    def own(self, half):
        return (self.x, self.z) if half == 0 else (self.z, self.x)

    def device(self, half, p, q):
        return {"expert": q * 4 + p if half == 0 else p * 4 + q}

    def others(self):
        return [{"expert": (self.me + step) % 16} for step in range(1, 16)]

    def neighbours(self):
        zn, zp, _ = next_to(self.z)
        xn, xp, _ = next_to(self.x)
        return [{"expert": k} for k in (zn * 4 + self.x, zp * 4 + self.x, self.z * 4 + xn, self.z * 4 + xp)]


class Column:
    def __init__(self):
        self.me = lax.axis_index("dp")
        self.y = self.me // 2
        self.c = self.me % 2

    def neighbours(self):
        yn, yp, _ = next_to(self.y)
        return [self.to(yn), self.to(yp), self.other()]

    def to(self, y):
        return {"dp": y * 2 + self.c}

    def other(self):
        return {"dp": self.y * 2 + 1 - self.c}


class PlaneStep:
    def at(self, half, p, q, rows):
        return self.ref.at[q, p, rows] if half == 0 else self.ref.at[p, q, rows]

    def line(self, half, q, rows):
        return self.ref.at[q, :, rows] if half == 0 else self.ref.at[:, q, rows]

    def rows(self, half):
        quarter = self.height // 4
        base = 2 * quarter * half
        return pl.ds(base, 2 * quarter), pl.ds(base, quarter), pl.ds(base + quarter, quarter)


class Gather(PlaneStep):
    def __init__(self, plane, ref, sems, height=128):
        self.plane, self.ref, self.sems, self.height = plane, ref, sems, height

    def message(self, half, i):
        p, q = self.plane.own(half)
        pn, pp, _ = next_to(p)
        qn, qp, _ = next_to(q)
        full, first, second = self.rows(half)
        view, to = [
            lambda: (self.at(half, p, q, full), (pn, q)),
            lambda: (self.at(half, p, q, full), (pp, q)),
            lambda: (self.at(half, pp, q, first), (pn, q)),
            lambda: (self.at(half, pn, q, second), (pp, q)),
            lambda: (self.line(half, q, full), (p, qn)),
            lambda: (self.line(half, q, full), (p, qp)),
            lambda: (self.line(half, qp, first), (p, qn)),
            lambda: (self.line(half, qn, second), (p, qp)),
        ][i]()
        sems = self.sems
        return send(view, view, sems.at[0, half, i], sems.at[1, half, i], self.plane.device(half, *to))

    def step(self, n):
        waits, starts = [
            ((), (0, 1)),
            ((0, 1), (2, 3)),
            ((2, 3), (4, 5)),
            ((4, 5), (6, 7)),
            ((6, 7), ()),
        ][n]
        for half in range(2):
            for i in waits:
                self.message(half, i).wait_recv()
            for i in starts:
                self.message(half, i).start()
        if n == 4:
            for half in range(2):
                for i in range(8):
                    self.message(half, i).wait_send()


class Scatter(PlaneStep):
    def __init__(self, plane, ref, slots, sems, store, free=None, height=128):
        self.plane, self.ref, self.slots, self.sems = plane, ref, slots, sems
        self.store, self.free, self.height = store, free, height

    def message(self, half, i):
        p, q = self.plane.own(half)
        pn, pp, po = next_to(p)
        qn, qp, qo = next_to(q)
        full, first, second = self.rows(half)
        r1, r2, r3, r4 = self.slots
        view, slot, to = [
            lambda: (self.line(half, qo, first), r1.at[half, 0], (p, qn)),
            lambda: (self.line(half, qo, second), r1.at[half, 1], (p, qp)),
            lambda: (self.line(half, qn, full), r2.at[half, 0], (p, qn)),
            lambda: (self.line(half, qp, full), r2.at[half, 1], (p, qp)),
            lambda: (self.at(half, po, q, first), r3.at[half, 0], (pn, q)),
            lambda: (self.at(half, po, q, second), r3.at[half, 1], (pp, q)),
            lambda: (self.at(half, pn, q, full), r4.at[half, 0], (pn, q)),
            lambda: (self.at(half, pp, q, full), r4.at[half, 1], (pp, q)),
        ][i]()
        sems = self.sems
        return send(view, slot, sems.at[0, half, i], sems.at[1, half, i], self.plane.device(half, *to))

    def add_line(self, half, q, part, parts, slots):
        quarter = self.height // 4
        offset = quarter * (2 * half + part)
        groups = quarter * parts // 16

        @pl.loop(0, 4 * groups)
        def _(n):
            j, k = n // groups, n % groups
            rows = pl.ds(pl.multiple_of(offset + k * 16, 16), 16)
            some = pl.ds(pl.multiple_of(k * 16, 16), 16)
            place = (q, j, rows) if half == 0 else (j, q, rows)
            total = self.ref[place].astype(F32)
            for ref, side in slots:
                total += ref[half, side, j, some].astype(F32)
            self.ref[place] = total.astype(BF)

    def add_at(self, half, p, q, part, slot):
        quarter = self.height // 4
        ref, side = slot

        @pl.loop(0, quarter // 16)
        def _(k):
            rows = pl.ds(pl.multiple_of(quarter * (2 * half + part) + k * 16, 16), 16)
            place = (q, p, rows) if half == 0 else (p, q, rows)
            got = ref[half, side, pl.ds(pl.multiple_of(k * 16, 16), 16)].astype(F32)
            self.ref[place] = (self.ref[place].astype(F32) + got).astype(BF)

    def step(self, n):
        r1, r2, r3, r4 = self.slots
        for half in range(2):
            p, q = self.plane.own(half)
            pn, pp, po = next_to(p)
            qn, qp, qo = next_to(q)
            if n == 0:
                self.message(half, 0).start()
                self.message(half, 1).start()
            elif n == 1:
                self.message(half, 0).wait_recv()
                self.add_line(half, qn, 0, 1, [(r1, 0)])
                self.message(half, 2).start()
                self.message(half, 1).wait_recv()
                self.add_line(half, qp, 1, 1, [(r1, 1)])
                self.message(half, 3).start()
            elif n == 2:
                self.message(half, 2).wait_recv()
                self.message(half, 3).wait_recv()
                self.add_line(half, q, 0, 2, [(r2, 0), (r2, 1)])
                self.message(half, 4).start()
                self.message(half, 5).start()
            elif n == 3:
                self.message(half, 4).wait_recv()
                self.add_at(half, pn, q, 0, (r3, 0))
                self.message(half, 6).start()
                self.message(half, 5).wait_recv()
                self.add_at(half, pp, q, 1, (r3, 1))
                self.message(half, 7).start()
            elif n == 4:
                self.message(half, 6).wait_recv()
                self.message(half, 7).wait_recv()

                @pl.loop(0, self.height // 32)
                def _(k):
                    rows = pl.ds(pl.multiple_of(self.height // 2 * half + k * 16, 16), 16)
                    place = (q, p, rows) if half == 0 else (p, q, rows)
                    some = pl.ds(pl.multiple_of(k * 16, 16), 16)
                    total = self.ref[place].astype(F32)
                    total += r4[half, 0, some].astype(F32)
                    total += r4[half, 1, some].astype(F32)
                    self.store(place, rows, total)
        if n == 4:
            for half in range(2):
                for i in range(8):
                    self.message(half, i).wait_send()

    def give_credit(self):
        for device in self.plane.neighbours():
            pl.semaphore_signal(self.free, inc=1, device_id=device)

    def take_credit(self):
        pl.semaphore_wait(self.free, 4)


def scatter_slots(height, width, lead=()):
    quarter = height // 4
    return [
        pltpu.VMEM((*lead, 2, 2, 4, quarter, width), BF),
        pltpu.VMEM((*lead, 2, 2, 4, 2 * quarter, width), BF),
        pltpu.VMEM((*lead, 2, 2, quarter, width), BF),
        pltpu.VMEM((*lead, 2, 2, 2 * quarter, width), BF),
    ]


class ColumnGather:
    def __init__(self, column, ref, sems, count):
        self.column, self.ref, self.sems, self.count = column, ref, sems, count

    def message(self, i):
        y, c = self.column.y, self.column.c
        yn, yp, yo = next_to(y)
        half = self.count // 2
        ref, column = self.ref, self.column
        view, device = [
            lambda: (ref.at[y, c], column.to(yn)),
            lambda: (ref.at[y, c], column.to(yp)),
            lambda: (ref.at[y, c], column.other()),
            lambda: (ref.at[yp, c, pl.ds(0, half)], column.to(yn)),
            lambda: (ref.at[yn, c, pl.ds(half, half)], column.to(yp)),
            lambda: (ref.at[yp, c], column.other()),
            lambda: (ref.at[yn, c], column.other()),
            lambda: (ref.at[yo, c], column.other()),
        ][i]()
        return send(view, view, self.sems.at[0, i], self.sems.at[1, i], device)

    def step(self, n):
        order = [
            [("s", 0), ("s", 1), ("s", 2)],
            [("w", 0), ("s", 3), ("s", 5), ("w", 1), ("s", 4), ("s", 6)],
            [("w", 3), ("w", 4), ("s", 7)],
            [("w", 2), ("w", 5), ("w", 6), ("w", 7)],
        ][n]
        for what, i in order:
            if what == "s":
                self.message(i).start()
            else:
                self.message(i).wait_recv()
        if n == 3:
            for i in range(8):
                self.message(i).wait_send()


class ColumnScatter:
    def __init__(self, column, ref, slots, sems, count, store, group=16):
        self.column, self.ref, self.slots, self.sems = column, ref, slots, sems
        self.count, self.store, self.group = count, store, group

    def message(self, i):
        y, c = self.column.y, self.column.c
        yn, yp, yo = next_to(y)
        half = self.count // 2
        ref, column = self.ref, self.column
        ra, rb, rc = self.slots
        view, slot, device = [
            lambda: (ref.at[:, 1 - c], ra, column.other()),
            lambda: (ref.at[yo, c, pl.ds(0, half)], rb.at[0], column.to(yn)),
            lambda: (ref.at[yo, c, pl.ds(half, half)], rb.at[1], column.to(yp)),
            lambda: (ref.at[yn, c], rc.at[0], column.to(yn)),
            lambda: (ref.at[yp, c], rc.at[1], column.to(yp)),
        ][i]()
        return send(view, slot, self.sems.at[0, i], self.sems.at[1, i], device)

    def some(self, k, base=0):
        return pl.ds(pl.multiple_of(base + k * self.group, self.group), self.group)

    def step(self, n):
        y, c = self.column.y, self.column.c
        yn, yp, yo = next_to(y)
        ref, (ra, rb, rc) = self.ref, self.slots
        low = ref.dtype
        half = self.count // 2
        groups = self.count // self.group
        if n == 0:
            self.message(0).start()
        elif n == 1:
            self.message(0).wait_recv()

            @pl.loop(0, 4 * groups)
            def _(k):
                j, r = k // groups, self.some(k % groups)
                ref[j, c, r] = (ref[j, c, r].astype(F32) + ra[j, r].astype(F32)).astype(low)

            self.message(1).start()
            self.message(2).start()
        elif n == 2:
            for side, to in ((0, yn), (1, yp)):
                self.message(1 + side).wait_recv()

                @pl.loop(0, groups // 2)
                def _(k):
                    r = self.some(k, side * half)
                    got = rb[side, self.some(k)].astype(F32)
                    ref[to, c, r] = (ref[to, c, r].astype(F32) + got).astype(low)

                self.message(3 + side).start()
        else:
            self.message(3).wait_recv()
            self.message(4).wait_recv()

            @pl.loop(0, groups)
            def _(k):
                r = self.some(k)
                total = ref[y, c, r].astype(F32) + rc[0, r].astype(F32) + rc[1, r].astype(F32)
                self.store(r, total)

            for i in range(5):
                self.message(i).wait_send()


def column_slots(shape, dtype=BF, lead=()):
    count, rest = shape[0], shape[1:]
    return [
        pltpu.VMEM((*lead, 4, count, *rest), dtype),
        pltpu.VMEM((*lead, 2, count // 2, *rest), dtype),
        pltpu.VMEM((*lead, 2, count, *rest), dtype),
    ]


def turned(v, cosine, sine):
    a, b = v[:32], v[32:]
    return jnp.concatenate([a * cosine - b * sine, b * cosine + a * sine], axis=0)


def inverse_rms(v, axis):
    return lax.rsqrt(jnp.mean(v * v, axis=axis, keepdims=True) + EPSILON)


def head_gain(small_t, row):
    pieces = [small_t[:, 128 * b : 128 * (b + 1)] for b in range(8)]
    tall = jnp.concatenate([piece.T[:8] for piece in pieces], axis=0)
    return jnp.broadcast_to(tall[:, row : row + 1], (64, 128))


def document_bias(seg_ref, bias, mb, mine):
    own = seg_ref[mb, mine]
    for b in range(8):
        keys = jnp.broadcast_to(seg_ref[mb, b], (128, 128)).T
        bias[mb, 128 * b : 128 * (b + 1)] = jnp.where(keys == own, 0.0, MASKED)


def pair_columns(ref, mb, g):
    both = ref[mb, pl.ds(pl.multiple_of(g * 128, 128), 128)]
    return jnp.concatenate([both[:64], both[64:]], axis=1)


def front_kernel(
    tok, cot, wq, wo, small, seg_ref, routes_ref, turn_hbm,
    dy_all, wq_all, wo_all, small_t, raw_t, q_t, kv_all, mix_t, lsum, res, ffn, gates_t, sent,
    small_all, normed, bias, turn, plane_sems, column_sems, local,
):
    plane, column = Plane(), Column()
    y, c = column.y, column.c
    copies = [
        pltpu.make_async_copy(wq, wq_all.at[y, c], local.at[0]),
        pltpu.make_async_copy(wo, wo_all.at[y, c], local.at[1]),
        pltpu.make_async_copy(small, small_all.at[y, c], local.at[2]),
        pltpu.make_async_copy(turn_hbm.at[column.me], turn, local.at[3]),
        pltpu.make_async_copy(cot.at[0], dy_all.at[0, plane.z, plane.x], local.at[4]),
        pltpu.make_async_copy(cot.at[1], dy_all.at[1, plane.z, plane.x], local.at[5]),
    ]
    for copy in copies:
        copy.start()
    greet(plane.neighbours() + column.neighbours())
    for copy in copies:
        copy.wait()
    gdy = [Gather(plane, dy_all.at[mb], plane_sems.at[mb]) for mb in range(2)]
    w_small = ColumnGather(column, small_all, column_sems.at[0], 128)
    w_q = ColumnGather(column, wq_all, column_sems.at[1], 128)
    w_o = ColumnGather(column, wo_all, column_sems.at[2], 128)
    kv = [ColumnGather(column, kv_all.at[mb], column_sems.at[3 + mb], 8) for mb in range(2)]
    w_small.step(0)
    w_q.step(0)
    gdy[0].step(0)
    w_small.step(1)
    w_small.step(2)
    w_small.step(3)
    for b in range(8):
        small_t[:, 128 * b : 128 * (b + 1)] = small_all[b // 2, b % 2].astype(F32).T
    for mb in range(2):
        document_bias(seg_ref, bias, mb, column.me)
    attn_gain = small_t[32:33]
    for mb in range(2):
        v = tok[mb].astype(F32)
        normed[128 * mb : 128 * (mb + 1)] = (v * inverse_rms(v, 1) * attn_gain).astype(BF)
    gdy[0].step(1)
    w_q.step(1)
    w_o.step(0)
    w_q.step(2)
    gdy[0].step(2)
    w_q.step(3)

    @pl.loop(0, 4)
    def _(n):
        cols = pl.ds(pl.multiple_of(n * 512, 512), 512)
        got = nn(normed[...], wq_all[:, :, :, cols].reshape(1024, 512))
        for mb in range(2):
            raw_t[mb, cols] = got[128 * mb : 128 * (mb + 1)].T

    query_gain = head_gain(small_t[...], 34)
    key_gain = head_gain(small_t[...], 35)
    cosine, sine = turn[:32], turn[32:]

    def heads(mb):
        @pl.loop(0, 8)
        def _(g):
            v = raw_t[mb, pl.ds(pl.multiple_of(1024 + g * 64, 64), 64)]
            key = turned(v * inverse_rms(v, 0) * key_gain, cosine, sine)
            value = raw_t[mb, pl.ds(pl.multiple_of(1536 + g * 64, 64), 64)]
            kv_all[mb, y, c, g] = jnp.concatenate([key, value], axis=0).T.astype(BF)

        kv[mb].step(0)

        @pl.loop(0, 16)
        def _(h):
            rows = pl.ds(pl.multiple_of(h * 64, 64), 64)
            v = raw_t[mb, rows]
            query = turned(v * inverse_rms(v, 0) * query_gain, cosine, sine)
            q_t[mb, rows] = (query.astype(BF).astype(F32) * HD ** (-0.5)).astype(BF)

    def attend(mb, start, stop):
        @pl.loop(start, stop)
        def _(g):
            query = pair_columns(q_t, mb, g)
            query = jnp.concatenate([query, jnp.zeros_like(query)], axis=0)
            total = jnp.zeros((1, 256), F32)
            mixed = jnp.zeros((128, 256), F32)
            for j in range(4):
                keys = kv_all[mb, j, :, g].reshape(256, 128)
                there = bias[mb, 256 * j : 256 * (j + 1)]
                p = jnp.exp(nn(keys, query) + jnp.concatenate([there, there], axis=1))
                total += jnp.sum(p, axis=0, keepdims=True)
                mixed += tn(keys, p.astype(BF))
            lsum[mb, g] = total
            mixed = (mixed[64:] / total).astype(BF)
            both = jnp.concatenate([mixed[:, :128], mixed[:, 128:]], axis=0)
            mix_t[mb, pl.ds(pl.multiple_of(g * 128, 128), 128)] = both

    def finish(mb):
        @pl.loop(0, 2)
        def _(n):
            cols = pl.ds(pl.multiple_of(n * 512, 512), 512)
            got = tn(mix_t[mb], wo_all[:, :, :, cols].reshape(1024, 512))
            res[mb, :, cols] = tok[mb, :, cols].astype(F32) + got

        v = res[mb]
        low = (v * inverse_rms(v, 1) * small_t[33:34]).astype(BF)
        ffn[mb] = low
        logits = nt(small_t[:32].astype(BF), low)
        ids = lax.broadcasted_iota(jnp.int32, (32, 128), 0)
        routed = ids == routes_ref[mb, 0:1]
        for k in range(1, 8):
            routed = routed | (ids == routes_ref[mb, k : k + 1])
        top = jnp.max(jnp.where(routed, logits, MASKED), axis=0, keepdims=True)
        weight = jnp.where(routed, jnp.exp(logits - top), 0.0)
        gates = weight / jnp.sum(weight, axis=0, keepdims=True)
        gates_t[mb] = gates
        for k in range(16):
            sent[k, 2 * mb : 2 * mb + 2] = gates[2 * k : 2 * k + 2]

    sent[...] = jnp.zeros_like(sent)
    heads(0)
    heads(1)
    gdy[0].step(3)
    kv[0].step(1)
    w_o.step(1)
    kv[0].step(2)
    kv[1].step(1)
    kv[0].step(3)
    gdy[0].step(4)
    gdy[1].step(0)
    attend(0, 0, 4)
    w_o.step(2)
    kv[1].step(2)
    gdy[1].step(1)
    attend(0, 4, 8)
    gdy[1].step(2)
    w_o.step(3)
    finish(0)
    kv[1].step(3)
    attend(1, 0, 4)
    gdy[1].step(3)
    attend(1, 4, 8)
    finish(1)
    gdy[1].step(4)


def front(tok, cot, wq, wo, small, seg, routes_t, turn):
    vmem = pl.BlockSpec(memory_space=pltpu.VMEM)
    anywhere = pl.BlockSpec(memory_space=pl.ANY)
    return pl.pallas_call(
        front_kernel,
        out_shape=(
            jax.ShapeDtypeStruct((2, 4, 4, 128, 1024), BF),
            jax.ShapeDtypeStruct((4, 2, 128, 2048), BF),
            jax.ShapeDtypeStruct((4, 2, 128, 1024), BF),
            jax.ShapeDtypeStruct((128, 1024), F32),
            jax.ShapeDtypeStruct((2, 2048, 128), F32),
            jax.ShapeDtypeStruct((2, 1024, 128), BF),
            jax.ShapeDtypeStruct((2, 4, 2, 8, 128, 128), BF),
            jax.ShapeDtypeStruct((2, 1024, 128), BF),
            jax.ShapeDtypeStruct((2, 8, 1, 256), F32),
            jax.ShapeDtypeStruct((2, 128, 1024), F32),
            jax.ShapeDtypeStruct((2, 128, 1024), BF),
            jax.ShapeDtypeStruct((2, 32, 128), F32),
            jax.ShapeDtypeStruct((16, 8, 128), F32),
        ),
        in_specs=[vmem, anywhere, anywhere, anywhere, anywhere, vmem, vmem, anywhere],
        out_specs=(anywhere,) + (vmem,) * 12,
        scratch_shapes=[
            pltpu.VMEM((4, 2, 128, 128), BF),
            pltpu.VMEM((256, 1024), BF),
            pltpu.VMEM((2, 1024, 128), F32),
            pltpu.VMEM((64, 128), F32),
            pltpu.SemaphoreType.DMA((2, 2, 2, 8)),
            pltpu.SemaphoreType.DMA((5, 2, 8)),
            pltpu.SemaphoreType.DMA((6,)),
        ],
        compiler_params=pltpu.CompilerParams(
            collective_id=0, has_side_effects=True, vmem_limit_bytes=56 * MIB
        ),
        cost_estimate=pl.CostEstimate(
            flops=5_000_000_000, bytes_accessed=30_000_000, transcendentals=5_000_000
        ),
    )(tok, cot, wq, wo, small, seg, routes_t, turn)


def moe_kernel(
    ffn_ref, dy_hbm, gates_ref, wgu_hbm, wd_hbm,
    out_ref, dx_ref, h_ref, dw,
    x_all, dy_all, r1, r2, r3, r4, xs, ds, os, act, a1, a2, ggu, g_all, ranks, hcol, hs,
    wgu, wd, ra, rb, rc, sems, column_sems, gsend, grecv, hsend, hrecv, free, dfree, local,
):
    plane, column = Plane(), Column()
    me, z, x = plane.me, plane.z, plane.x
    w1 = pltpu.make_async_copy(wgu_hbm, wgu, local.at[0])
    w2 = pltpu.make_async_copy(wd_hbm, wd, local.at[1])
    w1.start()
    w2.start()
    own = [pltpu.make_async_copy(ffn_ref.at[mb], x_all.at[mb, z, x], local.at[4 + mb]) for mb in range(2)]
    dys = [pltpu.make_async_copy(dy_hbm.at[mb], dy_all.at[mb], local.at[2 + mb]) for mb in range(2)]
    for copy in own + dys:
        copy.start()
    greet(plane.others() + column.neighbours())
    for copy in own:
        copy.wait()

    def gate_message(step):
        to = (me + step) % 16
        return pltpu.make_async_remote_copy(
            src_ref=gates_ref.at[to], dst_ref=g_all.at[me],
            send_sem=gsend.at[step], recv_sem=grecv.at[step], device_id={"expert": to},
        )

    def h_message(step):
        to = (me + step) % 16
        return pltpu.make_async_remote_copy(
            src_ref=hs.at[to], dst_ref=h_ref.at[me],
            send_sem=hsend.at[step], recv_sem=hrecv.at[step], device_id={"expert": to},
        )

    for step in range(1, 16):
        gate_message(step).start()
    g_all[me] = gates_ref[me]
    gx = [Gather(plane, x_all.at[mb], sems.at[mb]) for mb in range(2)]

    def into(ref, mb):
        def store(place, rows, total):
            ref[mb, rows] = total

        return store

    def slots(k):
        return [r.at[k] for r in (r1, r2, r3, r4)]

    sout = [
        Scatter(plane, x_all.at[mb], slots(0), sems.at[2 + mb], into(out_ref, mb), free.at[0])
        for mb in range(2)
    ]
    sdx = [
        Scatter(plane, dy_all.at[mb], slots(1), sems.at[4 + mb], into(dx_ref, mb), free.at[1])
        for mb in range(2)
    ]

    def own_part(k):
        def store(r, total):
            dw[k, column.y, column.c, r] = total.astype(BF)

        return store

    dsum = [
        ColumnScatter(
            column, dw.at[k], (ra.at[k], rb.at[k], rc.at[k]), column_sems.at[k], 128, own_part(k)
        )
        for k in range(3)
    ]
    dall = [ColumnGather(column, dw.at[k], column_sems.at[3 + k], 128) for k in range(3)]

    def parts_free(k):
        for device in column.neighbours():
            pl.semaphore_signal(dfree.at[k], inc=1, device_id=device)

    def gather_part(k):
        pl.semaphore_wait(dfree.at[k], 3)
        dall[k].step(0)

    for n in range(5):
        gx[0].step(n)
    gx[1].step(0)
    for step in range(1, 16):
        gate_message(step).wait_recv()
    for step in range(1, 16):
        gate_message(step).wait_send()

    earlier = (
        lax.broadcasted_iota(jnp.int32, (128, 128), 0)
        < lax.broadcasted_iota(jnp.int32, (128, 128), 1)
    ).astype(F32).astype(BF)

    @pl.loop(0, 16)
    def _(s):
        named = g_all[s] > 0.0
        before = nn(named.astype(F32).astype(BF), earlier)
        ranks[s] = jnp.where(named, before, -1.0)

    slot_ids = lax.broadcasted_iota(jnp.int32, (SLOTS, 128), 0).astype(F32)

    def places(s, mb):
        r = ranks[s]
        return [(slot_ids == r[2 * mb + e : 2 * mb + e + 1]).astype(F32) for e in range(2)]

    def gated(s, mb, hot):
        g = g_all[s]
        return [hot[e] * g[2 * mb + e : 2 * mb + e + 1] for e in range(2)]

    def span(s):
        return pl.ds(pl.multiple_of(s * SLOTS, 16), SLOTS)

    def select(mb):
        @pl.loop(0, 16)
        def _(s):
            hot = places(s, mb)
            pick = jnp.concatenate(hot, axis=0).astype(BF)
            scaled = jnp.concatenate(gated(s, mb, hot), axis=0).astype(BF)
            rows = nn(pick, x_all[mb, s // 4, s % 4]).astype(BF)
            drows = nn(scaled, dy_all[mb, s // 4, s % 4]).astype(BF)
            for e in range(2):
                xs[e, span(s)] = rows[SLOTS * e : SLOTS * (e + 1)]
                ds[e, span(s)] = drows[SLOTS * e : SLOTS * (e + 1)]

    chunks = 16 * SLOTS // CHUNK

    def forward(e):
        @pl.loop(0, chunks)
        def _(c):
            r = pl.ds(pl.multiple_of(c * CHUNK, CHUNK), CHUNK)
            gu = nn(xs[e, r], wgu[e])
            g, u = gu[:, :512], gu[:, 512:]
            sig = 1.0 / (1.0 + jnp.exp(-g))
            silu = g * sig
            active = (silu * u).astype(BF)
            act[e, r] = active
            a1[e, r] = (u * sig * (1.0 + g * (1.0 - sig))).astype(BF)
            a2[e, r] = silu.astype(BF)
            o = nn(active, wd[e]).astype(BF)
            os[e, r] = o
            hcol[e, r] = jnp.sum(o.astype(F32) * ds[e, r].astype(F32), axis=-1, keepdims=True)

    def combine_out(mb):
        @pl.loop(0, 16)
        def _(s):
            hot = places(s, mb)
            scaled = jnp.concatenate(gated(s, mb, hot), axis=0).astype(BF)
            both = jnp.concatenate([os[0, span(s)], os[1, span(s)]], axis=0)
            x_all[mb, s // 4, s % 4] = tn(scaled, both).astype(BF)
            for e in range(2):
                row = 2 * mb + e
                hs[s, row : row + 1] = jnp.sum(hot[e] * hcol[e, span(s)], axis=0, keepdims=True)

    def add_part(mb, k, n, fresh):
        fresh = fresh.reshape(2, 128, 1024)
        if mb == 1:
            fresh += dw[k, n].astype(F32)
        dw[k, n] = fresh.astype(BF)

    def backward(mb, e):
        @pl.loop(0, chunks)
        def _(c):
            r = pl.ds(pl.multiple_of(c * CHUNK, CHUNK), CHUNK)
            ga = nt(ds[e, r], wd[e])
            grad = jnp.concatenate(
                [ga * a1[e, r].astype(F32), ga * a2[e, r].astype(F32)], axis=1
            ).astype(BF)
            ggu[r] = grad
            os[e, r] = nt(grad, wgu[e]).astype(BF)

        @pl.loop(0, 4)
        def _(m):
            cols = pl.ds(pl.multiple_of(m * 256, 256), 256)
            add_part(mb, e, m, tn(xs[e, :, cols], ggu[...]))

        @pl.loop(0, 2)
        def _(m):
            cols = pl.ds(pl.multiple_of(m * 256, 256), 256)
            add_part(mb, 2, 2 * e + m, tn(act[e, :, cols], ds[e]))

    def combine_dx(mb):
        @pl.loop(0, 16)
        def _(s):
            pick = jnp.concatenate(places(s, mb), axis=0).astype(BF)
            both = jnp.concatenate([os[0, span(s)], os[1, span(s)]], axis=0)
            dy_all[mb, s // 4, s % 4] = tn(pick, both).astype(BF)

    w1.wait()
    w2.wait()
    for copy in dys:
        copy.wait()
    select(0)
    gx[1].step(1)
    forward(0)
    gx[1].step(2)
    forward(1)
    combine_out(0)
    gx[1].step(3)
    sout[0].step(0)
    backward(0, 0)
    gx[1].step(4)
    sout[0].step(1)
    backward(0, 1)
    combine_dx(0)
    sout[0].step(2)
    sdx[0].step(0)
    select(1)
    sout[0].step(3)
    sdx[0].step(1)
    forward(0)
    sout[0].step(4)
    sout[0].give_credit()
    sdx[0].step(2)
    forward(1)
    sdx[0].step(3)
    combine_out(1)
    h_ref[me] = hs[me]
    for step in range(1, 16):
        h_message(step).start()
    sout[1].take_credit()
    sout[1].step(0)
    sdx[0].step(4)
    sdx[0].give_credit()
    backward(1, 0)
    dsum[0].step(0)
    sout[1].step(1)
    backward(1, 1)
    dsum[1].step(0)
    dsum[2].step(0)
    dsum[0].step(1)
    sout[1].step(2)
    combine_dx(1)
    sdx[1].take_credit()
    sdx[1].step(0)
    dsum[1].step(1)
    sout[1].step(3)
    dsum[0].step(2)
    sdx[1].step(1)
    dsum[2].step(1)
    sout[1].step(4)
    dsum[0].step(3)
    parts_free(0)
    dsum[1].step(2)
    gather_part(0)
    sdx[1].step(2)
    dsum[2].step(2)
    dsum[1].step(3)
    parts_free(1)
    dall[0].step(1)
    gather_part(1)
    sdx[1].step(3)
    dsum[2].step(3)
    parts_free(2)
    dall[1].step(1)
    dall[0].step(2)
    gather_part(2)
    sdx[1].step(4)
    dall[2].step(1)
    dall[1].step(2)
    dall[2].step(2)
    for k in range(3):
        dall[k].step(3)
    for step in range(1, 16):
        h_message(step).wait_recv()
    for step in range(1, 16):
        h_message(step).wait_send()


def moe(ffn, dy, gates, w_gate_up, w_down):
    vmem = pl.BlockSpec(memory_space=pltpu.VMEM)
    anywhere = pl.BlockSpec(memory_space=pl.ANY)
    rows = 16 * SLOTS
    return pl.pallas_call(
        moe_kernel,
        out_shape=(
            jax.ShapeDtypeStruct((2, 128, 1024), F32),
            jax.ShapeDtypeStruct((2, 128, 1024), F32),
            jax.ShapeDtypeStruct((16, 8, 128), F32),
            jax.ShapeDtypeStruct((3, 4, 2, 128, 1024), BF),
        ),
        in_specs=[anywhere, anywhere, vmem, anywhere, anywhere],
        out_specs=(vmem,) * 4,
        scratch_shapes=[
            pltpu.VMEM((2, 4, 4, 128, 1024), BF),
            pltpu.VMEM((2, 4, 4, 128, 1024), BF),
            *scatter_slots(128, 1024, lead=(2,)),
            pltpu.VMEM((2, rows, 1024), BF),
            pltpu.VMEM((2, rows, 1024), BF),
            pltpu.VMEM((2, rows, 1024), BF),
            pltpu.VMEM((2, rows, 512), BF),
            pltpu.VMEM((2, rows, 512), BF),
            pltpu.VMEM((2, rows, 512), BF),
            pltpu.VMEM((rows, 1024), BF),
            pltpu.VMEM((16, 8, 128), F32),
            pltpu.VMEM((16, 8, 128), F32),
            pltpu.VMEM((2, rows, 1), F32),
            pltpu.VMEM((16, 8, 128), F32),
            pltpu.VMEM((2, 1024, 1024), BF),
            pltpu.VMEM((2, 512, 1024), BF),
            *column_slots((128, 1024), lead=(3,)),
            pltpu.SemaphoreType.DMA((6, 2, 2, 8)),
            pltpu.SemaphoreType.DMA((6, 2, 8)),
            pltpu.SemaphoreType.DMA((16,)),
            pltpu.SemaphoreType.DMA((16,)),
            pltpu.SemaphoreType.DMA((16,)),
            pltpu.SemaphoreType.DMA((16,)),
            pltpu.SemaphoreType.REGULAR((2,)),
            pltpu.SemaphoreType.REGULAR((3,)),
            pltpu.SemaphoreType.DMA((6,)),
        ],
        compiler_params=pltpu.CompilerParams(
            collective_id=1, has_side_effects=True, vmem_limit_bytes=63 * MIB
        ),
        cost_estimate=pl.CostEstimate(
            flops=30_000_000_000, bytes_accessed=30_000_000, transcendentals=2_000_000
        ),
    )(ffn, dy, gates, w_gate_up, w_down)


def norm_grad(grad, v, inverse, gain, axis):
    scaled = grad * gain
    moment = jnp.mean(scaled * v, axis=axis, keepdims=True)
    return inverse * (scaled - v * (inverse * inverse * moment)), grad * (v * inverse)


def back_kernel(
    tok, cot, seg_ref, turn_hbm, wq_hbm, wo_hbm, small_t, raw_hbm, q_t, kv_hbm, mix_t, lsum,
    res, ffn, gates_t, share_ref, dx,
    in_grad, gq, go, gs,
    wq_all, wo_all, kv_all, raw_t, turn, bias, gres, branch, gm_t, dq_t, own_kv, gp, normed_t, gn,
    part_kv, part_w, part_s, q_sum, k_sum, ra, rb, rc, sa, sb, sc, plane_buf, plane_all, p1, p2, p3, p4, ta, tb, tc,
    logits, routers, router_sum,
    column_sems, plane_sems, local,
):
    plane, column = Plane(), Column()
    y, c = column.y, column.c
    copies = [
        pltpu.make_async_copy(wo_hbm, wo_all, local.at[0]),
        pltpu.make_async_copy(kv_hbm, kv_all, local.at[1]),
        pltpu.make_async_copy(raw_hbm, raw_t, local.at[2]),
        pltpu.make_async_copy(wq_hbm, wq_all, local.at[3]),
        pltpu.make_async_copy(turn_hbm.at[column.me], turn, local.at[4]),
    ]
    for copy in copies:
        copy.start()
    greet(plane.neighbours() + column.neighbours())
    plane_buf[...] = jnp.zeros_like(plane_buf)
    part_s[...] = jnp.zeros_like(part_s)
    q_sum[...] = jnp.zeros_like(q_sum)
    k_sum[...] = jnp.zeros_like(k_sum)
    for mb in range(2):
        document_bias(seg_ref, bias, mb, column.me)

    def place_w(first):
        def store(r, total):
            low = total.astype(BF)
            half = r.start // 64
            some = pl.ds(pl.multiple_of(r.start % 64, 16), 16)
            for k in range(2):
                n = half * 8 + first + k
                plane_buf[n // 4, n % 4, some] = low[:, 512 * k : 512 * (k + 1)]

        return store

    def place_s(r, total):
        plane_buf[1, 2, r, 0:128] = total.astype(BF)

    def place_kv(mb):
        def store(r, total):
            own_kv[mb, r] = total

        return store

    w_sums = [
        ColumnScatter(
            column, part_w.at[k], (ra.at[k], rb.at[k], rc.at[k]), column_sems.at[k], 128,
            place_w(first),
        )
        for k, first in ((0, 4), (1, 0), (2, 2))
    ]
    kv_sums = [
        ColumnScatter(
            column, part_kv.at[mb],
            (sa.at[mb], sb.at[mb], sc.at[mb]),
            column_sems.at[3 + mb], 8, place_kv(mb), group=1,
        )
        for mb in range(2)
    ]

    s_sum = ColumnScatter(column, part_s, (ta, tb, tc), column_sems.at[5], 64, place_s)
    def tokens_of(mb):
        return pl.ds(128 * mb, 128)

    router = small_t[:32].astype(BF)
    ffn_gain, attn_gain = small_t[33:34], small_t[32:33]
    routers[0:32] = router
    routers[32:64] = router
    ffn_gain_grad = jnp.zeros((1, 1024), F32)
    for mb in range(2):
        share = jnp.concatenate([share_ref[k, 2 * mb : 2 * mb + 2] for k in range(16)], axis=0)
        logit = share - gates_t[mb] * jnp.sum(share, axis=0, keepdims=True)
        high = logit.astype(BF)
        logits[0:32, tokens_of(mb)] = high
        logits[32:64, tokens_of(mb)] = (logit - high.astype(F32)).astype(BF)

    @pl.loop(0, 4)
    def _(n):
        cols = pl.ds(pl.multiple_of(n * 256, 256), 256)
        gn[:, cols] = tn(logits[...], routers[:, cols])
        router_sum[:, cols] = nn(logits[...], ffn[:, :, cols].reshape(256, 256))

    for mb in range(2):
        into = dx[mb] + gn[tokens_of(mb)]
        v = res[mb]
        inv = inverse_rms(v, 1)
        grad, gain = norm_grad(into, v, inv, ffn_gain, 1)
        ffn_gain_grad += jnp.sum(gain, axis=0, keepdims=True)
        total = cot[mb].astype(F32) + grad
        gres[mb] = total
        branch[128 * mb : 128 * (mb + 1)] = total.astype(BF)
    copies[0].wait()

    @pl.loop(0, 4)
    def _(n):
        rows = pl.ds(pl.multiple_of(n * 256, 256), 256)
        got = nt(wo_all[n].reshape(256, 1024), branch[...])
        gm_t[0, rows] = got[:, :128].astype(BF)
        gm_t[1, rows] = got[:, 128:].astype(BF)
        mixed = jnp.concatenate([mix_t[0, rows], mix_t[1, rows]], axis=1)
        part_w[0, n] = nn(mixed, branch[...]).astype(BF).reshape(2, 128, 1024)

    w_sums[0].step(0)
    copies[1].wait()

    def attend(mb, start, stop):
        @pl.loop(start, stop)
        def _(g):
            query = pair_columns(q_t, mb, g)
            grad = pair_columns(gm_t, mb, g)
            mixed = pair_columns(mix_t, mb, g)
            blank = jnp.zeros_like(query)
            inner = jnp.sum(grad.astype(F32) * mixed.astype(F32), axis=0, keepdims=True)
            query = jnp.concatenate([query, blank], axis=0)
            grad = jnp.concatenate([blank, grad], axis=0)
            both = jnp.concatenate([query, grad], axis=1)
            scale = 1.0 / lsum[mb, g]
            dq = jnp.zeros((128, 256), F32)
            for j in range(4):
                keys = kv_all[mb, j, :, g].reshape(256, 128)
                there = bias[mb, 256 * j : 256 * (j + 1)]
                got = nn(keys, both)
                p = jnp.exp(got[:, :256] + jnp.concatenate([there, there], axis=1)) * scale
                ds = (p * (got[:, 256:] - inner)).astype(BF)
                dq += tn(keys, ds)
                dkv = nt(jnp.concatenate([ds, p.astype(BF)], axis=1), both)
                part_kv[mb, j, :, g] = dkv.astype(BF).reshape(2, 128, 128)
            dq = dq[:64] * HD ** (-0.5)
            rows = pl.ds(pl.multiple_of(g * 128, 128), 128)
            dq_t[mb, rows] = jnp.concatenate([dq[:, :128], dq[:, 128:]], axis=0)

    attend(0, 0, 4)
    w_sums[0].step(1)
    attend(0, 4, 8)
    kv_sums[0].step(0)
    w_sums[0].step(2)
    attend(1, 0, 4)
    kv_sums[0].step(1)
    w_sums[0].step(3)
    attend(1, 4, 8)
    kv_sums[1].step(0)
    kv_sums[0].step(2)
    copies[2].wait()
    copies[4].wait()
    cosine, sine = turn[:32], turn[32:]
    query_gain = head_gain(small_t[...], 34)
    key_gain = head_gain(small_t[...], 35)

    def head_back(grad, v, gain, total):
        inv = inverse_rms(v, 0)
        grad = turned(grad, cosine, -sine)
        grad_v, gain_part = norm_grad(grad, v, inv, gain, 0)
        total[...] += gain_part
        return grad_v

    @pl.loop(0, 8)
    def _(g):
        for mb in range(2):
            pieces = []
            for r in range(2):
                rows = pl.ds(pl.multiple_of(g * 128 + r * 64, 64), 64)
                pieces.append(head_back(dq_t[mb, rows], raw_t[mb, rows], query_gain, q_sum))
            cols = pl.ds(pl.multiple_of(g * 128, 128), 128)
            gp[tokens_of(mb), cols] = jnp.concatenate(pieces, axis=0).T.astype(BF)

    kv_sums[0].step(3)
    kv_sums[1].step(1)
    for mb in range(2):
        v = tok[mb].astype(F32)
        normed = (v * inverse_rms(v, 1) * attn_gain).astype(BF).astype(F32)
        for k in range(8):
            normed_t[128 * k : 128 * (k + 1), tokens_of(mb)] = (
                normed[:, 128 * k : 128 * (k + 1)].T.astype(BF)
            )

    def weight_part(which):
        cols = pl.ds(1024 * (which - 1), 1024)

        @pl.loop(0, 4)
        def _(n):
            rows = pl.ds(pl.multiple_of(n * 256, 256), 256)
            part_w[which, n] = nn(normed_t[rows], gp[:, cols]).astype(BF).reshape(2, 128, 1024)

    def keys_back(mb):
        @pl.loop(0, 4)
        def _(k):
            keys, values = [], []
            for r in range(2):
                g = 2 * k + r
                grad = own_kv[mb, g].T
                rows = pl.ds(pl.multiple_of(1024 + g * 64, 64), 64)
                keys.append(head_back(grad[:64], raw_t[mb, rows], key_gain, k_sum))
                values.append(grad[64:])
            cols = pl.ds(pl.multiple_of(1024 + k * 128, 128), 128)
            gp[tokens_of(mb), cols] = jnp.concatenate(keys, axis=0).T.astype(BF)
            cols = pl.ds(pl.multiple_of(1536 + k * 128, 128), 128)
            gp[tokens_of(mb), cols] = jnp.concatenate(values, axis=0).T.astype(BF)

    weight_part(1)
    w_sums[1].step(0)
    kv_sums[1].step(2)
    keys_back(0)
    w_sums[1].step(1)
    kv_sums[1].step(3)
    keys_back(1)
    weight_part(2)
    w_sums[2].step(0)
    w_sums[1].step(2)
    copies[3].wait()

    @pl.loop(0, 4)
    def _(n):
        cols = pl.ds(pl.multiple_of(n * 256, 256), 256)
        gn[:, cols] = nt(gp[...], wq_all[n].reshape(256, 2048))

    w_sums[2].step(1)
    attn_gain_grad = jnp.zeros((1, 1024), F32)
    for mb in range(2):
        v = tok[mb].astype(F32)
        grad, gain = norm_grad(gn[tokens_of(mb)], v, inverse_rms(v, 1), attn_gain, 1)
        attn_gain_grad += jnp.sum(gain, axis=0, keepdims=True)
        in_grad[mb] = (gres[mb] + grad).astype(BF)
    for b in range(8):
        cols = slice(128 * b, 128 * (b + 1))
        heads = slice(8 * b, 8 * (b + 1))
        part_s[b // 2, b % 2, 0:32] = router_sum[0:32, cols] + router_sum[32:64, cols]
        part_s[b // 2, b % 2, 32:33] = attn_gain_grad[:, cols]
        part_s[b // 2, b % 2, 33:34] = ffn_gain_grad[:, cols]
        part_s[b // 2, b % 2, 40:48] = jnp.broadcast_to(
            jnp.sum(q_sum[heads], axis=1, keepdims=True), (8, 128)
        )
        part_s[b // 2, b % 2, 48:56] = jnp.broadcast_to(
            jnp.sum(k_sum[heads], axis=1, keepdims=True), (8, 128)
        )
    s_sum.step(0)
    s_sum.step(1)
    w_sums[1].step(3)
    w_sums[2].step(2)
    s_sum.step(2)
    w_sums[2].step(3)
    s_sum.step(3)

    def keep(place, rows, total):
        plane_all[place] = total.astype(BF)

    over = Scatter(plane, plane_buf, (p1, p2, p3, p4), plane_sems.at[0], keep, height=64)
    back = Gather(plane, plane_all, plane_sems.at[1], height=64)
    for n in range(5):
        over.step(n)
    for n in range(5):
        back.step(n)
    for half in range(2):
        rows = pl.ds(64 * half, 64)
        for k in range(4):
            n = half * 8 + k
            gq[rows, 512 * k : 512 * (k + 1)] = plane_all[n // 4, n % 4].astype(F32)
        for k in range(2):
            n = half * 8 + 4 + k
            go[rows, 512 * k : 512 * (k + 1)] = plane_all[n // 4, n % 4].astype(F32)
    gs[...] = plane_all[1, 2, :, 0:128].astype(F32)


def back(tok, cot, seg, turn, wq_all, wo_all, small_t, raw_t, q_t, kv_all, mix_t, lsum, res, ffn, gates_t, share, dx):
    vmem = pl.BlockSpec(memory_space=pltpu.VMEM)
    anywhere = pl.BlockSpec(memory_space=pl.ANY)
    kv_slots = column_slots((8, 128, 128), lead=(2,))
    return pl.pallas_call(
        back_kernel,
        out_shape=(
            jax.ShapeDtypeStruct((2, 128, 1024), BF),
            jax.ShapeDtypeStruct((128, 2048), F32),
            jax.ShapeDtypeStruct((128, 1024), F32),
            jax.ShapeDtypeStruct((64, 128), F32),
        ),
        in_specs=[
            vmem, vmem, vmem, anywhere, anywhere, anywhere, vmem, anywhere, vmem, anywhere,
            vmem, vmem, vmem, vmem, vmem, vmem, vmem,
        ],
        out_specs=(vmem,) * 4,
        scratch_shapes=[
            pltpu.VMEM((4, 2, 128, 2048), BF),
            pltpu.VMEM((4, 2, 128, 1024), BF),
            pltpu.VMEM((2, 4, 2, 8, 128, 128), BF),
            pltpu.VMEM((2, 2048, 128), F32),
            pltpu.VMEM((64, 128), F32),
            pltpu.VMEM((2, 1024, 128), F32),
            pltpu.VMEM((2, 128, 1024), F32),
            pltpu.VMEM((256, 1024), BF),
            pltpu.VMEM((2, 1024, 128), BF),
            pltpu.VMEM((2, 1024, 128), F32),
            pltpu.VMEM((2, 8, 128, 128), F32),
            pltpu.VMEM((256, 2048), BF),
            pltpu.VMEM((1024, 256), BF),
            pltpu.VMEM((256, 1024), F32),
            pltpu.VMEM((2, 4, 2, 8, 128, 128), BF),
            pltpu.VMEM((3, 4, 2, 128, 1024), BF),
            pltpu.VMEM((4, 2, 64, 128), F32),
            pltpu.VMEM((64, 128), F32),
            pltpu.VMEM((64, 128), F32),
            *column_slots((128, 1024), lead=(3,)),
            *kv_slots,
            pltpu.VMEM((4, 4, 64, 512), BF),
            pltpu.VMEM((4, 4, 64, 512), BF),
            *scatter_slots(64, 512),
            *column_slots((64, 128), F32),
            pltpu.VMEM((64, 256), BF),
            pltpu.VMEM((64, 1024), BF),
            pltpu.VMEM((64, 1024), F32),
            pltpu.SemaphoreType.DMA((6, 2, 8)),
            pltpu.SemaphoreType.DMA((2, 2, 2, 8)),
            pltpu.SemaphoreType.DMA((5,)),
        ],
        compiler_params=pltpu.CompilerParams(
            collective_id=2, has_side_effects=True, vmem_limit_bytes=60 * MIB
        ),
        cost_estimate=pl.CostEstimate(
            flops=12_000_000_000, bytes_accessed=30_000_000, transcendentals=5_000_000
        ),
    )(tok, cot, seg, turn, wq_all, wo_all, small_t, raw_t, q_t, kv_all, mix_t, lsum, res, ffn, gates_t, share, dx)


def turn_table(length):
    frequency = np.power(np.float32(THETA), -2.0 * np.arange(HD // 2, dtype=np.float32) / HD)
    angle = np.arange(length, dtype=np.float32)[:, None] * frequency.astype(np.float32)[None, :]
    both = np.concatenate([np.cos(angle), np.sin(angle)], axis=1).astype(np.float32)
    return both.reshape(length // 128, 128, HD).transpose(0, 2, 1)


def body(
    tokens,
    cotangent,
    segments,
    routes,
    w_qkv,
    w_out,
    attn_norm,
    ffn_norm,
    q_gain,
    k_gain,
    router,
    w_gate_up,
    w_down,
):
    tok = tokens.reshape(2, 128, 1024)
    cot = cotangent.reshape(2, 128, 1024)
    seg = segments.reshape(2, 8, 1, 128).astype(F32)
    routes_t = routes.reshape(2, 128, 8).transpose(0, 2, 1)
    turn = jnp.asarray(turn_table(1024))
    gains = jnp.zeros((128, 2), BF).at[:8, 0].set(q_gain).at[:8, 1].set(k_gain)
    small = jnp.concatenate(
        [router, attn_norm[:, None], ffn_norm[:, None], gains, jnp.zeros((128, 92), BF)], axis=1
    )
    dy_all, wq_all, wo_all, small_t, raw_t, q_t, kv_all, mix_t, lsum, res, ffn, gates_t, sent = front(
        tok, cot, w_qkv, w_out, small, seg, routes_t, turn
    )
    moved_out, moved_dx, share, dw = moe(ffn, dy_all, sent, w_gate_up, w_down)
    in_grad, gq, go, gs = back(
        tok, cot, seg, turn, wq_all, wo_all, small_t, raw_t, q_t, kv_all, mix_t, lsum, res, ffn,
        gates_t, share, moved_dx,
    )
    output = (res + moved_out).astype(BF).reshape(tokens.shape)
    return (
        output,
        in_grad.reshape(tokens.shape),
        gq,
        go,
        gs[32],
        gs[33],
        gs[40:48, 0],
        gs[48:56, 0],
        gs[:32].T,
        dw[:2].astype(F32).reshape(2, 1024, 1024),
        dw[2].astype(F32).reshape(2, 512, 1024),
    )


def solution(mesh):
    return jax.shard_map(
        body,
        mesh=mesh,
        in_specs=(
            P(None, "expert", "dp", None),
            P(None, "expert", "dp", None),
            P(None, "expert", None),
            P(None, "expert", "dp", None),
            P("dp", None),
            P("dp", None),
            P("dp"),
            P("dp"),
            P("dp"),
            P("dp"),
            P("dp", None),
            P("expert", None, None),
            P("expert", None, None),
        ),
        out_specs=(
            P(None, "expert", "dp", None),
            P(None, "expert", "dp", None),
            P("dp", None),
            P("dp", None),
            P("dp"),
            P("dp"),
            P("dp"),
            P("dp"),
            P("dp", None),
            P("expert", None, None),
            P("expert", None, None),
        ),
        check_vma=False,
    )
```

time: 734 us -> 438 us (0.60); the launches traced: 725 us -> 437 us
  Pallas kernels: 209 us -> 409 us
  blocking collectives: 115 us -> 0 us
  waiting for transfers between devices: 99.1 us -> 0 us
  local copies, waits for them, and re-layouts: 113 us -> 17.7 us
  other arithmetic: 100 us -> 9.44 us
  matrix products: 71.7 us -> 0 us
  between operations: 17.1 us -> 0.74 us
    pallas_call x0 -> x2, Pallas kernels: none -> 212 us  [the longest x1 108 us: front(): pl.pallas_call(front_kernel, out_shape=(jax.ShapeDtypeStruct((2, 4, 4, 12...]
    psum x1 -> x0, blocking collectives: 74.6 us -> none  [body(): lax.psum(shard_part[2].astype(jnp.bfloat16), 'expert').astype(jnp.float32)]
    dot_general x30 -> x0, matrix products: 71.7 us -> none  [the longest x2 12 us: body(): jnp.einsum('sgrqk,sqgrd->skgd', probs.astype(jnp.bfloat16), grad_mixed, p...]
    reduce_scatter x3 -> x0, waiting for transfers between devices: 67.9 us -> none  [the longest x2 48.2 us: in_one_piece_2(): filled = lax.psum_scatter(both, axis, scatter_dimension=dim, tiled=True)]
    all_gather x3 -> x0, waiting for transfers between devices: 31.1 us -> none  [the longest x1 23.9 us: in_one_piece(): filled, at, done = (lax.all_gather(both, axis, axis=dim, tiled=True), 0, [])]
    concatenate x7 -> x0, other arithmetic: 30.5 us -> none  [the longest x1 23.2 us: together(): vector, at, done = (jnp.concatenate([a.reshape(-1) for a in arrays]), 0, [])]
    unnamed x2 -> x0, blocking collectives: 28.8 us -> none
    convert_element_type x12 -> x0, local copies, waits for them, and re-layouts: 24 us -> none  [the longest x2 14.3 us: body(): part.astype(jnp.float32)]
  transfers between devices with their start and end apart: 9 -> 0, of which waited for: 5 -> 0; matrix products, arithmetic and copies ran while one was open for 28% -> 0% of each run, Pallas kernels for 0% -> 0%
where the time goes in v2:
time: 438 us; the launch traced here: 437 us
  Pallas kernels  409 us (93%)
  local copies, waits for them, and re-layouts  17.7 us (4%)
  other arithmetic  9.44 us (2%)
    pallas_call x1, Pallas kernels, moe(): pl.pallas_call(moe_kernel, out_shape=(jax.ShapeDtypeStruct((2, 128, 1024)...  198 us
    pallas_call x1, Pallas kernels, front(): pl.pallas_call(front_kernel, out_shape=(jax.ShapeDtypeStruct((2, 4, 4, 12...  108 us
    pallas_call x1, Pallas kernels, back(): pl.pallas_call(back_kernel, out_shape=(jax.ShapeDtypeStruct((2, 128, 1024...  104 us

profile of v2, /device:TPU:0, one launch (start us, length us, event | category | flops | bytes accessed | tf_op | source)
XLA Modules:
  0.0 437.1 jit_solution(5386208175805677412)
XLA Ops:
  0.7 0.6 fusion.1
  1.2 0.7 copy.32
  2.0 0.7 copy.33
  2.7 1.3 convert_bitcast_fusion.seg_ref
  4.0 1.6 scatter.9
  5.6 0.8 copy.35
  6.4 0.8 copy.36
  7.2 0.8 copy.34
  8.0 0.7 concatenate.7.small
  8.7 108.1 %shard_map.221 = (bf16[2,4,4,128,1024]{4,3,2,1,0:T(8,128)(2,1)}, bf16[4,2,128,2048]{3,2,1,0:T(8,128)(2,1)}, bf16[4,2,128,1024]{3,2,1,0:T(8,128)(2,1)}, f32[128,1...) custom-call(bf16[2,128,1024]{2,1,0:T(8,128)(2,1)} %bitcast.37, ...), custom_call_target="tpu_custom_call" | custom-call | flops 5000000000 | bytes 30000000 | tf_op jit(solution)/shard_map/pallas_call | solution.py:543
  116.8 197.6 %shard_map.222 = (f32[2,128,1024]{2,1,0:T(8,128)}, f32[2,128,1024]{2,1,0:T(8,128)}, f32[16,8,128]{2,1,0:T(8,128)}, bf16[3,4,2,128,1024]{4,3,2,1,0:T(8,128)(2,1)}) custom-call(bf16[2,128,1024]{2,1,0:T(8,128)(2,1)} %get-tuple-element.57.ffn_ref.ffn, bf16[2,4,4,128,1024]{4,3,2,1,0:T(8,128)(2,1)} %get-tuple-element.58.dy_hbm, ...), custom_call_target="tpu_custom_call" | custom-call | flops 30000001024 | bytes 30000000 | tf_op jit(solution)/shard_map/pallas_call | solution.py:851
  314.4 0.0 copy-start.1
  314.4 103.5 %shard_map.223 = (bf16[2,128,1024]{2,1,0:T(8,128)(2,1)}, f32[128,2048]{1,0:T(8,128)}, f32[128,1024]{1,0:T(8,128)}, f32[64,128]{1,0:T(8,128)}) custom-call(bf16[2,128,1024]{2,1,0:T(8,128)(2,1)} %bitcast.38, bf16[2,128,1024]{2,1,0:T(8,128)(2,1)} %bitcast.40, f32[2,8,1,128]{3,2,1,0:T(1,128)} %convert_bitcast_fusion.seg_ref, ...), custom_call_target="tpu_custom_call" | custom-call | flops 12000000000 | bytes 30000000 | tf_op jit(solution)/shard_map/pallas_call | solution.py:1174
  418.0 0.9 fusion
  418.9 1.3 slice_bitcast_fusion.1
  420.2 1.3 slice_reduce_fusion
  421.6 1.3 slice_bitcast_fusion
  422.9 1.8 slice.66
  424.6 2.6 slice.65
  427.3 2.5 convert.3
  429.8 4.7 %bitcast_convert_fusion = f32[2,1024,1024]{2,1,0:T(8,128)} fusion(bf16[2,4,2,128,1024]{4,3,2,1,0:T(8,128)(2,1)S(1)} %slice.65), kind=kLoop, calls=%fused_computation | loop fusion | flops 2097152 | bytes 12582912 | tf_op jit(solution)/shard_map/reshape | solution.py:1279
  434.5 0.8 copy.43
  435.3 1.0 copy.44
  436.3 0.8 copy.45
  (12 shorter events, 0.0 us)
Async XLA Ops:
  314.4 103.6 %copy-start.1 = (f32[2,128,1024]{2,1,0:T(8,128)S(1)}, f32[2,128,1024]{2,1,0:T(8,128)}, u32[]{:S(2)}) copy-start(f32[2,128,1024]{2,1,0:T(8,128)} %get-tuple-element.56.res) | copy-start | bytes 3145732
  314.4 103.6 %copy-start.2 = (f32[2,128,1024]{2,1,0:T(8,128)S(1)}, f32[2,128,1024]{2,1,0:T(8,128)}, u32[]{:S(2)}) copy-start(f32[2,128,1024]{2,1,0:T(8,128)} %get-tuple-element.60) | copy-start | bytes 3145732
  429.8 4.7 %copy-start.4 = (bf16[2,128,1024]{2,1,0:T(8,128)(2,1)S(1)}, bf16[2,128,1024]{2,1,0:T(8,128)(2,1)}, u32[]{:S(2)}) copy-start(bf16[2,128,1024]{2,1,0:T(8,128)(2,1)} %get-tuple-element.72) | copy-start | bytes 1572868
  429.8 5.5 %copy-start = (f32[128,2048]{1,0:T(8,128)S(1)}, f32[128,2048]{1,0:T(8,128)}, u32[]{:S(2)}) copy-start(f32[128,2048]{1,0:T(8,128)} %get-tuple-element.118) | copy-start | bytes 3145732
  429.8 6.5 %copy-start.3 = (f32[128,1024]{1,0:T(8,128)S(1)}, f32[128,1024]{1,0:T(8,128)}, u32[]{:S(2)}) copy-start(f32[128,1024]{1,0:T(8,128)} %get-tuple-element.119) | copy-start | bytes 1572868

commit v3 on v2

--- a/solution.py
+++ b/solution.py
@@ -385,10 +385,10 @@
 
 
 def document_bias(seg_ref, bias, mb, mine):
-    own = seg_ref[mb, mine]
+    own = seg_ref[mb, mine].astype(F32)
     for b in range(8):
-        keys = jnp.broadcast_to(seg_ref[mb, b], (128, 128)).T
-        bias[mb, 128 * b : 128 * (b + 1)] = jnp.where(keys == own, 0.0, MASKED)
+        keys = jnp.broadcast_to(seg_ref[mb, b].astype(F32), (128, 128)).T
+        bias[mb, 128 * b : 128 * (b + 1)] = jnp.where(keys == own, 0.0, MASKED).astype(bias.dtype)
 
 
 def pair_columns(ref, mb, g):
@@ -398,62 +398,80 @@
 
 def front_kernel(
     tok, cot, wq, wo, small, seg_ref, routes_ref, turn_hbm,
-    dy_all, wq_all, wo_all, small_t, raw_t, q_t, kv_all, mix_t, lsum, res, ffn, gates_t, sent,
-    small_all, normed, bias, turn, plane_sems, column_sems, local,
+    dy_all, x0_all, wq_out, wo_out, kv_out, raw_out,
+    small_t, q_t, mix_t, lsum, res, ffn, gates_t, sent,
+    wq_all, wo_all, kv_all, raw_t, small_all, normed, bias, turn, plane_sems, column_sems, local,
 ):
     plane, column = Plane(), Column()
     y, c = column.y, column.c
     copies = [
-        pltpu.make_async_copy(wq, wq_all.at[y, c], local.at[0]),
-        pltpu.make_async_copy(wo, wo_all.at[y, c], local.at[1]),
-        pltpu.make_async_copy(small, small_all.at[y, c], local.at[2]),
-        pltpu.make_async_copy(turn_hbm.at[column.me], turn, local.at[3]),
-        pltpu.make_async_copy(cot.at[0], dy_all.at[0, plane.z, plane.x], local.at[4]),
-        pltpu.make_async_copy(cot.at[1], dy_all.at[1, plane.z, plane.x], local.at[5]),
+        pltpu.make_async_copy(small, small_all.at[y, c], local.at[0]),
+        pltpu.make_async_copy(wq.at[:, 1024:2048], wq_all.at[1, y, c], local.at[1]),
+        pltpu.make_async_copy(cot.at[0], dy_all.at[0, plane.z, plane.x], local.at[2]),
+        pltpu.make_async_copy(wq.at[:, 0:1024], wq_all.at[0, y, c], local.at[3]),
+        pltpu.make_async_copy(cot.at[1], dy_all.at[1, plane.z, plane.x], local.at[4]),
+        pltpu.make_async_copy(wo, wo_all.at[y, c], local.at[5]),
+        pltpu.make_async_copy(turn_hbm.at[column.me], turn, local.at[6]),
     ]
     for copy in copies:
         copy.start()
+    outs = [
+        pltpu.make_async_copy(wq_all, wq_out, local.at[7]),
+        pltpu.make_async_copy(wo_all, wo_out, local.at[8]),
+        pltpu.make_async_copy(kv_all, kv_out, local.at[9]),
+        pltpu.make_async_copy(raw_t, raw_out, local.at[10]),
+    ]
+    own_x = pltpu.make_async_copy(ffn.at[0], x0_all.at[plane.z, plane.x], local.at[11])
     greet(plane.neighbours() + column.neighbours())
-    for copy in copies:
-        copy.wait()
     gdy = [Gather(plane, dy_all.at[mb], plane_sems.at[mb]) for mb in range(2)]
-    w_small = ColumnGather(column, small_all, column_sems.at[0], 128)
-    w_q = ColumnGather(column, wq_all, column_sems.at[1], 128)
-    w_o = ColumnGather(column, wo_all, column_sems.at[2], 128)
-    kv = [ColumnGather(column, kv_all.at[mb], column_sems.at[3 + mb], 8) for mb in range(2)]
+    gx = Gather(plane, x0_all, plane_sems.at[2])
+    w_small = ColumnGather(column, small_all, column_sems.at[0], 64)
+    w_q = ColumnGather(column, wq_all.at[0], column_sems.at[1], 128)
+    w_kv = ColumnGather(column, wq_all.at[1], column_sems.at[2], 128)
+    w_o = ColumnGather(column, wo_all, column_sems.at[3], 128)
+    kv = [ColumnGather(column, kv_all.at[mb], column_sems.at[4 + mb], 8) for mb in range(2)]
+    copies[0].wait()
     w_small.step(0)
-    w_q.step(0)
+    copies[1].wait()
+    w_kv.step(0)
+    copies[2].wait()
     gdy[0].step(0)
+    for mb in range(2):
+        document_bias(seg_ref, bias, mb, column.me)
     w_small.step(1)
     w_small.step(2)
     w_small.step(3)
     for b in range(8):
-        small_t[:, 128 * b : 128 * (b + 1)] = small_all[b // 2, b % 2].astype(F32).T
-    for mb in range(2):
-        document_bias(seg_ref, bias, mb, column.me)
+        small_t[:, 128 * b : 128 * (b + 1)] = small_all[b // 2, b % 2].astype(F32)
     attn_gain = small_t[32:33]
     for mb in range(2):
         v = tok[mb].astype(F32)
         normed[128 * mb : 128 * (mb + 1)] = (v * inverse_rms(v, 1) * attn_gain).astype(BF)
+    w_kv.step(1)
     gdy[0].step(1)
-    w_q.step(1)
-    w_o.step(0)
-    w_q.step(2)
+    copies[4].wait()
+    gdy[1].step(0)
+    w_kv.step(2)
+    copies[3].wait()
+    w_q.step(0)
     gdy[0].step(2)
-    w_q.step(3)
-
-    @pl.loop(0, 4)
-    def _(n):
-        cols = pl.ds(pl.multiple_of(n * 512, 512), 512)
-        got = nn(normed[...], wq_all[:, :, :, cols].reshape(1024, 512))
-        for mb in range(2):
-            raw_t[mb, cols] = got[128 * mb : 128 * (mb + 1)].T
+    w_kv.step(3)
+
+    def project(k):
+        @pl.loop(0, 2)
+        def _(n):
+            cols = pl.ds(pl.multiple_of(n * 512, 512), 512)
+            rows = pl.ds(pl.multiple_of(1024 * k + n * 512, 512), 512)
+            got = nn(normed[...], wq_all[k, :, :, :, cols].reshape(1024, 512))
+            for mb in range(2):
+                raw_t[mb, rows] = got[128 * mb : 128 * (mb + 1)].T
 
     query_gain = head_gain(small_t[...], 34)
     key_gain = head_gain(small_t[...], 35)
+    copies[6].wait()
     cosine, sine = turn[:32], turn[32:]
 
-    def heads(mb):
+    def key_heads(mb):
         @pl.loop(0, 8)
         def _(g):
             v = raw_t[mb, pl.ds(pl.multiple_of(1024 + g * 64, 64), 64)]
@@ -461,8 +479,7 @@
             value = raw_t[mb, pl.ds(pl.multiple_of(1536 + g * 64, 64), 64)]
             kv_all[mb, y, c, g] = jnp.concatenate([key, value], axis=0).T.astype(BF)
 
-        kv[mb].step(0)
-
+    def query_heads(mb):
         @pl.loop(0, 16)
         def _(h):
             rows = pl.ds(pl.multiple_of(h * 64, 64), 64)
@@ -479,7 +496,7 @@
             mixed = jnp.zeros((128, 256), F32)
             for j in range(4):
                 keys = kv_all[mb, j, :, g].reshape(256, 128)
-                there = bias[mb, 256 * j : 256 * (j + 1)]
+                there = bias[mb, 256 * j : 256 * (j + 1)].astype(F32)
                 p = jnp.exp(nn(keys, query) + jnp.concatenate([there, there], axis=1))
                 total += jnp.sum(p, axis=0, keepdims=True)
                 mixed += tn(keys, p.astype(BF))
@@ -510,31 +527,54 @@
         for k in range(16):
             sent[k, 2 * mb : 2 * mb + 2] = gates[2 * k : 2 * k + 2]
 
+    project(1)
+    key_heads(0)
+    kv[0].step(0)
+    w_q.step(1)
+    key_heads(1)
+    kv[0].step(1)
+    w_q.step(2)
+    copies[5].wait()
+    w_o.step(0)
     sent[...] = jnp.zeros_like(sent)
-    heads(0)
-    heads(1)
+    w_q.step(3)
+    outs[0].start()
+    project(0)
+    outs[3].start()
+    kv[0].step(2)
+    kv[1].step(0)
+    gdy[1].step(1)
+    query_heads(0)
+    kv[0].step(3)
+    attend(0, 0, 4)
+    w_o.step(1)
     gdy[0].step(3)
-    kv[0].step(1)
-    w_o.step(1)
-    kv[0].step(2)
+    attend(0, 4, 8)
+    w_o.step(2)
     kv[1].step(1)
-    kv[0].step(3)
     gdy[0].step(4)
-    gdy[1].step(0)
-    attend(0, 0, 4)
-    w_o.step(2)
+    query_heads(1)
+    w_o.step(3)
+    outs[1].start()
+    finish(0)
+    own_x.start()
     kv[1].step(2)
-    gdy[1].step(1)
-    attend(0, 4, 8)
     gdy[1].step(2)
-    w_o.step(3)
-    finish(0)
+    own_x.wait()
+    gx.step(0)
     kv[1].step(3)
+    outs[2].start()
     attend(1, 0, 4)
+    gx.step(1)
+    attend(1, 4, 8)
+    gx.step(2)
     gdy[1].step(3)
-    attend(1, 4, 8)
     finish(1)
     gdy[1].step(4)
+    gx.step(3)
+    gx.step(4)
+    for copy in outs:
+        copy.wait()
 
 
 def front(tok, cot, wq, wo, small, seg, routes_t, turn):
@@ -544,12 +584,13 @@
         front_kernel,
         out_shape=(
             jax.ShapeDtypeStruct((2, 4, 4, 128, 1024), BF),
-            jax.ShapeDtypeStruct((4, 2, 128, 2048), BF),
+            jax.ShapeDtypeStruct((4, 4, 128, 1024), BF),
+            jax.ShapeDtypeStruct((2, 4, 2, 128, 1024), BF),
             jax.ShapeDtypeStruct((4, 2, 128, 1024), BF),
-            jax.ShapeDtypeStruct((128, 1024), F32),
+            jax.ShapeDtypeStruct((2, 4, 2, 8, 128, 128), BF),
             jax.ShapeDtypeStruct((2, 2048, 128), F32),
+            jax.ShapeDtypeStruct((64, 1024), F32),
             jax.ShapeDtypeStruct((2, 1024, 128), BF),
-            jax.ShapeDtypeStruct((2, 4, 2, 8, 128, 128), BF),
             jax.ShapeDtypeStruct((2, 1024, 128), BF),
             jax.ShapeDtypeStruct((2, 8, 1, 256), F32),
             jax.ShapeDtypeStruct((2, 128, 1024), F32),
@@ -557,16 +598,20 @@
             jax.ShapeDtypeStruct((2, 32, 128), F32),
             jax.ShapeDtypeStruct((16, 8, 128), F32),
         ),
-        in_specs=[vmem, anywhere, anywhere, anywhere, anywhere, vmem, vmem, anywhere],
-        out_specs=(anywhere,) + (vmem,) * 12,
+        in_specs=[vmem, vmem, anywhere, anywhere, anywhere, vmem, vmem, anywhere],
+        out_specs=(anywhere,) * 6 + (vmem,) * 8,
         scratch_shapes=[
-            pltpu.VMEM((4, 2, 128, 128), BF),
+            pltpu.VMEM((2, 4, 2, 128, 1024), BF),
+            pltpu.VMEM((4, 2, 128, 1024), BF),
+            pltpu.VMEM((2, 4, 2, 8, 128, 128), BF),
+            pltpu.VMEM((2, 2048, 128), F32),
+            pltpu.VMEM((4, 2, 64, 128), BF),
             pltpu.VMEM((256, 1024), BF),
             pltpu.VMEM((2, 1024, 128), F32),
             pltpu.VMEM((64, 128), F32),
-            pltpu.SemaphoreType.DMA((2, 2, 2, 8)),
-            pltpu.SemaphoreType.DMA((5, 2, 8)),
-            pltpu.SemaphoreType.DMA((6,)),
+            pltpu.SemaphoreType.DMA((3, 2, 2, 8)),
+            pltpu.SemaphoreType.DMA((6, 2, 8)),
+            pltpu.SemaphoreType.DMA((12,)),
         ],
         compiler_params=pltpu.CompilerParams(
             collective_id=0, has_side_effects=True, vmem_limit_bytes=56 * MIB
@@ -578,10 +623,10 @@
 
 
 def moe_kernel(
-    ffn_ref, dy_hbm, gates_ref, wgu_hbm, wd_hbm,
-    out_ref, dx_ref, h_ref, dw,
-    x_all, dy_all, r1, r2, r3, r4, xs, ds, os, act, a1, a2, ggu, g_all, ranks, hcol, hs,
-    wgu, wd, ra, rb, rc, sems, column_sems, gsend, grecv, hsend, hrecv, free, dfree, local,
+    ffn_ref, x0_hbm, dy_hbm, gates_ref, wgu_hbm, wd_hbm,
+    out_hbm, dx_ref, h_ref, dw_own,
+    dw, x_all, dy_all, r1, r2, r3, r4, xs, ds, os, gc, act, a1, a2, ggu, g_all, ranks, hcol, hs,
+    wgu, wd, ra, rb, rc, sems, column_sems, gsend, grecv, hsend, hrecv, free, local,
 ):
     plane, column = Plane(), Column()
     me, z, x = plane.me, plane.z, plane.x
@@ -589,13 +634,16 @@
     w2 = pltpu.make_async_copy(wd_hbm, wd, local.at[1])
     w1.start()
     w2.start()
-    own = [pltpu.make_async_copy(ffn_ref.at[mb], x_all.at[mb, z, x], local.at[4 + mb]) for mb in range(2)]
+    own = [
+        pltpu.make_async_copy(ffn_ref.at[1], x_all.at[1, z, x], local.at[4]),
+        pltpu.make_async_copy(x0_hbm, x_all.at[0], local.at[5]),
+    ]
+    outs = [pltpu.make_async_copy(x_all.at[mb], out_hbm.at[mb], local.at[6 + mb]) for mb in range(2)]
     dys = [pltpu.make_async_copy(dy_hbm.at[mb], dy_all.at[mb], local.at[2 + mb]) for mb in range(2)]
     for copy in own + dys:
         copy.start()
     greet(plane.others() + column.neighbours())
-    for copy in own:
-        copy.wait()
+    own[0].wait()
 
     def gate_message(step):
         to = (me + step) % 16
@@ -614,29 +662,23 @@
     for step in range(1, 16):
         gate_message(step).start()
     g_all[me] = gates_ref[me]
-    gx = [Gather(plane, x_all.at[mb], sems.at[mb]) for mb in range(2)]
-
-    def into(ref, mb):
+    gx = Gather(plane, x_all.at[1], sems.at[0])
+    gx.step(0)
+
+    def into(mb):
         def store(place, rows, total):
-            ref[mb, rows] = total
+            dx_ref[mb, rows] = total
 
         return store
 
-    def slots(k):
-        return [r.at[k] for r in (r1, r2, r3, r4)]
-
-    sout = [
-        Scatter(plane, x_all.at[mb], slots(0), sems.at[2 + mb], into(out_ref, mb), free.at[0])
+    sdx = [
+        Scatter(plane, dy_all.at[mb], (r1, r2, r3, r4), sems.at[1 + mb], into(mb), free)
         for mb in range(2)
     ]
-    sdx = [
-        Scatter(plane, dy_all.at[mb], slots(1), sems.at[4 + mb], into(dx_ref, mb), free.at[1])
-        for mb in range(2)
-    ]
 
     def own_part(k):
         def store(r, total):
-            dw[k, column.y, column.c, r] = total.astype(BF)
+            dw_own[k, r] = total.astype(BF)
 
         return store
 
@@ -646,19 +688,6 @@
         )
         for k in range(3)
     ]
-    dall = [ColumnGather(column, dw.at[k], column_sems.at[3 + k], 128) for k in range(3)]
-
-    def parts_free(k):
-        for device in column.neighbours():
-            pl.semaphore_signal(dfree.at[k], inc=1, device_id=device)
-
-    def gather_part(k):
-        pl.semaphore_wait(dfree.at[k], 3)
-        dall[k].step(0)
-
-    for n in range(5):
-        gx[0].step(n)
-    gx[1].step(0)
     for step in range(1, 16):
         gate_message(step).wait_recv()
     for step in range(1, 16):
@@ -744,7 +773,7 @@
                 [ga * a1[e, r].astype(F32), ga * a2[e, r].astype(F32)], axis=1
             ).astype(BF)
             ggu[r] = grad
-            os[e, r] = nt(grad, wgu[e]).astype(BF)
+            gc[e, r] = nt(grad, wgu[e]).astype(BF)
 
         @pl.loop(0, 4)
         def _(m):
@@ -760,108 +789,89 @@
         @pl.loop(0, 16)
         def _(s):
             pick = jnp.concatenate(places(s, mb), axis=0).astype(BF)
-            both = jnp.concatenate([os[0, span(s)], os[1, span(s)]], axis=0)
+            both = jnp.concatenate([gc[0, span(s)], gc[1, span(s)]], axis=0)
             dy_all[mb, s // 4, s % 4] = tn(pick, both).astype(BF)
 
-    w1.wait()
-    w2.wait()
+    own[1].wait()
     for copy in dys:
         copy.wait()
     select(0)
-    gx[1].step(1)
+    gx.step(1)
+    w1.wait()
+    w2.wait()
     forward(0)
-    gx[1].step(2)
+    gx.step(2)
     forward(1)
-    combine_out(0)
-    gx[1].step(3)
-    sout[0].step(0)
     backward(0, 0)
-    gx[1].step(4)
-    sout[0].step(1)
+    gx.step(3)
     backward(0, 1)
     combine_dx(0)
-    sout[0].step(2)
     sdx[0].step(0)
+    gx.step(4)
+    combine_out(0)
+    outs[0].start()
+    sdx[0].step(1)
     select(1)
-    sout[0].step(3)
-    sdx[0].step(1)
     forward(0)
-    sout[0].step(4)
-    sout[0].give_credit()
     sdx[0].step(2)
+    backward(1, 0)
+    dsum[0].step(0)
+    sdx[0].step(3)
     forward(1)
-    sdx[0].step(3)
-    combine_out(1)
-    h_ref[me] = hs[me]
-    for step in range(1, 16):
-        h_message(step).start()
-    sout[1].take_credit()
-    sout[1].step(0)
+    dsum[0].step(1)
     sdx[0].step(4)
     sdx[0].give_credit()
-    backward(1, 0)
-    dsum[0].step(0)
-    sout[1].step(1)
     backward(1, 1)
     dsum[1].step(0)
     dsum[2].step(0)
-    dsum[0].step(1)
-    sout[1].step(2)
+    dsum[0].step(2)
     combine_dx(1)
     sdx[1].take_credit()
     sdx[1].step(0)
     dsum[1].step(1)
-    sout[1].step(3)
-    dsum[0].step(2)
+    dsum[2].step(1)
+    combine_out(1)
+    outs[1].start()
     sdx[1].step(1)
-    dsum[2].step(1)
-    sout[1].step(4)
     dsum[0].step(3)
-    parts_free(0)
+    h_ref[me] = hs[me]
+    for step in range(1, 16):
+        h_message(step).start()
     dsum[1].step(2)
-    gather_part(0)
     sdx[1].step(2)
     dsum[2].step(2)
     dsum[1].step(3)
-    parts_free(1)
-    dall[0].step(1)
-    gather_part(1)
     sdx[1].step(3)
     dsum[2].step(3)
-    parts_free(2)
-    dall[1].step(1)
-    dall[0].step(2)
-    gather_part(2)
     sdx[1].step(4)
-    dall[2].step(1)
-    dall[1].step(2)
-    dall[2].step(2)
-    for k in range(3):
-        dall[k].step(3)
     for step in range(1, 16):
         h_message(step).wait_recv()
     for step in range(1, 16):
         h_message(step).wait_send()
-
-
-def moe(ffn, dy, gates, w_gate_up, w_down):
+    for copy in outs:
+        copy.wait()
+
+
+def moe(ffn, x0, dy, gates, w_gate_up, w_down):
     vmem = pl.BlockSpec(memory_space=pltpu.VMEM)
     anywhere = pl.BlockSpec(memory_space=pl.ANY)
     rows = 16 * SLOTS
     return pl.pallas_call(
         moe_kernel,
         out_shape=(
-            jax.ShapeDtypeStruct((2, 128, 1024), F32),
+            jax.ShapeDtypeStruct((2, 4, 4, 128, 1024), BF),
             jax.ShapeDtypeStruct((2, 128, 1024), F32),
             jax.ShapeDtypeStruct((16, 8, 128), F32),
-            jax.ShapeDtypeStruct((3, 4, 2, 128, 1024), BF),
+            jax.ShapeDtypeStruct((3, 128, 1024), BF),
         ),
-        in_specs=[anywhere, anywhere, vmem, anywhere, anywhere],
-        out_specs=(vmem,) * 4,
+        in_specs=[anywhere, anywhere, anywhere, vmem, anywhere, anywhere],
+        out_specs=(anywhere,) + (vmem,) * 3,
         scratch_shapes=[
+            pltpu.VMEM((3, 4, 2, 128, 1024), BF),
             pltpu.VMEM((2, 4, 4, 128, 1024), BF),
             pltpu.VMEM((2, 4, 4, 128, 1024), BF),
-            *scatter_slots(128, 1024, lead=(2,)),
+            *scatter_slots(128, 1024),
+            pltpu.VMEM((2, rows, 1024), BF),
             pltpu.VMEM((2, rows, 1024), BF),
             pltpu.VMEM((2, rows, 1024), BF),
             pltpu.VMEM((2, rows, 1024), BF),
@@ -876,15 +886,14 @@
             pltpu.VMEM((2, 1024, 1024), BF),
             pltpu.VMEM((2, 512, 1024), BF),
             *column_slots((128, 1024), lead=(3,)),
-            pltpu.SemaphoreType.DMA((6, 2, 2, 8)),
-            pltpu.SemaphoreType.DMA((6, 2, 8)),
+            pltpu.SemaphoreType.DMA((3, 2, 2, 8)),
+            pltpu.SemaphoreType.DMA((3, 2, 8)),
             pltpu.SemaphoreType.DMA((16,)),
             pltpu.SemaphoreType.DMA((16,)),
             pltpu.SemaphoreType.DMA((16,)),
             pltpu.SemaphoreType.DMA((16,)),
-            pltpu.SemaphoreType.REGULAR((2,)),
-            pltpu.SemaphoreType.REGULAR((3,)),
-            pltpu.SemaphoreType.DMA((6,)),
+            pltpu.SemaphoreType.REGULAR,
+            pltpu.SemaphoreType.DMA((8,)),
         ],
         compiler_params=pltpu.CompilerParams(
             collective_id=1, has_side_effects=True, vmem_limit_bytes=63 * MIB
@@ -892,7 +901,7 @@
         cost_estimate=pl.CostEstimate(
             flops=30_000_000_000, bytes_accessed=30_000_000, transcendentals=2_000_000
         ),
-    )(ffn, dy, gates, w_gate_up, w_down)
+    )(ffn, x0, dy, gates, w_gate_up, w_down)
 
 
 def norm_grad(grad, v, inverse, gain, axis):
@@ -903,12 +912,12 @@
 
 def back_kernel(
     tok, cot, seg_ref, turn_hbm, wq_hbm, wo_hbm, small_t, raw_hbm, q_t, kv_hbm, mix_t, lsum,
-    res, ffn, gates_t, share_ref, dx,
-    in_grad, gq, go, gs,
+    res, ffn, gates_t, share_ref, dx, out_hbm, dw_own,
+    dgu_all, dd_all, output, in_grad, gq, go, gs,
     wq_all, wo_all, kv_all, raw_t, turn, bias, gres, branch, gm_t, dq_t, own_kv, gp, normed_t, gn,
     part_kv, part_w, part_s, q_sum, k_sum, ra, rb, rc, sa, sb, sc, plane_buf, plane_all, p1, p2, p3, p4, ta, tb, tc,
-    logits, routers, router_sum,
-    column_sems, plane_sems, local,
+    logits, routers, router_sum, out_part, r1, r2, r3, r4, parcels, got_parcels, small_own, kv_total,
+    column_sems, plane_sems, far_send, far_recv, all_send, all_recv, free, local,
 ):
     plane, column = Plane(), Column()
     y, c = column.y, column.c
@@ -919,53 +928,93 @@
         pltpu.make_async_copy(wq_hbm, wq_all, local.at[3]),
         pltpu.make_async_copy(turn_hbm.at[column.me], turn, local.at[4]),
     ]
-    for copy in copies:
+    parts = [pltpu.make_async_copy(out_hbm.at[mb], out_part, local.at[5 + mb]) for mb in range(2)]
+    dw_refs = [dgu_all.at[0], dgu_all.at[1], dd_all]
+    owns = [pltpu.make_async_copy(dw_own.at[n], dw_refs[n].at[y, c], local.at[7 + n]) for n in range(3)]
+    for copy in parts[:1] + owns + copies:
         copy.start()
-    greet(plane.neighbours() + column.neighbours())
-    plane_buf[...] = jnp.zeros_like(plane_buf)
+    greet(plane.others() + column.neighbours())
+    dall = [ColumnGather(column, dw_refs[n], column_sems.at[8 + n], 128) for n in range(3)]
+
+    def add_residual(mb):
+        def store(place, rows, total):
+            output[mb, rows] = (res[mb, rows] + total).astype(BF)
+
+        return store
+
+    sout = [
+        Scatter(plane, out_part, (r1, r2, r3, r4), plane_sems.at[mb], add_residual(mb), free)
+        for mb in range(2)
+    ]
+    parts[0].wait()
+    sout[0].step(0)
+    for copy in owns:
+        copy.wait()
+    dall[0].step(0)
     part_s[...] = jnp.zeros_like(part_s)
     q_sum[...] = jnp.zeros_like(q_sum)
     k_sum[...] = jnp.zeros_like(k_sum)
     for mb in range(2):
         document_bias(seg_ref, bias, mb, column.me)
 
-    def place_w(first):
+    def place_w(which):
         def store(r, total):
             low = total.astype(BF)
             half = r.start // 64
             some = pl.ds(pl.multiple_of(r.start % 64, 16), 16)
-            for k in range(2):
-                n = half * 8 + first + k
-                plane_buf[n // 4, n % 4, some] = low[:, 512 * k : 512 * (k + 1)]
+            for k in range(8):
+                n = half * 8 + k
+                piece = low[:, 128 * k : 128 * (k + 1)]
+                if which == 2:
+                    parcels[n, some] = piece
+                else:
+                    plane_buf[which, n // 4, n % 4, some] = piece
 
         return store
 
     def place_s(r, total):
-        plane_buf[1, 2, r, 0:128] = total.astype(BF)
-
-    def place_kv(mb):
+        small_own[r] = total.astype(BF)
+
+    def place_kv(mb, half):
         def store(r, total):
-            own_kv[mb, r] = total
+            own_kv[mb, pl.ds(r.start + 4 * half, 1)] = total
 
         return store
 
     w_sums = [
         ColumnScatter(
-            column, part_w.at[k], (ra.at[k], rb.at[k], rc.at[k]), column_sems.at[k], 128,
-            place_w(first),
+            column, part_w.at[n], (ra.at[n], rb.at[n], rc.at[n]), column_sems.at[n], 128, place_w(n)
         )
-        for k, first in ((0, 4), (1, 0), (2, 2))
+        for n in range(3)
     ]
     kv_sums = [
-        ColumnScatter(
-            column, part_kv.at[mb],
-            (sa.at[mb], sb.at[mb], sc.at[mb]),
-            column_sems.at[3 + mb], 8, place_kv(mb), group=1,
-        )
+        [
+            ColumnScatter(
+                column, part_kv.at[mb, half],
+                (sa.at[mb, half], sb.at[mb, half], sc.at[mb, half]),
+                column_sems.at[4 + 2 * mb + half], 4, place_kv(mb, half), group=1,
+            )
+            for half in range(2)
+        ]
         for mb in range(2)
     ]
-
-    s_sum = ColumnScatter(column, part_s, (ta, tb, tc), column_sems.at[5], 64, place_s)
+    s_sum = ColumnScatter(column, part_s, (ta, tb, tc), column_sems.at[3], 64, place_s)
+
+    def keep(n):
+        def store(place, rows, total):
+            plane_all[(n, *place)] = total.astype(BF)
+
+        return store
+
+    over = [
+        Scatter(
+            plane, plane_buf.at[n], (p1.at[n], p2.at[n], p3.at[n], p4.at[n]), plane_sems.at[2 + n],
+            keep(n), height=64,
+        )
+        for n in range(2)
+    ]
+    spread = [Gather(plane, plane_all.at[n], plane_sems.at[4 + n], height=64) for n in range(2)]
+
     def tokens_of(mb):
         return pl.ds(128 * mb, 128)
 
@@ -1008,6 +1057,7 @@
         part_w[0, n] = nn(mixed, branch[...]).astype(BF).reshape(2, 128, 1024)
 
     w_sums[0].step(0)
+    dall[1].step(0)
     copies[1].wait()
 
     def attend(mb, start, stop):
@@ -1025,28 +1075,58 @@
             dq = jnp.zeros((128, 256), F32)
             for j in range(4):
                 keys = kv_all[mb, j, :, g].reshape(256, 128)
-                there = bias[mb, 256 * j : 256 * (j + 1)]
+                there = bias[mb, 256 * j : 256 * (j + 1)].astype(F32)
                 got = nn(keys, both)
                 p = jnp.exp(got[:, :256] + jnp.concatenate([there, there], axis=1)) * scale
                 ds = (p * (got[:, 256:] - inner)).astype(BF)
                 dq += tn(keys, ds)
                 dkv = nt(jnp.concatenate([ds, p.astype(BF)], axis=1), both)
-                part_kv[mb, j, :, g] = dkv.astype(BF).reshape(2, 128, 128)
+                part_kv[mb, g // 4, j, :, g % 4] = dkv.astype(BF).reshape(2, 128, 128)
             dq = dq[:64] * HD ** (-0.5)
             rows = pl.ds(pl.multiple_of(g * 128, 128), 128)
             dq_t[mb, rows] = jnp.concatenate([dq[:, :128], dq[:, 128:]], axis=0)
 
-    attend(0, 0, 4)
+    attend(0, 0, 2)
+    dall[0].step(1)
+    sout[0].step(1)
+    attend(0, 2, 4)
+    kv_sums[0][0].step(0)
     w_sums[0].step(1)
-    attend(0, 4, 8)
-    kv_sums[0].step(0)
+    dall[0].step(2)
+    dall[1].step(1)
+    dall[2].step(0)
+    attend(0, 4, 6)
+    kv_sums[0][0].step(1)
+    sout[0].step(2)
+    attend(0, 6, 8)
+    kv_sums[0][1].step(0)
     w_sums[0].step(2)
-    attend(1, 0, 4)
-    kv_sums[0].step(1)
+    dall[1].step(2)
+    dall[2].step(1)
+    attend(1, 0, 2)
+    kv_sums[0][1].step(1)
+    kv_sums[0][0].step(2)
+    sout[0].step(3)
+    dall[0].step(3)
+    attend(1, 2, 4)
+    kv_sums[1][0].step(0)
     w_sums[0].step(3)
-    attend(1, 4, 8)
-    kv_sums[1].step(0)
-    kv_sums[0].step(2)
+    sout[0].step(4)
+    parts[1].start()
+    sout[0].give_credit()
+    dall[2].step(2)
+    attend(1, 4, 6)
+    kv_sums[1][0].step(1)
+    kv_sums[0][1].step(2)
+    kv_sums[0][0].step(3)
+    over[0].step(0)
+    parts[1].wait()
+    sout[1].take_credit()
+    sout[1].step(0)
+    attend(1, 6, 8)
+    kv_sums[1][1].step(0)
+    dall[1].step(3)
+    over[0].step(1)
     copies[2].wait()
     copies[4].wait()
     cosine, sine = turn[:32], turn[32:]
@@ -1060,9 +1140,9 @@
         total[...] += gain_part
         return grad_v
 
-    @pl.loop(0, 8)
-    def _(g):
-        for mb in range(2):
+    def queries_back(mb):
+        @pl.loop(0, 8)
+        def _(g):
             pieces = []
             for r in range(2):
                 rows = pl.ds(pl.multiple_of(g * 128 + r * 64, 64), 64)
@@ -1070,8 +1150,14 @@
             cols = pl.ds(pl.multiple_of(g * 128, 128), 128)
             gp[tokens_of(mb), cols] = jnp.concatenate(pieces, axis=0).T.astype(BF)
 
-    kv_sums[0].step(3)
-    kv_sums[1].step(1)
+    queries_back(0)
+    kv_sums[1][1].step(1)
+    kv_sums[1][0].step(2)
+    queries_back(1)
+    kv_sums[0][1].step(3)
+    over[0].step(2)
+    sout[1].step(1)
+    dall[2].step(3)
     for mb in range(2):
         v = tok[mb].astype(F32)
         normed = (v * inverse_rms(v, 1) * attn_gain).astype(BF).astype(F32)
@@ -1105,22 +1191,37 @@
 
     weight_part(1)
     w_sums[1].step(0)
-    kv_sums[1].step(2)
+    kv_sums[1][1].step(2)
+    kv_sums[1][0].step(3)
+    over[0].step(3)
     keys_back(0)
     w_sums[1].step(1)
-    kv_sums[1].step(3)
+    sout[1].step(2)
+    copies[3].wait()
+
+    @pl.loop(0, 4)
+    def _(n):
+        cols = pl.ds(pl.multiple_of(n * 256, 256), 256)
+        gn[:, cols] = nt(gp[:, 0:1024], wq_all[0, n].reshape(256, 1024))
+
+    kv_sums[1][1].step(3)
     keys_back(1)
     weight_part(2)
     w_sums[2].step(0)
     w_sums[1].step(2)
-    copies[3].wait()
+    over[0].step(4)
+    spread[0].step(0)
+    sout[1].step(3)
 
     @pl.loop(0, 4)
     def _(n):
         cols = pl.ds(pl.multiple_of(n * 256, 256), 256)
-        gn[:, cols] = nt(gp[...], wq_all[n].reshape(256, 2048))
+        gn[:, cols] = gn[:, cols] + nt(gp[:, 1024:2048], wq_all[1, n].reshape(256, 1024))
 
     w_sums[2].step(1)
+    w_sums[1].step(3)
+    over[1].step(0)
+    spread[0].step(1)
     attn_gain_grad = jnp.zeros((1, 1024), F32)
     for mb in range(2):
         v = tok[mb].astype(F32)
@@ -1140,40 +1241,78 @@
             jnp.sum(k_sum[heads], axis=1, keepdims=True), (8, 128)
         )
     s_sum.step(0)
+    over[1].step(1)
+    spread[0].step(2)
     s_sum.step(1)
-    w_sums[1].step(3)
     w_sums[2].step(2)
     s_sum.step(2)
+    over[1].step(2)
+    spread[0].step(3)
+    sout[1].step(4)
+    over[1].step(3)
+    s_sum.step(3)
     w_sums[2].step(3)
-    s_sum.step(3)
-
-    def keep(place, rows, total):
-        plane_all[place] = total.astype(BF)
-
-    over = Scatter(plane, plane_buf, (p1, p2, p3, p4), plane_sems.at[0], keep, height=64)
-    back = Gather(plane, plane_all, plane_sems.at[1], height=64)
-    for n in range(5):
-        over.step(n)
-    for n in range(5):
-        back.step(n)
-    for half in range(2):
-        rows = pl.ds(64 * half, 64)
-        for k in range(4):
-            n = half * 8 + k
-            gq[rows, 512 * k : 512 * (k + 1)] = plane_all[n // 4, n % 4].astype(F32)
-        for k in range(2):
-            n = half * 8 + 4 + k
-            go[rows, 512 * k : 512 * (k + 1)] = plane_all[n // 4, n % 4].astype(F32)
-    gs[...] = plane_all[1, 2, :, 0:128].astype(F32)
-
-
-def back(tok, cot, seg, turn, wq_all, wo_all, small_t, raw_t, q_t, kv_all, mix_t, lsum, res, ffn, gates_t, share, dx):
+    me = plane.me
+
+    @pl.loop(0, 16)
+    def _(n):
+        parcels[n, 64:128] = small_own[...]
+
+    def parcel(step):
+        to = (me + step) % 16
+        return send(
+            parcels.at[to], got_parcels.at[me], far_send.at[step], far_recv.at[step], {"expert": to}
+        )
+
+    def total_message(step):
+        to = (me + step) % 16
+        return send(
+            kv_total.at[me], kv_total.at[me], all_send.at[step], all_recv.at[step], {"expert": to}
+        )
+
+    for step in range(1, 16):
+        parcel(step).start()
+    got_parcels[me] = parcels[me]
+    over[1].step(4)
+    spread[1].step(0)
+    spread[0].step(4)
+    for step in range(1, 16):
+        parcel(step).wait_recv()
+    total = got_parcels[0].astype(F32)
+    for n in range(1, 16):
+        total += got_parcels[n].astype(F32)
+    kv_total[me] = total[:64].astype(BF)
+    for step in range(1, 16):
+        total_message(step).start()
+    gs[...] = total[64:]
+    for n in range(16):
+        place = slice(64 * (n // 8), 64 * (n // 8) + 64), slice(128 * (n % 8), 128 * (n % 8) + 128)
+        go[place] = plane_all[0, n // 4, n % 4].astype(F32)
+    for n in range(1, 5):
+        spread[1].step(n)
+    for n in range(16):
+        place = slice(64 * (n // 8), 64 * (n // 8) + 64), slice(128 * (n % 8), 128 * (n % 8) + 128)
+        gq[place] = plane_all[1, n // 4, n % 4].astype(F32)
+    for step in range(1, 16):
+        total_message(step).wait_recv()
+    for n in range(16):
+        first = 1024 + 128 * (n % 8)
+        gq[64 * (n // 8) : 64 * (n // 8) + 64, first : first + 128] = kv_total[n].astype(F32)
+    for step in range(1, 16):
+        parcel(step).wait_send()
+        total_message(step).wait_send()
+
+
+def back(tok, cot, seg, turn, wq_all, wo_all, small_t, raw_t, q_t, kv_all, mix_t, lsum, res, ffn, gates_t, share, dx, out_part, dw_own):
     vmem = pl.BlockSpec(memory_space=pltpu.VMEM)
     anywhere = pl.BlockSpec(memory_space=pl.ANY)
-    kv_slots = column_slots((8, 128, 128), lead=(2,))
+    kv_slots = column_slots((4, 128, 128), lead=(2, 2))
     return pl.pallas_call(
         back_kernel,
         out_shape=(
+            jax.ShapeDtypeStruct((2, 4, 2, 128, 1024), BF),
+            jax.ShapeDtypeStruct((4, 2, 128, 1024), BF),
+            jax.ShapeDtypeStruct((2, 128, 1024), BF),
             jax.ShapeDtypeStruct((2, 128, 1024), BF),
             jax.ShapeDtypeStruct((128, 2048), F32),
             jax.ShapeDtypeStruct((128, 1024), F32),
@@ -1181,16 +1320,16 @@
         ),
         in_specs=[
             vmem, vmem, vmem, anywhere, anywhere, anywhere, vmem, anywhere, vmem, anywhere,
-            vmem, vmem, vmem, vmem, vmem, vmem, vmem,
+            vmem, vmem, vmem, vmem, vmem, vmem, vmem, anywhere, vmem,
         ],
-        out_specs=(vmem,) * 4,
+        out_specs=(anywhere,) * 2 + (vmem,) * 5,
         scratch_shapes=[
-            pltpu.VMEM((4, 2, 128, 2048), BF),
+            pltpu.VMEM((2, 4, 2, 128, 1024), BF),
             pltpu.VMEM((4, 2, 128, 1024), BF),
             pltpu.VMEM((2, 4, 2, 8, 128, 128), BF),
             pltpu.VMEM((2, 2048, 128), F32),
             pltpu.VMEM((64, 128), F32),
-            pltpu.VMEM((2, 1024, 128), F32),
+            pltpu.VMEM((2, 1024, 128), BF),
             pltpu.VMEM((2, 128, 1024), F32),
             pltpu.VMEM((256, 1024), BF),
             pltpu.VMEM((2, 1024, 128), BF),
@@ -1199,31 +1338,42 @@
             pltpu.VMEM((256, 2048), BF),
             pltpu.VMEM((1024, 256), BF),
             pltpu.VMEM((256, 1024), F32),
-            pltpu.VMEM((2, 4, 2, 8, 128, 128), BF),
+            pltpu.VMEM((2, 2, 4, 2, 4, 128, 128), BF),
             pltpu.VMEM((3, 4, 2, 128, 1024), BF),
             pltpu.VMEM((4, 2, 64, 128), F32),
             pltpu.VMEM((64, 128), F32),
             pltpu.VMEM((64, 128), F32),
             *column_slots((128, 1024), lead=(3,)),
             *kv_slots,
-            pltpu.VMEM((4, 4, 64, 512), BF),
-            pltpu.VMEM((4, 4, 64, 512), BF),
-            *scatter_slots(64, 512),
+            pltpu.VMEM((2, 4, 4, 64, 128), BF),
+            pltpu.VMEM((2, 4, 4, 64, 128), BF),
+            *scatter_slots(64, 128, lead=(2,)),
             *column_slots((64, 128), F32),
             pltpu.VMEM((64, 256), BF),
             pltpu.VMEM((64, 1024), BF),
             pltpu.VMEM((64, 1024), F32),
-            pltpu.SemaphoreType.DMA((6, 2, 8)),
-            pltpu.SemaphoreType.DMA((2, 2, 2, 8)),
-            pltpu.SemaphoreType.DMA((5,)),
+            pltpu.VMEM((4, 4, 128, 1024), BF),
+            *scatter_slots(128, 1024),
+            pltpu.VMEM((16, 128, 128), BF),
+            pltpu.VMEM((16, 128, 128), BF),
+            pltpu.VMEM((64, 128), BF),
+            pltpu.VMEM((16, 64, 128), BF),
+            pltpu.SemaphoreType.DMA((11, 2, 8)),
+            pltpu.SemaphoreType.DMA((6, 2, 2, 8)),
+            pltpu.SemaphoreType.DMA((16,)),
+            pltpu.SemaphoreType.DMA((16,)),
+            pltpu.SemaphoreType.DMA((16,)),
+            pltpu.SemaphoreType.DMA((16,)),
+            pltpu.SemaphoreType.REGULAR,
+            pltpu.SemaphoreType.DMA((10,)),
         ],
         compiler_params=pltpu.CompilerParams(
-            collective_id=2, has_side_effects=True, vmem_limit_bytes=60 * MIB
+            collective_id=2, has_side_effects=True, vmem_limit_bytes=63 * MIB
         ),
         cost_estimate=pl.CostEstimate(
             flops=12_000_000_000, bytes_accessed=30_000_000, transcendentals=5_000_000
         ),
-    )(tok, cot, seg, turn, wq_all, wo_all, small_t, raw_t, q_t, kv_all, mix_t, lsum, res, ffn, gates_t, share, dx)
+    )(tok, cot, seg, turn, wq_all, wo_all, small_t, raw_t, q_t, kv_all, mix_t, lsum, res, ffn, gates_t, share, dx, out_part, dw_own)
 
 
 def turn_table(length):
@@ -1250,24 +1400,21 @@
 ):
     tok = tokens.reshape(2, 128, 1024)
     cot = cotangent.reshape(2, 128, 1024)
-    seg = segments.reshape(2, 8, 1, 128).astype(F32)
+    seg = segments.reshape(2, 8, 1, 128)
     routes_t = routes.reshape(2, 128, 8).transpose(0, 2, 1)
     turn = jnp.asarray(turn_table(1024))
-    gains = jnp.zeros((128, 2), BF).at[:8, 0].set(q_gain).at[:8, 1].set(k_gain)
-    small = jnp.concatenate(
-        [router, attn_norm[:, None], ffn_norm[:, None], gains, jnp.zeros((128, 92), BF)], axis=1
+    gains = jnp.pad(jnp.stack([q_gain, k_gain]), ((0, 28), (0, 120)))
+    small = jnp.concatenate([router.T, attn_norm[None], ffn_norm[None], gains])
+    (
+        dy_all, x0, wq_all, wo_all, kv_all, raw_t, small_t, q_t, mix_t, lsum, res, ffn, gates_t, sent
+    ) = front(tok, cot, w_qkv, w_out, small, seg, routes_t, turn)
+    out_part, moved_dx, share, dw_own = moe(ffn, x0, dy_all, sent, w_gate_up, w_down)
+    dgu, dd, output, in_grad, gq, go, gs = back(
+        tok, cot, seg, turn, wq_all, wo_all, small_t, raw_t, q_t, kv_all, mix_t, lsum, res, ffn,
+        gates_t, share, moved_dx, out_part, dw_own,
     )
-    dy_all, wq_all, wo_all, small_t, raw_t, q_t, kv_all, mix_t, lsum, res, ffn, gates_t, sent = front(
-        tok, cot, w_qkv, w_out, small, seg, routes_t, turn
-    )
-    moved_out, moved_dx, share, dw = moe(ffn, dy_all, sent, w_gate_up, w_down)
-    in_grad, gq, go, gs = back(
-        tok, cot, seg, turn, wq_all, wo_all, small_t, raw_t, q_t, kv_all, mix_t, lsum, res, ffn,
-        gates_t, share, moved_dx,
-    )
-    output = (res + moved_out).astype(BF).reshape(tokens.shape)
     return (
-        output,
+        output.reshape(tokens.shape),
         in_grad.reshape(tokens.shape),
         gq,
         go,
@@ -1276,8 +1423,8 @@
         gs[40:48, 0],
         gs[48:56, 0],
         gs[:32].T,
-        dw[:2].astype(F32).reshape(2, 1024, 1024),
-        dw[2].astype(F32).reshape(2, 512, 1024),
+        dgu.astype(F32).reshape(2, 1024, 1024),
+        dd.astype(F32).reshape(2, 512, 1024),
     )
 
 

time: 438 us -> 359 us (0.82)
  Pallas kernels: 409 us -> 340 us
  local copies, waits for them, and re-layouts: 17.7 us -> 7.38 us
    pallas_call x2, Pallas kernels: 301 us -> 233 us  [the longest x1 117 us: moe(): pl.pallas_call(moe_kernel, out_shape=(jax.ShapeDtypeStruct((2, 4, 4, 128,...]
    slice x2 -> x0, local copies, waits for them, and re-layouts: 4.39 us -> none  [the longest x1 2.63 us: body(): dw[:2].astype(F32).reshape(2, 1024, 1024)]
    reshape x1 -> x2, other arithmetic: 4.73 us -> 8.8 us  [the longest x1 4.73 us: body(): dgu.astype(F32).reshape(2, 1024, 1024)]
where the time goes in v3:
time: 359 us
  Pallas kernels  340 us (95%)
  other arithmetic  10.8 us (3%)
  local copies, waits for them, and re-layouts  7.38 us (2%)
    pallas_call x1, Pallas kernels, moe(): pl.pallas_call(moe_kernel, out_shape=(jax.ShapeDtypeStruct((2, 4, 4, 128,...  117 us
    pallas_call x1, Pallas kernels, back(): pl.pallas_call(back_kernel, out_shape=(jax.ShapeDtypeStruct((2, 4, 2, 128...  116 us
    pallas_call x1, Pallas kernels, front(): pl.pallas_call(front_kernel, out_shape=(jax.ShapeDtypeStruct((2, 4, 4, 12...  107 us

profile of v3, /device:TPU:0, one launch (start us, length us, event | category | flops | bytes accessed | tf_op | source)
XLA Modules:
  0.0 358.7 jit_solution(12965465825160810617)
XLA Ops:
  0.6 0.7 fusion.5
  1.3 1.3 pad_maximum_fusion.small
  2.7 107.0 %shard_map.221 = (bf16[2,4,4,128,1024]{4,3,2,1,0:T(8,128)(2,1)}, bf16[4,4,128,1024]{3,2,1,0:T(8,128)(2,1)}, bf16[2,4,2,128,1024]{4,3,2,1,0:T(8,128)(2,1)}, bf16[...) custom-call(bf16[2,128,1024]{2,1,0:T(8,128)(2,1)} %bitcast.36, ...), custom_call_target="tpu_custom_call" | custom-call | flops 5000000000 | bytes 30000000 | tf_op jit(solution)/shard_map/pallas_call | solution.py:583
  109.6 117.3 %shard_map.222 = (bf16[2,4,4,128,1024]{4,3,2,1,0:T(8,128)(2,1)}, f32[2,128,1024]{2,1,0:T(8,128)}, f32[16,8,128]{2,1,0:T(8,128)}, bf16[3,128,1024]{2,1,0:T(8,128)(2,1)}) custom-call(bf16[2,128,1024]{2,1,0:T(8,128)(2,1)} %get-tuple-element.45.ffn_ref.ffn, bf16[4,4,128,1024]{3,2,1,0:T(8,128)(2,1)} %get-tuple-element.47.x0_hbm, ...), custom_call_target="tpu_custom_call" | custom-call | flops 30000001024 | bytes 30000000 | tf_op jit(solution)/shard_map/pallas_call | solution.py:859
  227.0 115.5 %shard_map.223 = (bf16[2,4,2,128,1024]{4,3,2,1,0:T(8,128)(2,1)}, bf16[4,2,128,1024]{3,2,1,0:T(8,128)(2,1)}, bf16[2,128,1024]{2,1,0:T(8,128)(2,1)}, bf16[2,128,10...) custom-call(bf16[2,128,1024]{2,1,0:T(8,128)(2,1)} %bitcast.37, ...), custom_call_target="tpu_custom_call" | custom-call | flops 12000000000 | bytes 30000000 | tf_op jit(solution)/shard_map/pallas_call | solution.py:1310
  342.5 0.0 copy-start
  342.5 1.3 slice_bitcast_fusion.1
  343.9 1.3 slice_reduce_fusion
  345.2 1.3 slice_bitcast_fusion
  346.5 4.1 %convert.3 = f32[2,512,1024]{2,1,0:T(8,128)} convert(bf16[2,512,1024]{2,1,0:T(8,128)(2,1)} %bitcast.28) | non-fusion elementwise | flops 1048576 | bytes 6291456 | tf_op jit(solution)/shard_map/reshape | solution.py:1427
  350.6 0.0 copy-done
  350.6 0.0 copy-start.4
  350.6 0.0 copy-start.3
  350.6 0.0 copy-start.1
  350.6 4.7 %bitcast_convert_fusion = f32[2,1024,1024]{2,1,0:T(8,128)} fusion(bf16[2,4,2,128,1024]{4,3,2,1,0:T(8,128)(2,1)S(1)} %copy-done), kind=kLoop, calls=%fused_computation | loop fusion | flops 2097152 | bytes 12582912 | tf_op jit(solution)/shard_map/reshape | solution.py:1426
  355.3 0.0 copy-done.4
  355.3 0.0 copy-start.2
  355.3 0.8 copy.33
  356.1 0.0 copy-done.3
  356.1 0.8 copy.34
  356.9 0.0 copy-done.1
  356.9 1.0 copy.35
  357.9 0.0 copy-done.2
  357.9 0.8 copy.36
Async XLA Ops:
  342.5 8.1 %copy-start = (bf16[2,4,2,128,1024]{4,3,2,1,0:T(8,128)(2,1)S(1)}, bf16[2,4,2,128,1024]{4,3,2,1,0:T(8,128)(2,1)}, u32[]{:S(2)}) copy-start(bf16[2,4,2,128,1024]{4,3,2,1,0:T(8,128)(2,1)} %get-tuple-element.59) | copy-start | bytes 12582916
  350.6 4.7 %copy-start.4 = (bf16[2,128,1024]{2,1,0:T(8,128)(2,1)S(1)}, bf16[2,128,1024]{2,1,0:T(8,128)(2,1)}, u32[]{:S(2)}) copy-start(bf16[2,128,1024]{2,1,0:T(8,128)(2,1)} %get-tuple-element.54) | copy-start | bytes 1572868
  350.6 5.5 %copy-start.3 = (bf16[2,128,1024]{2,1,0:T(8,128)(2,1)S(1)}, bf16[2,128,1024]{2,1,0:T(8,128)(2,1)}, u32[]{:S(2)}) copy-start(bf16[2,128,1024]{2,1,0:T(8,128)(2,1)} %get-tuple-element.55) | copy-start | bytes 1572868
  350.6 6.3 %copy-start.1 = (f32[128,2048]{1,0:T(8,128)S(1)}, f32[128,2048]{1,0:T(8,128)}, u32[]{:S(2)}) copy-start(f32[128,2048]{1,0:T(8,128)} %get-tuple-element.100) | copy-start | bytes 3145732
  355.3 2.6 copy-start.2

commit v4 on v3

--- a/solution.py
+++ b/solution.py
@@ -256,8 +256,9 @@
 
 
 class ColumnGather:
-    def __init__(self, column, ref, sems, count):
+    def __init__(self, column, ref, sems, count, own=None):
         self.column, self.ref, self.sems, self.count = column, ref, sems, count
+        self.own = own
 
     def message(self, i):
         y, c = self.column.y, self.column.c
@@ -274,7 +275,8 @@
             lambda: (ref.at[yn, c], column.other()),
             lambda: (ref.at[yo, c], column.other()),
         ][i]()
-        return send(view, view, self.sems.at[0, i], self.sems.at[1, i], device)
+        source = self.own if i < 3 and self.own is not None else view
+        return send(source, view, self.sems.at[0, i], self.sems.at[1, i], device)
 
     def step(self, n):
         order = [
@@ -398,18 +400,17 @@
 
 def front_kernel(
     tok, cot, wq, wo, small, seg_ref, routes_ref, turn_hbm,
-    dy_all, x0_all, wq_out, wo_out, kv_out, raw_out,
+    dy_out, x0_out, wq_out, wo_out, kv_out, raw_out,
     small_t, q_t, mix_t, lsum, res, ffn, gates_t, sent,
-    wq_all, wo_all, kv_all, raw_t, small_all, normed, bias, turn, plane_sems, column_sems, local,
+    dy_all, x0_all, wq_all, wo_all, kv_all, raw_t, small_all, normed, bias, turn, plane_sems, column_sems,
+    local,
 ):
     plane, column = Plane(), Column()
     y, c = column.y, column.c
     copies = [
         pltpu.make_async_copy(small, small_all.at[y, c], local.at[0]),
         pltpu.make_async_copy(wq.at[:, 1024:2048], wq_all.at[1, y, c], local.at[1]),
-        pltpu.make_async_copy(cot.at[0], dy_all.at[0, plane.z, plane.x], local.at[2]),
         pltpu.make_async_copy(wq.at[:, 0:1024], wq_all.at[0, y, c], local.at[3]),
-        pltpu.make_async_copy(cot.at[1], dy_all.at[1, plane.z, plane.x], local.at[4]),
         pltpu.make_async_copy(wo, wo_all.at[y, c], local.at[5]),
         pltpu.make_async_copy(turn_hbm.at[column.me], turn, local.at[6]),
     ]
@@ -420,8 +421,12 @@
         pltpu.make_async_copy(wo_all, wo_out, local.at[8]),
         pltpu.make_async_copy(kv_all, kv_out, local.at[9]),
         pltpu.make_async_copy(raw_t, raw_out, local.at[10]),
+        pltpu.make_async_copy(dy_all.at[0], dy_out.at[0], local.at[11]),
+        pltpu.make_async_copy(dy_all.at[1], dy_out.at[1], local.at[2]),
+        pltpu.make_async_copy(x0_all, x0_out, local.at[4]),
     ]
-    own_x = pltpu.make_async_copy(ffn.at[0], x0_all.at[plane.z, plane.x], local.at[11])
+    for mb in range(2):
+        dy_all[mb, plane.z, plane.x] = cot[mb]
     greet(plane.neighbours() + column.neighbours())
     gdy = [Gather(plane, dy_all.at[mb], plane_sems.at[mb]) for mb in range(2)]
     gx = Gather(plane, x0_all, plane_sems.at[2])
@@ -430,32 +435,17 @@
     w_kv = ColumnGather(column, wq_all.at[1], column_sems.at[2], 128)
     w_o = ColumnGather(column, wo_all, column_sems.at[3], 128)
     kv = [ColumnGather(column, kv_all.at[mb], column_sems.at[4 + mb], 8) for mb in range(2)]
-    copies[0].wait()
-    w_small.step(0)
-    copies[1].wait()
-    w_kv.step(0)
-    copies[2].wait()
-    gdy[0].step(0)
-    for mb in range(2):
-        document_bias(seg_ref, bias, mb, column.me)
-    w_small.step(1)
-    w_small.step(2)
-    w_small.step(3)
-    for b in range(8):
-        small_t[:, 128 * b : 128 * (b + 1)] = small_all[b // 2, b % 2].astype(F32)
-    attn_gain = small_t[32:33]
-    for mb in range(2):
-        v = tok[mb].astype(F32)
-        normed[128 * mb : 128 * (mb + 1)] = (v * inverse_rms(v, 1) * attn_gain).astype(BF)
-    w_kv.step(1)
-    gdy[0].step(1)
-    copies[4].wait()
-    gdy[1].step(0)
-    w_kv.step(2)
-    copies[3].wait()
-    w_q.step(0)
-    gdy[0].step(2)
-    w_kv.step(3)
+    def both_biases():
+        for mb in range(2):
+            document_bias(seg_ref, bias, mb, column.me)
+
+    def norm_tokens():
+        for b in range(8):
+            small_t[:, 128 * b : 128 * (b + 1)] = small_all[b // 2, b % 2].astype(F32)
+        attn_gain = small_t[32:33]
+        for mb in range(2):
+            v = tok[mb].astype(F32)
+            normed[128 * mb : 128 * (mb + 1)] = (v * inverse_rms(v, 1) * attn_gain).astype(BF)
 
     def project(k):
         @pl.loop(0, 2)
@@ -465,11 +455,6 @@
             got = nn(normed[...], wq_all[k, :, :, :, cols].reshape(1024, 512))
             for mb in range(2):
                 raw_t[mb, rows] = got[128 * mb : 128 * (mb + 1)].T
-
-    query_gain = head_gain(small_t[...], 34)
-    key_gain = head_gain(small_t[...], 35)
-    copies[6].wait()
-    cosine, sine = turn[:32], turn[32:]
 
     def key_heads(mb):
         @pl.loop(0, 8)
@@ -527,52 +512,76 @@
         for k in range(16):
             sent[k, 2 * mb : 2 * mb + 2] = gates[2 * k : 2 * k + 2]
 
+    sent[...] = jnp.zeros_like(sent)
+    copies[1].wait()
+    w_kv.step(0)
+    copies[0].wait()
+    w_small.step(0)
+    gdy[1].step(0)
+    gdy[1].step(1)
+    gdy[0].step(0)
+    copies[2].wait()
+    w_q.step(0)
+    w_small.step(1)
+    w_kv.step(1)
+    w_small.step(2)
+    gdy[1].step(2)
+    w_small.step(3)
+    norm_tokens()
+    copies[3].wait()
+    w_o.step(0)
+    gdy[0].step(1)
+    w_kv.step(2)
+    w_kv.step(3)
     project(1)
+    w_q.step(1)
+    query_gain = head_gain(small_t[...], 34)
+    key_gain = head_gain(small_t[...], 35)
+    copies[4].wait()
+    cosine, sine = turn[:32], turn[32:]
     key_heads(0)
     kv[0].step(0)
-    w_q.step(1)
-    key_heads(1)
+    gdy[0].step(2)
+    w_q.step(2)
+    both_biases()
+    w_o.step(1)
     kv[0].step(1)
-    w_q.step(2)
-    copies[5].wait()
-    w_o.step(0)
-    sent[...] = jnp.zeros_like(sent)
     w_q.step(3)
     outs[0].start()
+    gdy[1].step(3)
     project(0)
     outs[3].start()
     kv[0].step(2)
-    kv[1].step(0)
-    gdy[1].step(1)
     query_heads(0)
+    gdy[0].step(3)
+    key_heads(1)
+    w_o.step(2)
     kv[0].step(3)
     attend(0, 0, 4)
-    w_o.step(1)
-    gdy[0].step(3)
     attend(0, 4, 8)
-    w_o.step(2)
-    kv[1].step(1)
-    gdy[0].step(4)
-    query_heads(1)
     w_o.step(3)
     outs[1].start()
     finish(0)
-    own_x.start()
+    x0_all[plane.z, plane.x] = ffn[0]
+    gx.step(0)
+    query_heads(1)
+    kv[1].step(0)
+    gx.step(1)
+    gx.step(2)
+    gdy[1].step(4)
+    outs[5].start()
+    kv[1].step(1)
     kv[1].step(2)
-    gdy[1].step(2)
-    own_x.wait()
-    gx.step(0)
     kv[1].step(3)
     outs[2].start()
     attend(1, 0, 4)
-    gx.step(1)
     attend(1, 4, 8)
-    gx.step(2)
-    gdy[1].step(3)
+    gx.step(3)
     finish(1)
-    gdy[1].step(4)
-    gx.step(3)
+    gdy[0].step(4)
+    outs[4].start()
     gx.step(4)
+    outs[6].start()
     for copy in outs:
         copy.wait()
 
@@ -601,6 +610,8 @@
         in_specs=[vmem, vmem, anywhere, anywhere, anywhere, vmem, vmem, anywhere],
         out_specs=(anywhere,) * 6 + (vmem,) * 8,
         scratch_shapes=[
+            pltpu.VMEM((2, 4, 4, 128, 1024), BF),
+            pltpu.VMEM((4, 4, 128, 1024), BF),
             pltpu.VMEM((2, 4, 2, 128, 1024), BF),
             pltpu.VMEM((4, 2, 128, 1024), BF),
             pltpu.VMEM((2, 4, 2, 8, 128, 128), BF),
@@ -663,7 +674,6 @@
         gate_message(step).start()
     g_all[me] = gates_ref[me]
     gx = Gather(plane, x_all.at[1], sems.at[0])
-    gx.step(0)
 
     def into(mb):
         def store(place, rows, total):
@@ -688,21 +698,22 @@
         )
         for k in range(3)
     ]
-    for step in range(1, 16):
-        gate_message(step).wait_recv()
-    for step in range(1, 16):
-        gate_message(step).wait_send()
-
-    earlier = (
-        lax.broadcasted_iota(jnp.int32, (128, 128), 0)
-        < lax.broadcasted_iota(jnp.int32, (128, 128), 1)
-    ).astype(F32).astype(BF)
-
-    @pl.loop(0, 16)
-    def _(s):
-        named = g_all[s] > 0.0
-        before = nn(named.astype(F32).astype(BF), earlier)
-        ranks[s] = jnp.where(named, before, -1.0)
+    def gates_here():
+        for step in range(1, 16):
+            gate_message(step).wait_recv()
+        for step in range(1, 16):
+            gate_message(step).wait_send()
+
+        earlier = (
+            lax.broadcasted_iota(jnp.int32, (128, 128), 0)
+            < lax.broadcasted_iota(jnp.int32, (128, 128), 1)
+        ).astype(F32).astype(BF)
+
+        @pl.loop(0, 16)
+        def _(s):
+            named = g_all[s] > 0.0
+            before = nn(named.astype(F32).astype(BF), earlier)
+            ranks[s] = jnp.where(named, before, -1.0)
 
     slot_ids = lax.broadcasted_iota(jnp.int32, (SLOTS, 128), 0).astype(F32)
 
@@ -792,56 +803,58 @@
             both = jnp.concatenate([gc[0, span(s)], gc[1, span(s)]], axis=0)
             dy_all[mb, s // 4, s % 4] = tn(pick, both).astype(BF)
 
+    gx.step(0)
+    gates_here()
     own[1].wait()
     for copy in dys:
         copy.wait()
     select(0)
-    gx.step(1)
     w1.wait()
     w2.wait()
+    gx.step(1)
+    forward(1)
     forward(0)
     gx.step(2)
-    forward(1)
     backward(0, 0)
+    backward(0, 1)
     gx.step(3)
-    backward(0, 1)
     combine_dx(0)
     sdx[0].step(0)
-    gx.step(4)
     combine_out(0)
     outs[0].start()
+    gx.step(4)
+    select(1)
     sdx[0].step(1)
-    select(1)
     forward(0)
+    backward(1, 0)
+    forward(1)
     sdx[0].step(2)
-    backward(1, 0)
+    backward(1, 1)
+    sdx[0].step(3)
     dsum[0].step(0)
-    sdx[0].step(3)
-    forward(1)
-    dsum[0].step(1)
+    combine_dx(1)
     sdx[0].step(4)
     sdx[0].give_credit()
-    backward(1, 1)
+    sdx[1].take_credit()
+    sdx[1].step(0)
     dsum[1].step(0)
+    dsum[0].step(1)
+    combine_out(1)
+    outs[1].start()
     dsum[2].step(0)
     dsum[0].step(2)
-    combine_dx(1)
-    sdx[1].take_credit()
-    sdx[1].step(0)
+    sdx[1].step(1)
     dsum[1].step(1)
-    dsum[2].step(1)
-    combine_out(1)
-    outs[1].start()
-    sdx[1].step(1)
-    dsum[0].step(3)
     h_ref[me] = hs[me]
     for step in range(1, 16):
         h_message(step).start()
+    dsum[2].step(1)
     dsum[1].step(2)
+    dsum[2].step(2)
     sdx[1].step(2)
-    dsum[2].step(2)
+    sdx[1].step(3)
     dsum[1].step(3)
-    sdx[1].step(3)
+    dsum[0].step(3)
     dsum[2].step(3)
     sdx[1].step(4)
     for step in range(1, 16):
@@ -917,7 +930,7 @@
     wq_all, wo_all, kv_all, raw_t, turn, bias, gres, branch, gm_t, dq_t, own_kv, gp, normed_t, gn,
     part_kv, part_w, part_s, q_sum, k_sum, ra, rb, rc, sa, sb, sc, plane_buf, plane_all, p1, p2, p3, p4, ta, tb, tc,
     logits, routers, router_sum, out_part, r1, r2, r3, r4, parcels, got_parcels, small_own, kv_total,
-    column_sems, plane_sems, far_send, far_recv, all_send, all_recv, free, local,
+    column_sems, plane_sems, far_send, far_recv, all_send, all_recv, free, local, gain_sums,
 ):
     plane, column = Plane(), Column()
     y, c = column.y, column.c
@@ -934,7 +947,7 @@
     for copy in parts[:1] + owns + copies:
         copy.start()
     greet(plane.others() + column.neighbours())
-    dall = [ColumnGather(column, dw_refs[n], column_sems.at[8 + n], 128) for n in range(3)]
+    dall = [ColumnGather(column, dw_refs[n], column_sems.at[8 + n], 128, dw_own.at[n]) for n in range(3)]
 
     def add_residual(mb):
         def store(place, rows, total):
@@ -946,11 +959,6 @@
         Scatter(plane, out_part, (r1, r2, r3, r4), plane_sems.at[mb], add_residual(mb), free)
         for mb in range(2)
     ]
-    parts[0].wait()
-    sout[0].step(0)
-    for copy in owns:
-        copy.wait()
-    dall[0].step(0)
     part_s[...] = jnp.zeros_like(part_s)
     q_sum[...] = jnp.zeros_like(q_sum)
     k_sum[...] = jnp.zeros_like(k_sum)
@@ -1022,43 +1030,43 @@
     ffn_gain, attn_gain = small_t[33:34], small_t[32:33]
     routers[0:32] = router
     routers[32:64] = router
-    ffn_gain_grad = jnp.zeros((1, 1024), F32)
-    for mb in range(2):
-        share = jnp.concatenate([share_ref[k, 2 * mb : 2 * mb + 2] for k in range(16)], axis=0)
-        logit = share - gates_t[mb] * jnp.sum(share, axis=0, keepdims=True)
-        high = logit.astype(BF)
-        logits[0:32, tokens_of(mb)] = high
-        logits[32:64, tokens_of(mb)] = (logit - high.astype(F32)).astype(BF)
-
-    @pl.loop(0, 4)
-    def _(n):
-        cols = pl.ds(pl.multiple_of(n * 256, 256), 256)
-        gn[:, cols] = tn(logits[...], routers[:, cols])
-        router_sum[:, cols] = nn(logits[...], ffn[:, :, cols].reshape(256, 256))
-
-    for mb in range(2):
-        into = dx[mb] + gn[tokens_of(mb)]
-        v = res[mb]
-        inv = inverse_rms(v, 1)
-        grad, gain = norm_grad(into, v, inv, ffn_gain, 1)
-        ffn_gain_grad += jnp.sum(gain, axis=0, keepdims=True)
-        total = cot[mb].astype(F32) + grad
-        gres[mb] = total
-        branch[128 * mb : 128 * (mb + 1)] = total.astype(BF)
-    copies[0].wait()
-
-    @pl.loop(0, 4)
-    def _(n):
-        rows = pl.ds(pl.multiple_of(n * 256, 256), 256)
-        got = nt(wo_all[n].reshape(256, 1024), branch[...])
-        gm_t[0, rows] = got[:, :128].astype(BF)
-        gm_t[1, rows] = got[:, 128:].astype(BF)
-        mixed = jnp.concatenate([mix_t[0, rows], mix_t[1, rows]], axis=1)
-        part_w[0, n] = nn(mixed, branch[...]).astype(BF).reshape(2, 128, 1024)
-
-    w_sums[0].step(0)
-    dall[1].step(0)
-    copies[1].wait()
+    def router_and_norm():
+        ffn_gain_grad = jnp.zeros((1, 1024), F32)
+        for mb in range(2):
+            share = jnp.concatenate([share_ref[k, 2 * mb : 2 * mb + 2] for k in range(16)], axis=0)
+            logit = share - gates_t[mb] * jnp.sum(share, axis=0, keepdims=True)
+            high = logit.astype(BF)
+            logits[0:32, tokens_of(mb)] = high
+            logits[32:64, tokens_of(mb)] = (logit - high.astype(F32)).astype(BF)
+
+        @pl.loop(0, 4)
+        def _(n):
+            cols = pl.ds(pl.multiple_of(n * 256, 256), 256)
+            gn[:, cols] = tn(logits[...], routers[:, cols])
+            router_sum[:, cols] = nn(logits[...], ffn[:, :, cols].reshape(256, 256))
+
+        for mb in range(2):
+            into = dx[mb] + gn[tokens_of(mb)]
+            v = res[mb]
+            inv = inverse_rms(v, 1)
+            grad, gain = norm_grad(into, v, inv, ffn_gain, 1)
+            ffn_gain_grad += jnp.sum(gain, axis=0, keepdims=True)
+            total = cot[mb].astype(F32) + grad
+            gres[mb] = total
+            branch[128 * mb : 128 * (mb + 1)] = total.astype(BF)
+        gain_sums[1:2] = ffn_gain_grad
+
+    def out_projection():
+        copies[0].wait()
+
+        @pl.loop(0, 4)
+        def _(n):
+            rows = pl.ds(pl.multiple_of(n * 256, 256), 256)
+            got = nt(wo_all[n].reshape(256, 1024), branch[...])
+            gm_t[0, rows] = got[:, :128].astype(BF)
+            gm_t[1, rows] = got[:, 128:].astype(BF)
+            mixed = jnp.concatenate([mix_t[0, rows], mix_t[1, rows]], axis=1)
+            part_w[0, n] = nn(mixed, branch[...]).astype(BF).reshape(2, 128, 1024)
 
     def attend(mb, start, stop):
         @pl.loop(start, stop)
@@ -1086,48 +1094,6 @@
             rows = pl.ds(pl.multiple_of(g * 128, 128), 128)
             dq_t[mb, rows] = jnp.concatenate([dq[:, :128], dq[:, 128:]], axis=0)
 
-    attend(0, 0, 2)
-    dall[0].step(1)
-    sout[0].step(1)
-    attend(0, 2, 4)
-    kv_sums[0][0].step(0)
-    w_sums[0].step(1)
-    dall[0].step(2)
-    dall[1].step(1)
-    dall[2].step(0)
-    attend(0, 4, 6)
-    kv_sums[0][0].step(1)
-    sout[0].step(2)
-    attend(0, 6, 8)
-    kv_sums[0][1].step(0)
-    w_sums[0].step(2)
-    dall[1].step(2)
-    dall[2].step(1)
-    attend(1, 0, 2)
-    kv_sums[0][1].step(1)
-    kv_sums[0][0].step(2)
-    sout[0].step(3)
-    dall[0].step(3)
-    attend(1, 2, 4)
-    kv_sums[1][0].step(0)
-    w_sums[0].step(3)
-    sout[0].step(4)
-    parts[1].start()
-    sout[0].give_credit()
-    dall[2].step(2)
-    attend(1, 4, 6)
-    kv_sums[1][0].step(1)
-    kv_sums[0][1].step(2)
-    kv_sums[0][0].step(3)
-    over[0].step(0)
-    parts[1].wait()
-    sout[1].take_credit()
-    sout[1].step(0)
-    attend(1, 6, 8)
-    kv_sums[1][1].step(0)
-    dall[1].step(3)
-    over[0].step(1)
-    copies[2].wait()
     copies[4].wait()
     cosine, sine = turn[:32], turn[32:]
     query_gain = head_gain(small_t[...], 34)
@@ -1150,21 +1116,14 @@
             cols = pl.ds(pl.multiple_of(g * 128, 128), 128)
             gp[tokens_of(mb), cols] = jnp.concatenate(pieces, axis=0).T.astype(BF)
 
-    queries_back(0)
-    kv_sums[1][1].step(1)
-    kv_sums[1][0].step(2)
-    queries_back(1)
-    kv_sums[0][1].step(3)
-    over[0].step(2)
-    sout[1].step(1)
-    dall[2].step(3)
-    for mb in range(2):
-        v = tok[mb].astype(F32)
-        normed = (v * inverse_rms(v, 1) * attn_gain).astype(BF).astype(F32)
-        for k in range(8):
-            normed_t[128 * k : 128 * (k + 1), tokens_of(mb)] = (
-                normed[:, 128 * k : 128 * (k + 1)].T.astype(BF)
-            )
+    def turn_normed():
+        for mb in range(2):
+            v = tok[mb].astype(F32)
+            normed = (v * inverse_rms(v, 1) * attn_gain).astype(BF).astype(F32)
+            for k in range(8):
+                normed_t[128 * k : 128 * (k + 1), tokens_of(mb)] = (
+                    normed[:, 128 * k : 128 * (k + 1)].T.astype(BF)
+                )
 
     def weight_part(which):
         cols = pl.ds(1024 * (which - 1), 1024)
@@ -1189,74 +1148,34 @@
             cols = pl.ds(pl.multiple_of(1536 + k * 128, 128), 128)
             gp[tokens_of(mb), cols] = jnp.concatenate(values, axis=0).T.astype(BF)
 
-    weight_part(1)
-    w_sums[1].step(0)
-    kv_sums[1][1].step(2)
-    kv_sums[1][0].step(3)
-    over[0].step(3)
-    keys_back(0)
-    w_sums[1].step(1)
-    sout[1].step(2)
-    copies[3].wait()
-
-    @pl.loop(0, 4)
-    def _(n):
-        cols = pl.ds(pl.multiple_of(n * 256, 256), 256)
-        gn[:, cols] = nt(gp[:, 0:1024], wq_all[0, n].reshape(256, 1024))
-
-    kv_sums[1][1].step(3)
-    keys_back(1)
-    weight_part(2)
-    w_sums[2].step(0)
-    w_sums[1].step(2)
-    over[0].step(4)
-    spread[0].step(0)
-    sout[1].step(3)
-
-    @pl.loop(0, 4)
-    def _(n):
-        cols = pl.ds(pl.multiple_of(n * 256, 256), 256)
-        gn[:, cols] = gn[:, cols] + nt(gp[:, 1024:2048], wq_all[1, n].reshape(256, 1024))
-
-    w_sums[2].step(1)
-    w_sums[1].step(3)
-    over[1].step(0)
-    spread[0].step(1)
-    attn_gain_grad = jnp.zeros((1, 1024), F32)
-    for mb in range(2):
-        v = tok[mb].astype(F32)
-        grad, gain = norm_grad(gn[tokens_of(mb)], v, inverse_rms(v, 1), attn_gain, 1)
-        attn_gain_grad += jnp.sum(gain, axis=0, keepdims=True)
-        in_grad[mb] = (gres[mb] + grad).astype(BF)
-    for b in range(8):
-        cols = slice(128 * b, 128 * (b + 1))
-        heads = slice(8 * b, 8 * (b + 1))
-        part_s[b // 2, b % 2, 0:32] = router_sum[0:32, cols] + router_sum[32:64, cols]
-        part_s[b // 2, b % 2, 32:33] = attn_gain_grad[:, cols]
-        part_s[b // 2, b % 2, 33:34] = ffn_gain_grad[:, cols]
-        part_s[b // 2, b % 2, 40:48] = jnp.broadcast_to(
-            jnp.sum(q_sum[heads], axis=1, keepdims=True), (8, 128)
-        )
-        part_s[b // 2, b % 2, 48:56] = jnp.broadcast_to(
-            jnp.sum(k_sum[heads], axis=1, keepdims=True), (8, 128)
-        )
-    s_sum.step(0)
-    over[1].step(1)
-    spread[0].step(2)
-    s_sum.step(1)
-    w_sums[2].step(2)
-    s_sum.step(2)
-    over[1].step(2)
-    spread[0].step(3)
-    sout[1].step(4)
-    over[1].step(3)
-    s_sum.step(3)
-    w_sums[2].step(3)
+    def normed_grad(k):
+        @pl.loop(0, 4)
+        def _(n):
+            cols = pl.ds(pl.multiple_of(n * 256, 256), 256)
+            got = nt(gp[:, 1024 * k : 1024 * (k + 1)], wq_all[k, n].reshape(256, 1024))
+            gn[:, cols] = got if k == 0 else gn[:, cols] + got
+
+    def finish():
+        attn_gain_grad = jnp.zeros((1, 1024), F32)
+        for mb in range(2):
+            v = tok[mb].astype(F32)
+            grad, gain = norm_grad(gn[tokens_of(mb)], v, inverse_rms(v, 1), attn_gain, 1)
+            attn_gain_grad += jnp.sum(gain, axis=0, keepdims=True)
+            in_grad[mb] = (gres[mb] + grad).astype(BF)
+        for b in range(8):
+            cols = slice(128 * b, 128 * (b + 1))
+            heads = slice(8 * b, 8 * (b + 1))
+            part_s[b // 2, b % 2, 0:32] = router_sum[0:32, cols] + router_sum[32:64, cols]
+            part_s[b // 2, b % 2, 32:33] = attn_gain_grad[:, cols]
+            part_s[b // 2, b % 2, 33:34] = gain_sums[1:2, cols]
+            part_s[b // 2, b % 2, 40:48] = jnp.broadcast_to(
+                jnp.sum(q_sum[heads], axis=1, keepdims=True), (8, 128)
+            )
+            part_s[b // 2, b % 2, 48:56] = jnp.broadcast_to(
+                jnp.sum(k_sum[heads], axis=1, keepdims=True), (8, 128)
+            )
+
     me = plane.me
-
-    @pl.loop(0, 16)
-    def _(n):
-        parcels[n, 64:128] = small_own[...]
 
     def parcel(step):
         to = (me + step) % 16
@@ -1270,37 +1189,151 @@
             kv_total.at[me], kv_total.at[me], all_send.at[step], all_recv.at[step], {"expert": to}
         )
 
-    for step in range(1, 16):
-        parcel(step).start()
-    got_parcels[me] = parcels[me]
+    def send_parcels():
+        @pl.loop(0, 16)
+        def _(n):
+            parcels[n, 64:128] = small_own[...]
+
+        for step in range(1, 16):
+            parcel(step).start()
+        got_parcels[me] = parcels[me]
+
+    def add_parcels():
+        for step in range(1, 16):
+            parcel(step).wait_recv()
+        total = got_parcels[0].astype(F32)
+        for n in range(1, 16):
+            total += got_parcels[n].astype(F32)
+        kv_total[me] = total[:64].astype(BF)
+        for step in range(1, 16):
+            total_message(step).start()
+        gs[...] = total[64:]
+
+    def write_out(k):
+        for n in range(16):
+            rows = slice(64 * (n // 8), 64 * (n // 8) + 64)
+            cols = slice(128 * (n % 8), 128 * (n % 8) + 128)
+            (go, gq)[k][rows, cols] = plane_all[k, n // 4, n % 4].astype(F32)
+
+    def take_totals():
+        for step in range(1, 16):
+            total_message(step).wait_recv()
+        for n in range(16):
+            first = 1024 + 128 * (n % 8)
+            gq[64 * (n // 8) : 64 * (n // 8) + 64, first : first + 128] = kv_total[n].astype(F32)
+
+    parts[0].wait()
+    sout[0].step(0)
+    dall[1].step(0)
+    router_and_norm()
+    dall[2].step(0)
+    out_projection()
+    w_sums[0].step(0)
+    copies[1].wait()
+    attend(1, 0, 2)
+    dall[1].step(1)
+    attend(0, 0, 2)
+    w_sums[0].step(1)
+    attend(0, 2, 4)
+    kv_sums[0][0].step(0)
+    dall[0].step(0)
+    sout[0].step(1)
+    attend(1, 2, 4)
+    w_sums[0].step(2)
+    attend(0, 4, 6)
+    attend(1, 4, 6)
+    attend(1, 6, 8)
+    attend(0, 6, 8)
+    kv_sums[1][1].step(0)
+    sout[0].step(2)
+    kv_sums[0][1].step(0)
+    kv_sums[0][0].step(1)
+    kv_sums[1][0].step(0)
+    dall[2].step(1)
+    w_sums[0].step(3)
+    sout[0].step(3)
+    over[0].step(0)
+    dall[0].step(1)
+    turn_normed()
+    kv_sums[0][1].step(1)
+    kv_sums[0][0].step(2)
+    copies[2].wait()
+    queries_back(0)
+    queries_back(1)
+    weight_part(1)
+    kv_sums[1][1].step(1)
+    kv_sums[1][0].step(1)
+    sout[0].step(4)
+    parts[1].start()
+    sout[0].give_credit()
+    w_sums[1].step(0)
+    kv_sums[0][1].step(2)
+    over[0].step(1)
+    parts[1].wait()
+    sout[1].take_credit()
+    sout[1].step(0)
+    over[0].step(2)
+    kv_sums[1][1].step(2)
+    dall[1].step(2)
+    kv_sums[0][0].step(3)
+    dall[0].step(2)
+    copies[3].wait()
+    normed_grad(0)
+    kv_sums[1][0].step(2)
+    over[0].step(3)
+    kv_sums[0][1].step(3)
+    keys_back(0)
+    w_sums[1].step(1)
+    sout[1].step(1)
+    over[0].step(4)
+    kv_sums[1][1].step(3)
+    kv_sums[1][0].step(3)
+    keys_back(1)
+    weight_part(2)
+    w_sums[1].step(2)
+    dall[2].step(2)
+    normed_grad(1)
+    spread[0].step(0)
+    w_sums[2].step(0)
+    spread[0].step(1)
+    finish()
+    w_sums[2].step(1)
+    w_sums[1].step(3)
+    s_sum.step(0)
+    over[1].step(0)
+    spread[0].step(2)
+    s_sum.step(1)
+    over[1].step(1)
+    w_sums[2].step(2)
+    spread[0].step(3)
+    s_sum.step(2)
+    over[1].step(2)
+    over[1].step(3)
+    s_sum.step(3)
+    dall[1].step(3)
+    sout[1].step(2)
     over[1].step(4)
     spread[1].step(0)
+    w_sums[2].step(3)
+    send_parcels()
+    spread[1].step(1)
+    spread[1].step(2)
+    dall[2].step(3)
     spread[0].step(4)
-    for step in range(1, 16):
-        parcel(step).wait_recv()
-    total = got_parcels[0].astype(F32)
-    for n in range(1, 16):
-        total += got_parcels[n].astype(F32)
-    kv_total[me] = total[:64].astype(BF)
-    for step in range(1, 16):
-        total_message(step).start()
-    gs[...] = total[64:]
-    for n in range(16):
-        place = slice(64 * (n // 8), 64 * (n // 8) + 64), slice(128 * (n % 8), 128 * (n % 8) + 128)
-        go[place] = plane_all[0, n // 4, n % 4].astype(F32)
-    for n in range(1, 5):
-        spread[1].step(n)
-    for n in range(16):
-        place = slice(64 * (n // 8), 64 * (n // 8) + 64), slice(128 * (n % 8), 128 * (n % 8) + 128)
-        gq[place] = plane_all[1, n // 4, n % 4].astype(F32)
-    for step in range(1, 16):
-        total_message(step).wait_recv()
-    for n in range(16):
-        first = 1024 + 128 * (n % 8)
-        gq[64 * (n // 8) : 64 * (n // 8) + 64, first : first + 128] = kv_total[n].astype(F32)
+    dall[0].step(3)
+    write_out(0)
+    sout[1].step(3)
+    spread[1].step(3)
+    add_parcels()
+    spread[1].step(4)
+    write_out(1)
+    sout[1].step(4)
+    take_totals()
     for step in range(1, 16):
         parcel(step).wait_send()
         total_message(step).wait_send()
+    for copy in owns:
+        copy.wait()
 
 
 def back(tok, cot, seg, turn, wq_all, wo_all, small_t, raw_t, q_t, kv_all, mix_t, lsum, res, ffn, gates_t, share, dx, out_part, dw_own):
@@ -1366,6 +1399,7 @@
             pltpu.SemaphoreType.DMA((16,)),
             pltpu.SemaphoreType.REGULAR,
             pltpu.SemaphoreType.DMA((10,)),
+            pltpu.VMEM((8, 1024), F32),
         ],
         compiler_params=pltpu.CompilerParams(
             collective_id=2, has_side_effects=True, vmem_limit_bytes=63 * MIB

time: 359 us -> 329 us (0.916)
  Pallas kernels: 340 us -> 310 us
    pallas_call x1, Pallas kernels: 107 us -> 89.3 us  [front(): pl.pallas_call(front_kernel, out_shape=(jax.ShapeDtypeStruct((2, 4, 4, 12...]
    pallas_call x1, Pallas kernels: 117 us -> 110 us  [moe(): pl.pallas_call(moe_kernel, out_shape=(jax.ShapeDtypeStruct((2, 4, 4, 128,...]
    pallas_call x1, Pallas kernels: 116 us -> 110 us  [back(): pl.pallas_call(back_kernel, out_shape=(jax.ShapeDtypeStruct((2, 4, 2, 128...]
where the time goes in v4:
time: 329 us
  Pallas kernels  310 us (94%)
  other arithmetic  10.8 us (3%)
  local copies, waits for them, and re-layouts  7.38 us (2%)
    pallas_call x1, Pallas kernels, moe(): pl.pallas_call(moe_kernel, out_shape=(jax.ShapeDtypeStruct((2, 4, 4, 128,...  110 us
    pallas_call x1, Pallas kernels, back(): pl.pallas_call(back_kernel, out_shape=(jax.ShapeDtypeStruct((2, 4, 2, 128...  110 us
    pallas_call x1, Pallas kernels, front(): pl.pallas_call(front_kernel, out_shape=(jax.ShapeDtypeStruct((2, 4, 4, 12...  89.3 us

profile of v4, /device:TPU:0, one launch (start us, length us, event | category | flops | bytes accessed | tf_op | source)
XLA Modules:
  0.0 328.6 jit_solution(12756480492469842333)
XLA Ops:
  0.6 0.7 fusion.5
  1.3 1.3 pad_maximum_fusion.small
  2.7 89.3 %shard_map.221 = (bf16[2,4,4,128,1024]{4,3,2,1,0:T(8,128)(2,1)}, bf16[4,4,128,1024]{3,2,1,0:T(8,128)(2,1)}, bf16[2,4,2,128,1024]{4,3,2,1,0:T(8,128)(2,1)}, bf16[...) custom-call(bf16[2,128,1024]{2,1,0:T(8,128)(2,1)} %bitcast.36, ...), custom_call_target="tpu_custom_call" | custom-call | flops 5000000000 | bytes 30000000 | tf_op jit(solution)/shard_map/pallas_call | solution.py:592
  92.0 110.3 %shard_map.222 = (bf16[2,4,4,128,1024]{4,3,2,1,0:T(8,128)(2,1)}, f32[2,128,1024]{2,1,0:T(8,128)}, f32[16,8,128]{2,1,0:T(8,128)}, bf16[3,128,1024]{2,1,0:T(8,128)(2,1)}) custom-call(bf16[2,128,1024]{2,1,0:T(8,128)(2,1)} %get-tuple-element.45.ffn_ref.ffn, bf16[4,4,128,1024]{3,2,1,0:T(8,128)(2,1)} %get-tuple-element.47.x0_hbm, ...), custom_call_target="tpu_custom_call" | custom-call | flops 30000001024 | bytes 30000000 | tf_op jit(solution)/shard_map/pallas_call | solution.py:872
  202.3 110.1 %shard_map.223 = (bf16[2,4,2,128,1024]{4,3,2,1,0:T(8,128)(2,1)}, bf16[4,2,128,1024]{3,2,1,0:T(8,128)(2,1)}, bf16[2,128,1024]{2,1,0:T(8,128)(2,1)}, bf16[2,128,10...) custom-call(bf16[2,128,1024]{2,1,0:T(8,128)(2,1)} %bitcast.37, ...), custom_call_target="tpu_custom_call" | custom-call | flops 12000000000 | bytes 30000000 | tf_op jit(solution)/shard_map/pallas_call | solution.py:1343
  312.4 0.0 copy-start
  312.4 1.3 slice_bitcast_fusion.1
  313.8 1.3 slice_reduce_fusion
  315.1 1.3 slice_bitcast_fusion
  316.5 4.1 %convert.3 = f32[2,512,1024]{2,1,0:T(8,128)} convert(bf16[2,512,1024]{2,1,0:T(8,128)(2,1)} %bitcast.28) | non-fusion elementwise | flops 1048576 | bytes 6291456 | tf_op jit(solution)/shard_map/reshape | solution.py:1461
  320.5 0.0 copy-done
  320.5 0.0 copy-start.4
  320.5 0.0 copy-start.3
  320.5 0.0 copy-start.1
  320.5 4.7 %bitcast_convert_fusion = f32[2,1024,1024]{2,1,0:T(8,128)} fusion(bf16[2,4,2,128,1024]{4,3,2,1,0:T(8,128)(2,1)S(1)} %copy-done), kind=kLoop, calls=%fused_computation | loop fusion | flops 2097152 | bytes 12582912 | tf_op jit(solution)/shard_map/reshape | solution.py:1460
  325.3 0.0 copy-done.4
  325.3 0.0 copy-start.2
  325.3 0.8 copy.33
  326.1 0.0 copy-done.3
  326.1 0.8 copy.34
  326.9 0.0 copy-done.1
  326.9 1.0 copy.35
  327.8 0.0 copy-done.2
  327.8 0.8 copy.36
Async XLA Ops:
  312.4 8.1 %copy-start = (bf16[2,4,2,128,1024]{4,3,2,1,0:T(8,128)(2,1)S(1)}, bf16[2,4,2,128,1024]{4,3,2,1,0:T(8,128)(2,1)}, u32[]{:S(2)}) copy-start(bf16[2,4,2,128,1024]{4,3,2,1,0:T(8,128)(2,1)} %get-tuple-element.59) | copy-start | bytes 12582916
  320.5 4.7 %copy-start.4 = (bf16[2,128,1024]{2,1,0:T(8,128)(2,1)S(1)}, bf16[2,128,1024]{2,1,0:T(8,128)(2,1)}, u32[]{:S(2)}) copy-start(bf16[2,128,1024]{2,1,0:T(8,128)(2,1)} %get-tuple-element.54) | copy-start | bytes 1572868
  320.5 5.5 %copy-start.3 = (bf16[2,128,1024]{2,1,0:T(8,128)(2,1)S(1)}, bf16[2,128,1024]{2,1,0:T(8,128)(2,1)}, u32[]{:S(2)}) copy-start(bf16[2,128,1024]{2,1,0:T(8,128)(2,1)} %get-tuple-element.55) | copy-start | bytes 1572868
  320.5 6.3 %copy-start.1 = (f32[128,2048]{1,0:T(8,128)S(1)}, f32[128,2048]{1,0:T(8,128)}, u32[]{:S(2)}) copy-start(f32[128,2048]{1,0:T(8,128)} %get-tuple-element.100) | copy-start | bytes 3145732
  325.3 2.6 copy-start.2

commit v5 on v4

--- a/solution.py
+++ b/solution.py
@@ -401,9 +401,9 @@
 def front_kernel(
     tok, cot, wq, wo, small, seg_ref, routes_ref, turn_hbm,
     dy_out, x0_out, wq_out, wo_out, kv_out, raw_out,
-    small_t, q_t, mix_t, lsum, res, ffn, gates_t, sent,
+    small_t, q_t, mix_t, lsum, res, ffn, gates_t, g_all,
     dy_all, x0_all, wq_all, wo_all, kv_all, raw_t, small_all, normed, bias, turn, plane_sems, column_sems,
-    local,
+    sent, gsend, grecv, local,
 ):
     plane, column = Plane(), Column()
     y, c = column.y, column.c
@@ -427,7 +427,7 @@
     ]
     for mb in range(2):
         dy_all[mb, plane.z, plane.x] = cot[mb]
-    greet(plane.neighbours() + column.neighbours())
+    greet(plane.others() + column.neighbours())
     gdy = [Gather(plane, dy_all.at[mb], plane_sems.at[mb]) for mb in range(2)]
     gx = Gather(plane, x0_all, plane_sems.at[2])
     w_small = ColumnGather(column, small_all, column_sems.at[0], 64)
@@ -512,50 +512,68 @@
         for k in range(16):
             sent[k, 2 * mb : 2 * mb + 2] = gates[2 * k : 2 * k + 2]
 
+    def gate_message(step):
+        to = (plane.me + step) % 16
+        return send(
+            sent.at[to], g_all.at[plane.me], gsend.at[step], grecv.at[step], {"expert": to}
+        )
+
+    def send_gates():
+        for step in range(1, 16):
+            gate_message(step).start()
+        g_all[plane.me] = sent[plane.me]
+
+    def take_gates():
+        for step in range(1, 16):
+            gate_message(step).wait_recv()
+        for step in range(1, 16):
+            gate_message(step).wait_send()
+
     sent[...] = jnp.zeros_like(sent)
+    copies[0].wait()
+    w_small.step(0)
+    gdy[0].step(0)
     copies[1].wait()
     w_kv.step(0)
-    copies[0].wait()
-    w_small.step(0)
+    w_small.step(1)
     gdy[1].step(0)
-    gdy[1].step(1)
-    gdy[0].step(0)
     copies[2].wait()
     w_q.step(0)
-    w_small.step(1)
+    gdy[0].step(1)
+    gdy[0].step(2)
+    w_small.step(2)
     w_kv.step(1)
-    w_small.step(2)
-    gdy[1].step(2)
+    gdy[1].step(1)
+    w_q.step(1)
+    copies[3].wait()
+    w_o.step(0)
     w_small.step(3)
     norm_tokens()
-    copies[3].wait()
-    w_o.step(0)
-    gdy[0].step(1)
     w_kv.step(2)
     w_kv.step(3)
     project(1)
-    w_q.step(1)
+    gdy[1].step(2)
     query_gain = head_gain(small_t[...], 34)
     key_gain = head_gain(small_t[...], 35)
     copies[4].wait()
     cosine, sine = turn[:32], turn[32:]
     key_heads(0)
     kv[0].step(0)
-    gdy[0].step(2)
+    kv[0].step(1)
+    both_biases()
+    key_heads(1)
     w_q.step(2)
-    both_biases()
+    gdy[0].step(3)
     w_o.step(1)
-    kv[0].step(1)
+    kv[0].step(2)
     w_q.step(3)
     outs[0].start()
-    gdy[1].step(3)
     project(0)
     outs[3].start()
-    kv[0].step(2)
+    kv[1].step(0)
+    w_o.step(2)
+    gdy[1].step(3)
     query_heads(0)
-    gdy[0].step(3)
-    key_heads(1)
-    w_o.step(2)
     kv[0].step(3)
     attend(0, 0, 4)
     attend(0, 4, 8)
@@ -565,21 +583,22 @@
     x0_all[plane.z, plane.x] = ffn[0]
     gx.step(0)
     query_heads(1)
-    kv[1].step(0)
+    kv[1].step(1)
     gx.step(1)
-    gx.step(2)
+    kv[1].step(2)
     gdy[1].step(4)
     outs[5].start()
-    kv[1].step(1)
-    kv[1].step(2)
+    gx.step(2)
     kv[1].step(3)
     outs[2].start()
     attend(1, 0, 4)
+    gx.step(3)
     attend(1, 4, 8)
-    gx.step(3)
     finish(1)
+    send_gates()
     gdy[0].step(4)
     outs[4].start()
+    take_gates()
     gx.step(4)
     outs[6].start()
     for copy in outs:
@@ -622,6 +641,9 @@
             pltpu.VMEM((64, 128), F32),
             pltpu.SemaphoreType.DMA((3, 2, 2, 8)),
             pltpu.SemaphoreType.DMA((6, 2, 8)),
+            pltpu.VMEM((16, 8, 128), F32),
+            pltpu.SemaphoreType.DMA((16,)),
+            pltpu.SemaphoreType.DMA((16,)),
             pltpu.SemaphoreType.DMA((12,)),
         ],
         compiler_params=pltpu.CompilerParams(
@@ -634,34 +656,26 @@
 
 
 def moe_kernel(
-    ffn_ref, x0_hbm, dy_hbm, gates_ref, wgu_hbm, wd_hbm,
+    ffn_ref, x0_hbm, dy_hbm, g_all, wgu_hbm, wd_hbm,
     out_hbm, dx_ref, h_ref, dw_own,
-    dw, x_all, dy_all, r1, r2, r3, r4, xs, ds, os, gc, act, a1, a2, ggu, g_all, ranks, hcol, hs,
-    wgu, wd, ra, rb, rc, sems, column_sems, gsend, grecv, hsend, hrecv, free, local,
+    dw, x_all, dy_all, r1, r2, r3, r4, xs, ds, os, gc, act, a1, a2, ggu, ranks, hcol, hs,
+    wgu, wd, ra, rb, rc, sems, column_sems, hsend, hrecv, free, local,
 ):
     plane, column = Plane(), Column()
     me, z, x = plane.me, plane.z, plane.x
-    w1 = pltpu.make_async_copy(wgu_hbm, wgu, local.at[0])
-    w2 = pltpu.make_async_copy(wd_hbm, wd, local.at[1])
-    w1.start()
-    w2.start()
     own = [
-        pltpu.make_async_copy(ffn_ref.at[1], x_all.at[1, z, x], local.at[4]),
-        pltpu.make_async_copy(x0_hbm, x_all.at[0], local.at[5]),
+        pltpu.make_async_copy(ffn_ref.at[1], x_all.at[1, z, x], local.at[0]),
+        pltpu.make_async_copy(x0_hbm, x_all.at[0], local.at[2]),
+        pltpu.make_async_copy(dy_hbm.at[0], dy_all.at[0], local.at[3]),
+        pltpu.make_async_copy(wgu_hbm, wgu, local.at[4]),
+        pltpu.make_async_copy(wd_hbm, wd, local.at[5]),
+        pltpu.make_async_copy(dy_hbm.at[1], dy_all.at[1], local.at[1]),
     ]
     outs = [pltpu.make_async_copy(x_all.at[mb], out_hbm.at[mb], local.at[6 + mb]) for mb in range(2)]
-    dys = [pltpu.make_async_copy(dy_hbm.at[mb], dy_all.at[mb], local.at[2 + mb]) for mb in range(2)]
-    for copy in own + dys:
+    for copy in own:
         copy.start()
     greet(plane.others() + column.neighbours())
     own[0].wait()
-
-    def gate_message(step):
-        to = (me + step) % 16
-        return pltpu.make_async_remote_copy(
-            src_ref=gates_ref.at[to], dst_ref=g_all.at[me],
-            send_sem=gsend.at[step], recv_sem=grecv.at[step], device_id={"expert": to},
-        )
 
     def h_message(step):
         to = (me + step) % 16
@@ -670,9 +684,6 @@
             send_sem=hsend.at[step], recv_sem=hrecv.at[step], device_id={"expert": to},
         )
 
-    for step in range(1, 16):
-        gate_message(step).start()
-    g_all[me] = gates_ref[me]
     gx = Gather(plane, x_all.at[1], sems.at[0])
 
     def into(mb):
@@ -698,47 +709,56 @@
         )
         for k in range(3)
     ]
-    def gates_here():
-        for step in range(1, 16):
-            gate_message(step).wait_recv()
-        for step in range(1, 16):
-            gate_message(step).wait_send()
-
-        earlier = (
-            lax.broadcasted_iota(jnp.int32, (128, 128), 0)
-            < lax.broadcasted_iota(jnp.int32, (128, 128), 1)
-        ).astype(F32).astype(BF)
-
-        @pl.loop(0, 16)
-        def _(s):
-            named = g_all[s] > 0.0
-            before = nn(named.astype(F32).astype(BF), earlier)
-            ranks[s] = jnp.where(named, before, -1.0)
+    earlier = (
+        lax.broadcasted_iota(jnp.int32, (128, 128), 0)
+        < lax.broadcasted_iota(jnp.int32, (128, 128), 1)
+    ).astype(F32).astype(BF)
+
+    @pl.loop(0, 16)
+    def _(s):
+        named = g_all[s] > 0.0
+        before = nn(named.astype(F32).astype(BF), earlier)
+        ranks[s] = jnp.where(named, before, -1.0)
 
     slot_ids = lax.broadcasted_iota(jnp.int32, (SLOTS, 128), 0).astype(F32)
 
-    def places(s, mb):
-        r = ranks[s]
-        return [(slot_ids == r[2 * mb + e : 2 * mb + e + 1]).astype(F32) for e in range(2)]
-
-    def gated(s, mb, hot):
-        g = g_all[s]
-        return [hot[e] * g[2 * mb + e : 2 * mb + e + 1] for e in range(2)]
-
-    def span(s):
-        return pl.ds(pl.multiple_of(s * SLOTS, 16), SLOTS)
+    def places(p, mb):
+        ranked = [ranks[2 * p + k] for k in range(2)]
+        return [
+            [(slot_ids == ranked[k][2 * mb + e : 2 * mb + e + 1]).astype(F32) for k in range(2)]
+            for e in range(2)
+        ]
+
+    def gated(p, mb, hot):
+        gates = [g_all[2 * p + k] for k in range(2)]
+        return [
+            [hot[e][k] * gates[k][2 * mb + e : 2 * mb + e + 1] for k in range(2)] for e in range(2)
+        ]
+
+    def spread(hot):
+        blank = jnp.zeros((SLOTS, 128), F32)
+        rows = []
+        for e in range(2):
+            rows.append(jnp.concatenate([hot[e][0], blank], axis=1))
+            rows.append(jnp.concatenate([blank, hot[e][1]], axis=1))
+        return jnp.concatenate(rows, axis=0).astype(BF)
+
+    def span(p):
+        return pl.ds(pl.multiple_of(p * 2 * SLOTS, 32), 2 * SLOTS)
+
+    def pair(p):
+        return p // 2, pl.ds(2 * (p % 2), 2)
 
     def select(mb):
-        @pl.loop(0, 16)
-        def _(s):
-            hot = places(s, mb)
-            pick = jnp.concatenate(hot, axis=0).astype(BF)
-            scaled = jnp.concatenate(gated(s, mb, hot), axis=0).astype(BF)
-            rows = nn(pick, x_all[mb, s // 4, s % 4]).astype(BF)
-            drows = nn(scaled, dy_all[mb, s // 4, s % 4]).astype(BF)
+        @pl.loop(0, 8)
+        def _(p):
+            hot = places(p, mb)
+            line, two = pair(p)
+            rows = nn(spread(hot), x_all[mb, line, two].reshape(256, 1024)).astype(BF)
+            drows = nn(spread(gated(p, mb, hot)), dy_all[mb, line, two].reshape(256, 1024)).astype(BF)
             for e in range(2):
-                xs[e, span(s)] = rows[SLOTS * e : SLOTS * (e + 1)]
-                ds[e, span(s)] = drows[SLOTS * e : SLOTS * (e + 1)]
+                xs[e, span(p)] = rows[2 * SLOTS * e : 2 * SLOTS * (e + 1)]
+                ds[e, span(p)] = drows[2 * SLOTS * e : 2 * SLOTS * (e + 1)]
 
     chunks = 16 * SLOTS // CHUNK
 
@@ -759,15 +779,19 @@
             hcol[e, r] = jnp.sum(o.astype(F32) * ds[e, r].astype(F32), axis=-1, keepdims=True)
 
     def combine_out(mb):
-        @pl.loop(0, 16)
-        def _(s):
-            hot = places(s, mb)
-            scaled = jnp.concatenate(gated(s, mb, hot), axis=0).astype(BF)
-            both = jnp.concatenate([os[0, span(s)], os[1, span(s)]], axis=0)
-            x_all[mb, s // 4, s % 4] = tn(scaled, both).astype(BF)
+        @pl.loop(0, 8)
+        def _(p):
+            hot = places(p, mb)
+            line, two = pair(p)
+            both = jnp.concatenate([os[0, span(p)], os[1, span(p)]], axis=0)
+            got = tn(spread(gated(p, mb, hot)), both).astype(BF)
+            x_all[mb, line, two] = got.reshape(2, 128, 1024)
             for e in range(2):
-                row = 2 * mb + e
-                hs[s, row : row + 1] = jnp.sum(hot[e] * hcol[e, span(s)], axis=0, keepdims=True)
+                column_of = hcol[e, span(p)]
+                for k in range(2):
+                    row = 2 * mb + e
+                    part = hot[e][k] * column_of[SLOTS * k : SLOTS * (k + 1)]
+                    hs[2 * p + k, row : row + 1] = jnp.sum(part, axis=0, keepdims=True)
 
     def add_part(mb, k, n, fresh):
         fresh = fresh.reshape(2, 128, 1024)
@@ -797,65 +821,65 @@
             add_part(mb, 2, 2 * e + m, tn(act[e, :, cols], ds[e]))
 
     def combine_dx(mb):
-        @pl.loop(0, 16)
-        def _(s):
-            pick = jnp.concatenate(places(s, mb), axis=0).astype(BF)
-            both = jnp.concatenate([gc[0, span(s)], gc[1, span(s)]], axis=0)
-            dy_all[mb, s // 4, s % 4] = tn(pick, both).astype(BF)
+        @pl.loop(0, 8)
+        def _(p):
+            line, two = pair(p)
+            both = jnp.concatenate([gc[0, span(p)], gc[1, span(p)]], axis=0)
+            got = tn(spread(places(p, mb)), both).astype(BF)
+            dy_all[mb, line, two] = got.reshape(2, 128, 1024)
 
     gx.step(0)
-    gates_here()
     own[1].wait()
-    for copy in dys:
-        copy.wait()
+    own[2].wait()
     select(0)
-    w1.wait()
-    w2.wait()
     gx.step(1)
-    forward(1)
+    own[3].wait()
+    own[4].wait()
     forward(0)
     gx.step(2)
+    forward(1)
+    combine_out(0)
+    outs[0].start()
     backward(0, 0)
+    gx.step(3)
     backward(0, 1)
-    gx.step(3)
     combine_dx(0)
     sdx[0].step(0)
-    combine_out(0)
-    outs[0].start()
     gx.step(4)
+    own[5].wait()
     select(1)
+    forward(1)
     sdx[0].step(1)
     forward(0)
     backward(1, 0)
-    forward(1)
+    dsum[0].step(0)
     sdx[0].step(2)
     backward(1, 1)
     sdx[0].step(3)
-    dsum[0].step(0)
+    dsum[1].step(0)
+    dsum[2].step(0)
+    dsum[0].step(1)
     combine_dx(1)
     sdx[0].step(4)
     sdx[0].give_credit()
     sdx[1].take_credit()
     sdx[1].step(0)
-    dsum[1].step(0)
-    dsum[0].step(1)
+    dsum[2].step(1)
     combine_out(1)
     outs[1].start()
-    dsum[2].step(0)
+    dsum[1].step(1)
+    sdx[1].step(1)
     dsum[0].step(2)
-    sdx[1].step(1)
-    dsum[1].step(1)
+    dsum[1].step(2)
+    dsum[2].step(2)
+    sdx[1].step(2)
     h_ref[me] = hs[me]
     for step in range(1, 16):
         h_message(step).start()
-    dsum[2].step(1)
-    dsum[1].step(2)
-    dsum[2].step(2)
-    sdx[1].step(2)
     sdx[1].step(3)
-    dsum[1].step(3)
     dsum[0].step(3)
     dsum[2].step(3)
+    dsum[1].step(3)
     sdx[1].step(4)
     for step in range(1, 16):
         h_message(step).wait_recv()
@@ -893,7 +917,6 @@
             pltpu.VMEM((2, rows, 512), BF),
             pltpu.VMEM((rows, 1024), BF),
             pltpu.VMEM((16, 8, 128), F32),
-            pltpu.VMEM((16, 8, 128), F32),
             pltpu.VMEM((2, rows, 1), F32),
             pltpu.VMEM((16, 8, 128), F32),
             pltpu.VMEM((2, 1024, 1024), BF),
@@ -901,8 +924,6 @@
             *column_slots((128, 1024), lead=(3,)),
             pltpu.SemaphoreType.DMA((3, 2, 2, 8)),
             pltpu.SemaphoreType.DMA((3, 2, 8)),
-            pltpu.SemaphoreType.DMA((16,)),
-            pltpu.SemaphoreType.DMA((16,)),
             pltpu.SemaphoreType.DMA((16,)),
             pltpu.SemaphoreType.DMA((16,)),
             pltpu.SemaphoreType.REGULAR,
@@ -976,7 +997,7 @@
                 if which == 2:
                     parcels[n, some] = piece
                 else:
-                    plane_buf[which, n // 4, n % 4, some] = piece
+                    plane_buf[n // 4, n % 4, some, 128 * which : 128 * (which + 1)] = piece
 
         return store
 
@@ -1008,20 +1029,11 @@
     ]
     s_sum = ColumnScatter(column, part_s, (ta, tb, tc), column_sems.at[3], 64, place_s)
 
-    def keep(n):
-        def store(place, rows, total):
-            plane_all[(n, *place)] = total.astype(BF)
-
-        return store
-
-    over = [
-        Scatter(
-            plane, plane_buf.at[n], (p1.at[n], p2.at[n], p3.at[n], p4.at[n]), plane_sems.at[2 + n],
-            keep(n), height=64,
-        )
-        for n in range(2)
-    ]
-    spread = [Gather(plane, plane_all.at[n], plane_sems.at[4 + n], height=64) for n in range(2)]
+    def keep(place, rows, total):
+        plane_all[place] = total.astype(BF)
+
+    over = Scatter(plane, plane_buf, (p1, p2, p3, p4), plane_sems.at[2], keep, height=64)
+    spread = Gather(plane, plane_all, plane_sems.at[3], height=64)
 
     def tokens_of(mb):
         return pl.ds(128 * mb, 128)
@@ -1213,7 +1225,7 @@
         for n in range(16):
             rows = slice(64 * (n // 8), 64 * (n // 8) + 64)
             cols = slice(128 * (n % 8), 128 * (n % 8) + 128)
-            (go, gq)[k][rows, cols] = plane_all[k, n // 4, n % 4].astype(F32)
+            (go, gq)[k][rows, cols] = plane_all[n // 4, n % 4, :, 128 * k : 128 * (k + 1)].astype(F32)
 
     def take_totals():
         for step in range(1, 16):
@@ -1222,112 +1234,102 @@
             first = 1024 + 128 * (n % 8)
             gq[64 * (n // 8) : 64 * (n // 8) + 64, first : first + 128] = kv_total[n].astype(F32)
 
+    dall[2].step(0)
+    router_and_norm()
     parts[0].wait()
     sout[0].step(0)
+    dall[0].step(0)
+    out_projection()
     dall[1].step(0)
-    router_and_norm()
-    dall[2].step(0)
-    out_projection()
-    w_sums[0].step(0)
     copies[1].wait()
     attend(1, 0, 2)
-    dall[1].step(1)
+    attend(1, 2, 4)
     attend(0, 0, 2)
-    w_sums[0].step(1)
-    attend(0, 2, 4)
-    kv_sums[0][0].step(0)
-    dall[0].step(0)
+    kv_sums[1][0].step(0)
+    w_sums[0].step(0)
     sout[0].step(1)
-    attend(1, 2, 4)
-    w_sums[0].step(2)
-    attend(0, 4, 6)
     attend(1, 4, 6)
     attend(1, 6, 8)
+    dall[0].step(1)
+    kv_sums[1][0].step(1)
+    kv_sums[1][1].step(0)
+    attend(0, 2, 4)
+    w_sums[0].step(1)
+    attend(0, 4, 6)
+    dall[2].step(1)
+    kv_sums[1][1].step(1)
+    sout[0].step(2)
+    w_sums[0].step(2)
     attend(0, 6, 8)
-    kv_sums[1][1].step(0)
-    sout[0].step(2)
+    sout[0].step(3)
     kv_sums[0][1].step(0)
-    kv_sums[0][0].step(1)
-    kv_sums[1][0].step(0)
-    dall[2].step(1)
-    w_sums[0].step(3)
-    sout[0].step(3)
-    over[0].step(0)
-    dall[0].step(1)
+    kv_sums[0][0].step(0)
+    kv_sums[1][1].step(2)
     turn_normed()
+    copies[2].wait()
+    queries_back(1)
+    queries_back(0)
+    kv_sums[1][0].step(2)
     kv_sums[0][1].step(1)
-    kv_sums[0][0].step(2)
-    copies[2].wait()
-    queries_back(0)
-    queries_back(1)
     weight_part(1)
-    kv_sums[1][1].step(1)
-    kv_sums[1][0].step(1)
+    copies[3].wait()
+    normed_grad(0)
     sout[0].step(4)
     parts[1].start()
     sout[0].give_credit()
     w_sums[1].step(0)
+    kv_sums[0][0].step(1)
     kv_sums[0][1].step(2)
-    over[0].step(1)
     parts[1].wait()
     sout[1].take_credit()
     sout[1].step(0)
-    over[0].step(2)
-    kv_sums[1][1].step(2)
+    dall[0].step(2)
+    w_sums[1].step(1)
+    kv_sums[1][1].step(3)
+    kv_sums[0][1].step(3)
+    kv_sums[0][0].step(2)
+    w_sums[1].step(2)
+    sout[1].step(1)
+    kv_sums[0][0].step(3)
+    kv_sums[1][0].step(3)
+    keys_back(0)
+    dall[2].step(2)
+    keys_back(1)
+    dall[1].step(1)
+    weight_part(2)
+    w_sums[2].step(0)
+    w_sums[0].step(3)
+    normed_grad(1)
+    w_sums[1].step(3)
+    over.step(0)
+    finish()
+    dall[0].step(3)
     dall[1].step(2)
-    kv_sums[0][0].step(3)
-    dall[0].step(2)
-    copies[3].wait()
-    normed_grad(0)
-    kv_sums[1][0].step(2)
-    over[0].step(3)
-    kv_sums[0][1].step(3)
-    keys_back(0)
-    w_sums[1].step(1)
-    sout[1].step(1)
-    over[0].step(4)
-    kv_sums[1][1].step(3)
-    kv_sums[1][0].step(3)
-    keys_back(1)
-    weight_part(2)
-    w_sums[1].step(2)
-    dall[2].step(2)
-    normed_grad(1)
-    spread[0].step(0)
-    w_sums[2].step(0)
-    spread[0].step(1)
-    finish()
+    s_sum.step(0)
     w_sums[2].step(1)
-    w_sums[1].step(3)
-    s_sum.step(0)
-    over[1].step(0)
-    spread[0].step(2)
+    over.step(1)
+    dall[2].step(3)
+    sout[1].step(2)
     s_sum.step(1)
-    over[1].step(1)
     w_sums[2].step(2)
-    spread[0].step(3)
+    over.step(2)
+    over.step(3)
     s_sum.step(2)
-    over[1].step(2)
-    over[1].step(3)
+    sout[1].step(3)
+    dall[1].step(3)
+    over.step(4)
     s_sum.step(3)
-    dall[1].step(3)
-    sout[1].step(2)
-    over[1].step(4)
-    spread[1].step(0)
+    spread.step(0)
     w_sums[2].step(3)
     send_parcels()
-    spread[1].step(1)
-    spread[1].step(2)
-    dall[2].step(3)
-    spread[0].step(4)
-    dall[0].step(3)
+    spread.step(1)
+    spread.step(2)
+    sout[1].step(4)
+    add_parcels()
+    spread.step(3)
+    spread.step(4)
     write_out(0)
-    sout[1].step(3)
-    spread[1].step(3)
-    add_parcels()
-    spread[1].step(4)
     write_out(1)
-    sout[1].step(4)
     take_totals()
     for step in range(1, 16):
         parcel(step).wait_send()
@@ -1378,9 +1380,9 @@
             pltpu.VMEM((64, 128), F32),
             *column_slots((128, 1024), lead=(3,)),
             *kv_slots,
-            pltpu.VMEM((2, 4, 4, 64, 128), BF),
-            pltpu.VMEM((2, 4, 4, 64, 128), BF),
-            *scatter_slots(64, 128, lead=(2,)),
+            pltpu.VMEM((4, 4, 64, 256), BF),
+            pltpu.VMEM((4, 4, 64, 256), BF),
+            *scatter_slots(64, 256),
             *column_slots((64, 128), F32),
             pltpu.VMEM((64, 256), BF),
             pltpu.VMEM((64, 1024), BF),
@@ -1392,7 +1394,7 @@
             pltpu.VMEM((64, 128), BF),
             pltpu.VMEM((16, 64, 128), BF),
             pltpu.SemaphoreType.DMA((11, 2, 8)),
-            pltpu.SemaphoreType.DMA((6, 2, 2, 8)),
+            pltpu.SemaphoreType.DMA((4, 2, 2, 8)),
             pltpu.SemaphoreType.DMA((16,)),
             pltpu.SemaphoreType.DMA((16,)),
             pltpu.SemaphoreType.DMA((16,)),

time: 329 us -> 318 us (0.967)
  Pallas kernels: 310 us -> 299 us
    pallas_call x1, Pallas kernels: 110 us -> 105 us  [moe(): pl.pallas_call(moe_kernel, out_shape=(jax.ShapeDtypeStruct((2, 4, 4, 128,...]
    pallas_call x1, Pallas kernels: 110 us -> 105 us  [back(): pl.pallas_call(back_kernel, out_shape=(jax.ShapeDtypeStruct((2, 4, 2, 128...]
where the time goes in v5:
time: 318 us
  Pallas kernels  299 us (94%)
  other arithmetic  10.8 us (3%)
  local copies, waits for them, and re-layouts  7.38 us (2%)
    pallas_call x1, Pallas kernels, moe(): pl.pallas_call(moe_kernel, out_shape=(jax.ShapeDtypeStruct((2, 4, 4, 128,...  105 us
    pallas_call x1, Pallas kernels, back(): pl.pallas_call(back_kernel, out_shape=(jax.ShapeDtypeStruct((2, 4, 2, 128...  105 us
    pallas_call x1, Pallas kernels, front(): pl.pallas_call(front_kernel, out_shape=(jax.ShapeDtypeStruct((2, 4, 4, 12...  88.5 us

profile of v5, /device:TPU:0, one launch (start us, length us, event | category | flops | bytes accessed | tf_op | source)
XLA Modules:
  0.0 317.5 jit_solution(12603039304509351313)
XLA Ops:
  0.6 0.7 fusion.5
  1.3 1.3 pad_maximum_fusion.small
  2.7 88.5 %shard_map.221 = (bf16[2,4,4,128,1024]{4,3,2,1,0:T(8,128)(2,1)}, bf16[4,4,128,1024]{3,2,1,0:T(8,128)(2,1)}, bf16[2,4,2,128,1024]{4,3,2,1,0:T(8,128)(2,1)}, bf16[...) custom-call(bf16[2,128,1024]{2,1,0:T(8,128)(2,1)} %bitcast.36, ...), custom_call_target="tpu_custom_call" | custom-call | flops 5000000000 | bytes 30000000 | tf_op jit(solution)/shard_map/pallas_call | solution.py:611
  91.2 105.1 %shard_map.222 = (bf16[2,4,4,128,1024]{4,3,2,1,0:T(8,128)(2,1)}, f32[2,128,1024]{2,1,0:T(8,128)}, f32[16,8,128]{2,1,0:T(8,128)}, bf16[3,128,1024]{2,1,0:T(8,128)(2,1)}) custom-call(bf16[2,128,1024]{2,1,0:T(8,128)(2,1)} %get-tuple-element.45.ffn_ref.ffn, bf16[4,4,128,1024]{3,2,1,0:T(8,128)(2,1)} %get-tuple-element.47.x0_hbm, ...), custom_call_target="tpu_custom_call" | custom-call | flops 30000001024 | bytes 30000000 | tf_op jit(solution)/shard_map/pallas_call | solution.py:896
  196.3 105.0 %shard_map.223 = (bf16[2,4,2,128,1024]{4,3,2,1,0:T(8,128)(2,1)}, bf16[4,2,128,1024]{3,2,1,0:T(8,128)(2,1)}, bf16[2,128,1024]{2,1,0:T(8,128)(2,1)}, bf16[2,128,10...) custom-call(bf16[2,128,1024]{2,1,0:T(8,128)(2,1)} %bitcast.37, ...), custom_call_target="tpu_custom_call" | custom-call | flops 12000000000 | bytes 30000000 | tf_op jit(solution)/shard_map/pallas_call | solution.py:1345
  301.3 0.0 copy-start
  301.3 1.3 slice_bitcast_fusion.1
  302.7 1.3 slice_reduce_fusion
  304.0 1.3 slice_bitcast_fusion
  305.3 4.1 %convert.3 = f32[2,512,1024]{2,1,0:T(8,128)} convert(bf16[2,512,1024]{2,1,0:T(8,128)(2,1)} %bitcast.28) | non-fusion elementwise | flops 1048576 | bytes 6291456 | tf_op jit(solution)/shard_map/reshape | solution.py:1463
  309.4 0.0 copy-done
  309.4 0.0 copy-start.4
  309.4 0.0 copy-start.3
  309.4 0.0 copy-start.1
  309.4 4.7 %bitcast_convert_fusion = f32[2,1024,1024]{2,1,0:T(8,128)} fusion(bf16[2,4,2,128,1024]{4,3,2,1,0:T(8,128)(2,1)S(1)} %copy-done), kind=kLoop, calls=%fused_computation | loop fusion | flops 2097152 | bytes 12582912 | tf_op jit(solution)/shard_map/reshape | solution.py:1462
  314.1 0.0 copy-done.4
  314.1 0.0 copy-start.2
  314.1 0.8 copy.33
  314.9 0.0 copy-done.3
  314.9 0.8 copy.34
  315.7 0.0 copy-done.1
  315.7 1.0 copy.35
  316.7 0.0 copy-done.2
  316.7 0.8 copy.36
Async XLA Ops:
  301.3 8.1 %copy-start = (bf16[2,4,2,128,1024]{4,3,2,1,0:T(8,128)(2,1)S(1)}, bf16[2,4,2,128,1024]{4,3,2,1,0:T(8,128)(2,1)}, u32[]{:S(2)}) copy-start(bf16[2,4,2,128,1024]{4,3,2,1,0:T(8,128)(2,1)} %get-tuple-element.59) | copy-start | bytes 12582916
  309.4 4.7 %copy-start.4 = (bf16[2,128,1024]{2,1,0:T(8,128)(2,1)S(1)}, bf16[2,128,1024]{2,1,0:T(8,128)(2,1)}, u32[]{:S(2)}) copy-start(bf16[2,128,1024]{2,1,0:T(8,128)(2,1)} %get-tuple-element.54) | copy-start | bytes 1572868
  309.4 5.5 %copy-start.3 = (bf16[2,128,1024]{2,1,0:T(8,128)(2,1)S(1)}, bf16[2,128,1024]{2,1,0:T(8,128)(2,1)}, u32[]{:S(2)}) copy-start(bf16[2,128,1024]{2,1,0:T(8,128)(2,1)} %get-tuple-element.55) | copy-start | bytes 1572868
  309.4 6.3 %copy-start.1 = (f32[128,2048]{1,0:T(8,128)S(1)}, f32[128,2048]{1,0:T(8,128)}, u32[]{:S(2)}) copy-start(f32[128,2048]{1,0:T(8,128)} %get-tuple-element.100) | copy-start | bytes 3145732
  314.1 2.6 copy-start.2
